TPU v7x, 32 devices: a whole 2x2x4 slice. The times are simulated.
32 devices in a mesh: dp: 8 (over y, x, core), mp: 4 (over z).
Axes of the slice: x: 2, y: 2, z: 4, core: 2. Of those that a mesh axis runs over, the one named last changes fastest.
Arguments:
- frames: bfloat16 [8, 1536, 768], P('dp', 'mp'), may hold values from -6 to 6
- cotangent: bfloat16 [8, 1536, 768], P('dp', 'mp'), may hold values from -6 to 6
- segments: int32 [8, 1536], P('dp'), may hold values from 0 to 3, as said below
- padding: int32 [8, 1536], P('dp'), may hold values from 0 to 1, as said below
- skip_flag: int32 [8], P('dp'), may hold values from 0 to 1, as said below
- w_query: bfloat16 [768, 768], P(None, 'mp'), may hold values from -0.21875 to 0.21875
- b_query: float32 [768], P('mp'), may hold values from -3 to 3
- w_key: bfloat16 [768, 768], P(None, 'mp'), may hold values from -0.21875 to 0.21875
- w_value: bfloat16 [768, 768], P(None, 'mp'), may hold values from -0.21875 to 0.21875
- b_value: float32 [768], P('mp'), may hold values from -3 to 3
- w_out: bfloat16 [768, 768], P('mp'), may hold values from -3.5 to 3.5
- b_out: float32 [768], replicated, may hold values from -3 to 3
- gain_one: float32 [768], replicated, may hold values from 0.5 to 1.5
- shift_one: float32 [768], replicated, may hold values from -2 to 2
- w_up: bfloat16 [768, 3072], P(None, 'mp'), may hold values from -0.21875 to 0.21875
- b_up: float32 [3072], P('mp'), may hold values from -3 to 3
- w_down: bfloat16 [3072, 768], P('mp'), may hold values from -0.21875 to 0.21875
- b_down: float32 [768], replicated, may hold values from -3 to 3
- gain_two: float32 [768], replicated, may hold values from 0.5 to 1.5
- shift_two: float32 [768], replicated, may hold values from -2 to 2
Outputs:
- layer_out: bfloat16 [8, 1536, 768], P('dp', 'mp')
- frames_grad: bfloat16 [8, 1536, 768], P('dp', 'mp')
- w_query_grad: float32 [768, 768], P(None, 'mp')
- b_query_grad: float32 [768], P('mp')
- w_key_grad: float32 [768, 768], P(None, 'mp')
- w_value_grad: float32 [768, 768], P(None, 'mp')
- b_value_grad: float32 [768], P('mp')
- w_out_grad: float32 [768, 768], P('mp')
- b_out_grad: float32 [768], replicated
- gain_one_grad: float32 [768], replicated
- shift_one_grad: float32 [768], replicated
- w_up_grad: float32 [768, 3072], P(None, 'mp')
- b_up_grad: float32 [3072], P('mp')
- w_down_grad: float32 [3072, 768], P('mp')
- b_down_grad: float32 [768], replicated
- gain_two_grad: float32 [768], replicated
- shift_two_grad: float32 [768], replicated
Inputs may be any that keep to these rules, and one draw needn't show every extreme that they name: `segments`: along each row the ids start at 0 and never fall; padded frames carry the id of the row's last utterance, which also has frames that are not padding. `padding`: in each row the frames marked 0 form its tail, fewer than 96 of them. `skip_flag`: one row is always marked 1; each other row is marked 1 with chance one in twenty.
All inputs are finite; a program needn't handle non-finite values.
Results may differ from a plain program's by a relative error of at most 0.02.
Values may be sent and summed in bfloat16 or wider, within the bound.
A program may use at most 128 MiB of HBM per device.

v0:
```python
from functools import partial

import jax
import jax.numpy as jnp
from jax import lax
from jax.sharding import PartitionSpec as P

HEAD_DIM = 64


def layer_norm(values, gain, shift):
    centered = values - jnp.mean(values, -1, keepdims=True)
    spread = jnp.mean(centered * centered, -1, keepdims=True)
    return centered * lax.rsqrt(spread + 1e-05) * gain + shift


def block_layout(seg_row):
    length = seg_row.shape[0]
    block_rows = min(512, length)
    return (length // block_rows, block_rows)


def masked_scores(query_block, key_heads, seg_block, seg_row, pad_row):
    scores = jnp.einsum("qhd,khd->hqk", query_block, key_heads, preferred_element_type=jnp.float32)
    allowed = (seg_block[:, None] == seg_row[None, :]) & (pad_row[None, :] == 1)
    return jnp.where(allowed[None], scores, -1e30)


def attend_forward(query_heads, key_heads, value_heads, seg_row, pad_row):
    block_count, block_rows = block_layout(seg_row)
    head_count = query_heads.shape[1]
    query_blocks = query_heads.reshape(block_count, block_rows, head_count, HEAD_DIM)
    seg_blocks = seg_row.reshape(block_count, block_rows)

    def one_block(pieces):
        query_block, seg_block = pieces
        scores = masked_scores(query_block, key_heads, seg_block, seg_row, pad_row)
        row_peak = jnp.max(scores, -1, keepdims=True)
        raised = jnp.exp(scores - row_peak)
        summed = jnp.sum(raised, -1, keepdims=True)
        weights = (raised / summed).astype(jnp.bfloat16)
        mixed_block = jnp.einsum(
            "hqk,khd->qhd", weights, value_heads, preferred_element_type=jnp.float32
        )
        return (mixed_block.astype(jnp.bfloat16), (row_peak + jnp.log(summed))[..., 0])

    mixed_blocks, log_total = lax.map(one_block, (query_blocks, seg_blocks))
    return (mixed_blocks.reshape(-1, head_count, HEAD_DIM), log_total)


def attend_backward(query_heads, key_heads, value_heads, grad_mixed, log_total, seg_row, pad_row):
    block_count, block_rows = block_layout(seg_row)
    head_count = query_heads.shape[1]
    query_blocks = query_heads.reshape(block_count, block_rows, head_count, HEAD_DIM)
    grad_blocks = grad_mixed.reshape(block_count, block_rows, head_count, HEAD_DIM)
    seg_blocks = seg_row.reshape(block_count, block_rows)

    def one_block(carried, pieces):
        grad_keys, grad_values = carried
        query_block, seg_block, grad_block, log_block = pieces
        scores = masked_scores(query_block, key_heads, seg_block, seg_row, pad_row)
        weights = jnp.exp(scores - log_block[..., None])
        rounded = weights.astype(jnp.bfloat16)
        grad_values = grad_values + jnp.einsum(
            "hqk,qhd->khd", rounded, grad_block, preferred_element_type=jnp.float32
        )
        grad_weights = jnp.einsum(
            "qhd,khd->hqk", grad_block, value_heads, preferred_element_type=jnp.float32
        )
        inner_sum = jnp.sum(weights * grad_weights, -1, keepdims=True)
        grad_scores = (weights * (grad_weights - inner_sum)).astype(jnp.bfloat16)
        grad_query = jnp.einsum(
            "hqk,khd->qhd", grad_scores, key_heads, preferred_element_type=jnp.float32
        )
        grad_keys = grad_keys + jnp.einsum(
            "hqk,qhd->khd", grad_scores, query_block, preferred_element_type=jnp.float32
        )
        return ((grad_keys, grad_values), grad_query.astype(jnp.bfloat16))

    start_grads = (
        jnp.zeros(key_heads.shape, jnp.float32),
        jnp.zeros(value_heads.shape, jnp.float32),
    )
    (grad_keys, grad_values), grad_queries = lax.scan(
        one_block, start_grads, (query_blocks, seg_blocks, grad_blocks, log_total)
    )
    return (
        grad_queries.reshape(-1, head_count, HEAD_DIM),
        grad_keys.astype(jnp.bfloat16),
        grad_values.astype(jnp.bfloat16),
    )


def shards(
    frames,
    cotangent,
    segments,
    padding,
    skip_flag,
    w_query,
    b_query,
    w_key,
    w_value,
    b_value,
    w_out,
    b_out,
    gain_one,
    shift_one,
    w_up,
    b_up,
    w_down,
    b_down,
    gain_two,
    shift_two,
):
    row_count, share_rows, model_width = frames.shape
    length = segments.shape[1]
    local_width = w_query.shape[1]
    head_count = local_width // HEAD_DIM
    scale_factor = HEAD_DIM ** (-0.5)
    flat_rows = row_count * length
    everything = lax.all_gather(frames, "mp", axis=1, tiled=True).reshape(flat_rows, model_width)
    query_rows = (
        (jnp.dot(everything, w_query, preferred_element_type=jnp.float32) + b_query) * scale_factor
    ).astype(jnp.bfloat16)
    key_rows = jnp.dot(everything, w_key, preferred_element_type=jnp.float32).astype(jnp.bfloat16)
    value_rows = (
        jnp.dot(everything, w_value, preferred_element_type=jnp.float32) + b_value
    ).astype(jnp.bfloat16)
    query_heads = query_rows.reshape(row_count, length, head_count, HEAD_DIM)
    key_heads = key_rows.reshape(row_count, length, head_count, HEAD_DIM)
    value_heads = value_rows.reshape(row_count, length, head_count, HEAD_DIM)
    mixed_rows, log_total = lax.map(
        lambda row_items: attend_forward(*row_items),
        (query_heads, key_heads, value_heads, segments, padding),
    )
    mixed_flat = mixed_rows.reshape(flat_rows, local_width)
    attended_part = jnp.dot(mixed_flat, w_out, preferred_element_type=jnp.float32)
    own_frames = frames.astype(jnp.float32)
    attended_own = (
        lax.psum_scatter(
            attended_part.reshape(row_count, length, model_width),
            "mp",
            scatter_dimension=1,
            tiled=True,
        )
        + b_out
    )
    summed_one = own_frames + attended_own
    normed_own = layer_norm(summed_one, gain_one, shift_one)
    normed_low = lax.all_gather(normed_own.astype(jnp.bfloat16), "mp", axis=1, tiled=True).reshape(
        flat_rows, model_width
    )
    inner_rows = jnp.dot(normed_low, w_up, preferred_element_type=jnp.float32) + b_up
    activated = jax.nn.gelu(inner_rows, approximate=False).astype(jnp.bfloat16)
    branch_part = jnp.dot(activated, w_down, preferred_element_type=jnp.float32)
    branch_own = (
        lax.psum_scatter(
            branch_part.reshape(row_count, length, model_width).astype(jnp.bfloat16),
            "mp",
            scatter_dimension=1,
            tiled=True,
        ).astype(jnp.float32)
        + b_down
    )
    summed_two = normed_own + branch_own
    result = layer_norm(summed_two, gain_two, shift_two)
    skipped = (skip_flag == 1)[:, None, None]
    layer_out = jnp.where(skipped, own_frames, result).astype(jnp.bfloat16)
    cotangent_f = cotangent.astype(jnp.float32)
    grad_out = jnp.where(skipped, 0.0, cotangent_f)
    grad_two, gain_two_grad, shift_two_grad = jax.vjp(layer_norm, summed_two, gain_two, shift_two)[
        1
    ](grad_out)
    grad_branch = grad_two.astype(jnp.bfloat16)
    b_down_grad = jnp.sum(grad_branch.astype(jnp.float32), (0, 1))
    grad_branch_all = lax.all_gather(grad_branch, "mp", axis=1, tiled=True).reshape(
        flat_rows, model_width
    )
    w_down_grad = jnp.einsum(
        "nf,nd->fd", activated, grad_branch_all, preferred_element_type=jnp.float32
    )
    grad_activated = jnp.einsum(
        "nd,fd->nf", grad_branch_all, w_down, preferred_element_type=jnp.float32
    )
    grad_inner = jax.vjp(partial(jax.nn.gelu, approximate=False), inner_rows)[1](grad_activated)[
        0
    ].astype(jnp.bfloat16)
    b_up_grad = jnp.sum(grad_inner.astype(jnp.float32), 0)
    w_up_grad = jnp.einsum("nd,nf->df", normed_low, grad_inner, preferred_element_type=jnp.float32)
    grad_normed_part = jnp.einsum("nf,df->nd", grad_inner, w_up, preferred_element_type=jnp.float32)
    grad_normed = grad_two + lax.psum_scatter(
        grad_normed_part.reshape(row_count, length, model_width).astype(jnp.bfloat16),
        "mp",
        scatter_dimension=1,
        tiled=True,
    ).astype(jnp.float32)
    grad_one, gain_one_grad, shift_one_grad = jax.vjp(layer_norm, summed_one, gain_one, shift_one)[
        1
    ](grad_normed)
    grad_attended = grad_one.astype(jnp.bfloat16)
    b_out_grad = jnp.sum(grad_attended.astype(jnp.float32), (0, 1))
    grad_attended_all = lax.all_gather(grad_attended, "mp", axis=1, tiled=True).reshape(
        flat_rows, model_width
    )
    w_out_grad = jnp.einsum(
        "nk,nd->kd", mixed_flat, grad_attended_all, preferred_element_type=jnp.float32
    )
    grad_mixed = jnp.einsum(
        "nd,kd->nk", grad_attended_all, w_out, preferred_element_type=jnp.float32
    ).astype(jnp.bfloat16)
    grad_mixed = grad_mixed.reshape(row_count, length, head_count, HEAD_DIM)
    grad_query, grad_key, grad_value = lax.map(
        lambda row_items: attend_backward(*row_items),
        (query_heads, key_heads, value_heads, grad_mixed, log_total, segments, padding),
    )
    grad_query = grad_query.reshape(flat_rows, local_width)
    grad_key = grad_key.reshape(flat_rows, local_width)
    grad_value = grad_value.reshape(flat_rows, local_width)
    w_query_grad = (
        jnp.einsum("nd,nk->dk", everything, grad_query, preferred_element_type=jnp.float32)
        * scale_factor
    )
    b_query_grad = jnp.sum(grad_query.astype(jnp.float32), 0) * scale_factor
    w_key_grad = jnp.einsum("nd,nk->dk", everything, grad_key, preferred_element_type=jnp.float32)
    w_value_grad = jnp.einsum(
        "nd,nk->dk", everything, grad_value, preferred_element_type=jnp.float32
    )
    b_value_grad = jnp.sum(grad_value.astype(jnp.float32), 0)
    input_part = (
        jnp.einsum("nk,dk->nd", grad_query, w_query, preferred_element_type=jnp.float32)
        * scale_factor
        + jnp.einsum("nk,dk->nd", grad_key, w_key, preferred_element_type=jnp.float32)
        + jnp.einsum("nk,dk->nd", grad_value, w_value, preferred_element_type=jnp.float32)
    )
    grad_input = grad_one + lax.psum_scatter(
        input_part.reshape(row_count, length, model_width).astype(jnp.bfloat16),
        "mp",
        scatter_dimension=1,
        tiled=True,
    ).astype(jnp.float32)
    frames_grad = jnp.where(skipped, cotangent_f, grad_input).astype(jnp.bfloat16)
    (
        w_query_grad,
        b_query_grad,
        w_key_grad,
        w_value_grad,
        b_value_grad,
        w_out_grad,
        w_up_grad,
        b_up_grad,
        w_down_grad,
    ) = lax.psum(
        (
            w_query_grad,
            b_query_grad,
            w_key_grad,
            w_value_grad,
            b_value_grad,
            w_out_grad,
            w_up_grad,
            b_up_grad,
            w_down_grad,
        ),
        "dp",
    )
    b_out_grad, gain_one_grad, shift_one_grad, b_down_grad, gain_two_grad, shift_two_grad = (
        lax.psum(
            (b_out_grad, gain_one_grad, shift_one_grad, b_down_grad, gain_two_grad, shift_two_grad),
            ("dp", "mp"),
        )
    )
    return (
        layer_out,
        frames_grad,
        w_query_grad,
        b_query_grad,
        w_key_grad,
        w_value_grad,
        b_value_grad,
        w_out_grad,
        b_out_grad,
        gain_one_grad,
        shift_one_grad,
        w_up_grad,
        b_up_grad,
        w_down_grad,
        b_down_grad,
        gain_two_grad,
        shift_two_grad,
    )


def solution(mesh):
    placed = (
        P("dp", "mp", None),
        P("dp", "mp", None),
        P("dp", None),
        P("dp", None),
        P("dp"),
        P(None, "mp"),
        P("mp"),
        P(None, "mp"),
        P(None, "mp"),
        P("mp"),
        P("mp", None),
        P(),
        P(),
        P(),
        P(None, "mp"),
        P("mp"),
        P("mp", None),
        P(),
        P(),
        P(),
    )
    return jax.shard_map(
        shards,
        mesh=mesh,
        in_specs=placed,
        out_specs=(
            P("dp", "mp", None),
            P("dp", "mp", None),
            P(None, "mp"),
            P("mp"),
            P(None, "mp"),
            P(None, "mp"),
            P("mp"),
            P("mp", None),
            P(),
            P(),
            P(),
            P(None, "mp"),
            P("mp"),
            P("mp", None),
            P(),
            P(),
            P(),
        ),
        check_vma=False,
    )
```

profile of v0, /device:TPU:1, one launch (start us, length us, event | category | flops | bytes accessed | tf_op | source)
XLA Modules:
  0.0 726.9 jit_solution(2856187410171125991)
XLA Ops:
  10.0 52.1 %all-gather.5.cloned.1.call-done = bf16[1,1536,768]{2,1,0:T(8,128)(2,1)} async-done(((bf16[1,384,768]{2,1,0:T(8,128)(2,1)}), bf16[1,1536,768]{2,1,0:T(8,128)(2,1)}) %all-gather.5.cloned.1.call-update) | async-done | bytes 2359312 | tf_op jit(solution)/shard_map/all_gather | solution.py:122
  65.8 2.7 convolution_convert_fusion.4
  69.6 27.1 %while.47 = (s32[]{:T(128)}, bf16[3,512,3,64]{1,3,2,0:T(8,128)(2,1)S(1)}, f32[3,3,512]{2,1,0:T(4,128)}, s32[3,512]{1,0:T(4,128)}, s32[1536]{0:T(1024)S(1)}, /*in...) while((s32[]{:T(128)}, ...), condition=%wide.region_3.4_spmd, body=%wide.region_0.3_spmd.sunk | while | flops 626884608 | bytes 33107068 | solution.py:47
  75.2 2.8 fusion.157
  84.3 2.8 fusion.157
  93.3 2.8 fusion.157
  98.2 3.0 convolution_bitcast_fusion.1
  101.3 84.3 %reduce-scatter.5.cloned.1.call-done = f32[1,384,768]{2,1,0:T(8,128)} async-done(((f32[1,1536,768]{2,1,0:T(8,128)}), f32[1,384,768]{2,1,0:T(8,128)}) %reduce-scatter.5.cloned.1.call-update) | async-done | bytes 1179664 | tf_op jit(solution)/shard_map/reduce_scatter | solution.py:141
  190.7 50.9 %all-gather.7.cloned.1.call-done = bf16[1,1536,768]{2,1,0:T(8,128)(2,1)} async-done(((bf16[1,384,768]{2,1,0:T(8,128)(2,1)}), bf16[1,1536,768]{2,1,0:T(8,128)(2,1)}) %all-gather.7.cloned.1.call-update) | async-done | bytes 2359312 | tf_op jit(solution)/shard_map/all_gather | solution.py:151
  241.5 14.7 %multiply_convert_fusion.1 = (bf16[1536,768]{1,0:T(8,128)(2,1)S(1)}, f32[1536,768]{1,0:T(8,128)}, f32[1536,768]{1,0:T(8,128)}) fusion(f32[768]{0:T(1024)} %param.39, bf16[768,768]{1,0:T(8,128)(2,1)S(1)} %copy-done, bf16[1,1536,768]{2,1,0:T(8,128)(2,1)} %all-gather.7.cloned.1.call-done), kind=kOutput, calls=%fused_computation.56 | convolution fusion | flops 1889796096 | bytes 15338496 | tf_op jit(solution)/shard_map/dot_general | solution.py:154
  257.6 3.4 fusion.46
  261.7 46.2 %reduce-scatter.7.cloned.1.call-done = bf16[1,384,768]{2,1,0:T(8,128)(2,1)} async-done(((bf16[1,1536,768]{2,1,0:T(8,128)(2,1)}), bf16[1,384,768]{2,1,0:T(8,128)(2,1)}) %reduce-scatter.7.cloned.1.call-update) | async-done | bytes 589840 | tf_op jit(solution)/shard_map/reduce_scatter | solution.py:158
  315.3 50.0 %all-gather.9.cloned.1.call-done = bf16[1,1536,768]{2,1,0:T(8,128)(2,1)} async-done(((bf16[1,384,768]{2,1,0:T(8,128)(2,1)}), bf16[1,1536,768]{2,1,0:T(8,128)(2,1)}) %all-gather.9.cloned.1.call-update) | async-done | bytes 2359312 | tf_op jit(solution)/shard_map/all_gather | solution.py:177
  365.3 8.7 %convert_reduce_fusion = (f32[768]{0:T(1024)}, bf16[1536,768]{1,0:T(8,128)(2,1)S(1)}) fusion(f32[1536,768]{1,0:T(8,128)} %get-tuple-element.348, bf16[768,768]{1,0:T(8,128)(2,1)} %param.40, bf16[1,1536,768]{2,1,0:T(8,128)(2,1)} %all-gather.9.cloned.1.call-done, f32[1536,768]{1,0:T(8,128)} %get-tuple-element.356, f32[768]{0:T(1024)} %param.39), kind=kOutput, calls=%fused_computation.53 | convolution fusion | flops 1831992576 | bytes 15341568 | tf_op jit(solution)/shard_map/nd,fd->nf/dot_general | solution.py:183
  375.5 3.5 fusion.47
  379.0 46.8 %reduce-scatter.9.cloned.1.call-done = bf16[1,384,768]{2,1,0:T(8,128)(2,1)} async-done(((bf16[1,1536,768]{2,1,0:T(8,128)(2,1)}), bf16[1,384,768]{2,1,0:T(8,128)(2,1)}) %reduce-scatter.9.cloned.1.call-update) | async-done | bytes 589840 | tf_op jit(solution)/shard_map/reduce_scatter | solution.py:192
  432.0 49.9 %all-gather.11.cloned.1.call-done = bf16[1,1536,768]{2,1,0:T(8,128)(2,1)} async-done(((bf16[1,384,768]{2,1,0:T(8,128)(2,1)}), bf16[1,1536,768]{2,1,0:T(8,128)(2,1)}) %all-gather.11.cloned.1.call-update) | async-done | bytes 2359312 | tf_op jit(solution)/shard_map/all_gather | solution.py:203
  481.9 3.4 convolution_convert_fusion.3
  490.4 46.8 %while.48 = (s32[]{:T(128)}, f32[1536,3,64]{0,2,1:T(8,128)S(1)}, f32[1536,3,64]{0,2,1:T(8,128)S(1)}, bf16[3,512,3,64]{1,3,2,0:T(8,128)(2,1)}, bf16[3,512,3,64]{1...) while((s32[]{:T(128)}, f32[1536,3,64]{0,2,1:T(8,128)S(1)}, ...), condition=%wide.region_17.18_spmd.clone, body=%wide.region_15.17_spmd.clone.sunk | while | flops 1541111808 | bytes 86183144 | solution.py:84
  496.6 3.4 multiply_reduce_fusion.6
  499.9 2.7 multiply_convert_fusion.3
  509.4 2.7 fusion.169
  512.1 3.4 multiply_reduce_fusion.6
  515.4 2.7 multiply_convert_fusion.3
  524.9 2.7 fusion.169
  527.6 3.4 multiply_reduce_fusion.6
  530.9 2.7 multiply_convert_fusion.3
  543.5 6.0 fusion.55
  549.5 3.5 fusion.61
  559.9 41.5 %all-reduce = (f32[768]{0:T(1024)}, f32[768]{0:T(1024)}, f32[768]{0:T(1024)}, f32[768]{0:T(1024)}, f32[768]{0:T(1024)}, /*index=5*/f32[768]{0:T(1024)}) all-reduce(f32[768]{0:T(1024)S(1)} %copy-done.46, f32[768]{0:T(1024)S(1)} %copy-done.44, f32[768]{0:T(1024)S(1)} %copy-done.45, ...), channel_id=1, replica_groups=mesh['dp'=8,'mp'=4] {'dp','mp'}, use_global_device_ids=true, to_apply=%region_28.29 | all-reduce | flops 4608 | bytes 36864 | tf_op jit(solution)/shard_map/psum | solution.py:268
  601.8 13.7 %all-reduce.1 = (f32[192]{0:T(256)}, f32[192]{0:T(256)}, f32[768]{0:T(1024)}) all-reduce(f32[192]{0:T(256)S(1)} %mul.229, f32[192]{0:T(256)S(1)} %reduce_sum.189, f32[768]{0:T(1024)S(1)} %copy-done.48), channel_id=1, replica_groups=mesh['dp'=8,'mp'=4] {'dp'}, use_global_device_ids=true, to_apply=%region_21.22 | all-reduce | flops 1152 | bytes 9216 | tf_op jit(solution)/shard_map/psum | solution.py:253
  617.7 92.6 %all-reduce.5.cloned.1.call-done = (f32[768,192]{0,1:T(8,128)}, f32[768,192]{0,1:T(8,128)}, f32[768,192]{0,1:T(8,128)}, f32[192,768]{1,0:T(8,128)}, f32[768,768]{1,0:T(8,128)}, /*index=5*/f32[768,768]{1,0:T(8,128)}) async-done(((f32[768,192]{0,1:T(8,128)}, f32[768,192]{0,1:T(8,128)}, f32[768,192]{0,1:T(8,128)}, f32[192,768]{1,0:T(8,128)}, f32[768,768]{1,0:T(8,128)}, /*index=5*/f32[768,768]{1,0:T(8,128)}), ...) | async-done | bytes 7077904 | tf_op jit(solution)/shard_map/psum | solution.py:253
  (234 shorter events, 101.9 us)
Async XLA Ops:
  7.2 234.3 %copy-start = (bf16[768,768]{1,0:T(8,128)(2,1)S(1)}, bf16[768,768]{1,0:T(8,128)(2,1)}, u32[]{:S(2)}) copy-start(bf16[768,768]{1,0:T(8,128)(2,1)} %param.38) | copy-start | bytes 3538948
  7.2 55.0 %all-gather.5.cloned.1.call-start = ((), (), s32[]{:S(2)}) async-start(), calls=%async_computation.4 | async-start | bytes 2949120 | tf_op jit(solution)/shard_map/all_gather | solution.py:122
  7.9 177.6 %reduce-scatter.5.cloned.1.call-start = ((), (), s32[]{:S(2)}) async-start(), calls=%async_computation.5 | async-start | bytes 5898240 | tf_op jit(solution)/shard_map/reduce_scatter | solution.py:141
  65.8 2.7 copy-start.28
  65.8 2.8 copy-start.50
  65.8 2.8 copy-start.54
  96.7 4.5 copy-start.4
  101.2 140.3 %all-gather.7.cloned.1.call-start = ((), (), s32[]{:S(2)}) async-start(), calls=%async_computation.6 | async-start | bytes 2949120 | tf_op jit(solution)/shard_map/all_gather | solution.py:151
  190.4 117.5 %reduce-scatter.7.cloned.1.call-start = ((), (), s32[]{:S(2)}) async-start(), calls=%async_computation.7 | async-start | bytes 2949120 | tf_op jit(solution)/shard_map/reduce_scatter | solution.py:158
  241.5 16.1 %copy-start.53 = (bf16[768,768]{1,0:T(8,128)(2,1)S(1)}, bf16[768,768]{1,0:T(8,128)(2,1)}, u32[]{:S(2)}) copy-start(bf16[768,768]{1,0:T(8,128)(2,1)} %param.40) | copy-start | bytes 3538948
  261.0 104.3 %all-gather.9.cloned.1.call-start = ((), (), s32[]{:S(2)}) async-start(), calls=%async_computation.8 | async-start | bytes 2949120 | tf_op jit(solution)/shard_map/all_gather | solution.py:177
  307.9 3.0 copy-start.9
  307.9 3.0 copy-start.49
  315.1 110.8 %reduce-scatter.9.cloned.1.call-start = ((), (), s32[]{:S(2)}) async-start(), calls=%async_computation.9 | async-start | bytes 2949120 | tf_op jit(solution)/shard_map/reduce_scatter | solution.py:192
  379.0 46.9 %copy-start.3 = (f32[1,384,768]{2,1,0:T(8,128)S(1)}, f32[1,384,768]{2,1,0:T(8,128)}, u32[]{:S(2)}) copy-start(f32[1,384,768]{2,1,0:T(8,128)} %copy-done.2) | copy-start | bytes 3538948
  379.0 102.9 %all-gather.11.cloned.1.call-start = ((), (), s32[]{:S(2)}) async-start(), calls=%async_computation.10 | async-start | bytes 2949120 | tf_op jit(solution)/shard_map/all_gather | solution.py:203
  429.0 2.9 copy-start.39
  431.7 183.8 %reduce-scatter.11.cloned.1.call-start = ((), (), s32[]{:S(2)}) async-start(), calls=%async_computation.11 | async-start | bytes 2949120 | tf_op jit(solution)/shard_map/reduce_scatter | solution.py:236
  543.4 166.9 %all-reduce.5.cloned.1.call-start = ((), (), s32[]{:S(2)}) async-start(), calls=%async_computation.12 | async-start | bytes 14155776 | tf_op jit(solution)/shard_map/psum | solution.py:253
  543.5 6.0 copy-start.15
  543.5 6.0 copy-start.18
  549.5 3.5 copy-start.14
  549.5 3.5 copy-start.52
  559.2 42.2 %copy-start.12 = (bf16[3,512,3,64]{1,3,2,0:T(8,128)(2,1)S(1)}, bf16[3,512,3,64]{1,3,2,0:T(8,128)(2,1)}, u32[]{:S(2)}) copy-start(bf16[3,512,3,64]{1,3,2,0:T(8,128)(2,1)} %get-tuple-element.188) | copy-start | bytes 1769476
  559.2 42.6 %copy-start.48 = (f32[768]{0:T(1024)S(1)}, f32[768]{0:T(1024)}, u32[]{:S(2)}) copy-start(f32[768]{0:T(1024)} %get-tuple-element.357) | copy-start | bytes 9220
  559.2 56.2 %copy-start.8 = (f32[1,384,768]{2,1,0:T(8,128)S(1)}, f32[1,384,768]{2,1,0:T(8,128)}, u32[]{:S(2)}) copy-start(f32[1,384,768]{2,1,0:T(8,128)} %copy-done.7) | copy-start | bytes 3538948
  559.2 56.2 %copy-start.11 = (bf16[1,384,768]{2,1,0:T(8,128)(2,1)S(1)}, bf16[1,384,768]{2,1,0:T(8,128)(2,1)}, u32[]{:S(2)}) copy-start(bf16[1,384,768]{2,1,0:T(8,128)(2,1)} %param.25) | copy-start | bytes 1769476
  559.2 56.2 %copy-start.40 = (f32[384]{0:T(512)S(1)}, f32[384]{0:T(512)}, u32[]{:S(2)}) copy-start(f32[384]{0:T(512)} %copy-done.39) | copy-start | bytes 4612
  710.3 4.0 copy-start.23
  710.3 4.8 copy-start.22
  710.3 5.6 copy-start.21
  715.9 3.9 copy-start.1
  (36 other events, 56.3 us)
Sparse Core Ops, SparseCore 0:
  9.6 52.5 all-gather.4
  101.3 84.1 reduce-scatter.4
  190.6 50.9 all-gather.6
  261.2 46.7 reduce-scatter.6
  315.2 50.0 all-gather.8
  379.1 46.7 reduce-scatter.8
  431.8 50.0 all-gather.10
  543.6 47.5 reduce-scatter.10
  596.4 113.8 all-reduce.4
where the time goes:
time: 735 us; the launch traced here: 727 us
  waiting for transfers between devices  474 us (64%)
  matrix products  108 us (15%)
  blocking collectives  55.2 us (8%)
  other arithmetic  39.6 us (5%)
  local copies, waits for them, and re-layouts  33.4 us (5%)
  between operations  15.5 us (2%)
    psum x1, waiting for transfers between devices, shards(): lax.psum((w_query_grad, b_query_grad, w_key_grad, w_value_grad, b_value_g...  92.6 us
    reduce_scatter x1, waiting for transfers between devices, shards(): lax.psum_scatter(attended_part.reshape(row_count, length, model_width), '...  84.3 us
    all_gather x1, waiting for transfers between devices, shards(): lax.all_gather(frames, 'mp', axis=1, tiled=True)  52.1 us
    all_gather x1, waiting for transfers between devices, shards(): lax.all_gather(normed_own.astype(jnp.bfloat16), 'mp', axis=1, tiled=True)  50.9 us
    all_gather x1, waiting for transfers between devices, shards(): lax.all_gather(grad_branch, 'mp', axis=1, tiled=True)  50 us
    all_gather x1, waiting for transfers between devices, shards(): lax.all_gather(grad_attended, 'mp', axis=1, tiled=True)  49.9 us
    reduce_scatter x1, waiting for transfers between devices, shards(): lax.psum_scatter(grad_normed_part.reshape(row_count, length, model_width)...  46.8 us
    reduce_scatter x1, waiting for transfers between devices, shards(): lax.psum_scatter(branch_part.reshape(row_count, length, model_width).asty...  46.2 us
  transfers between devices with their start and end apart: 9, of which 8 were waited for; matrix products, arithmetic and copies ran while one was open for 3% of the time, Pallas kernels for 0%

commit v1 on v0

v1 whole, which is shorter than its diff:
```python
import functools

import jax
import jax.numpy as jnp
from jax import lax
from jax.experimental import pallas as pl
from jax.experimental.pallas import tpu as pltpu
from jax.sharding import PartitionSpec as P

HEAD_DIM = 64
F32, BF16 = jnp.float32, jnp.bfloat16
VMEM = pl.BlockSpec(memory_space=pltpu.VMEM)
SMEM = pl.BlockSpec(memory_space=pltpu.SMEM)
LIMIT = 60 << 20


def mm(a, b, ca=1, cb=0):
    return lax.dot_general(a, b, (((ca,), (cb,)), ((), ())), preferred_element_type=F32)


def split3(v):
    hi = v.astype(BF16)
    rest = v - hi.astype(F32)
    mid = rest.astype(BF16)
    low = (rest - mid.astype(F32)).astype(BF16)
    return hi, mid, low


def pad_rows(parts, rows, width):
    parts = [p.astype(F32) for p in parts]
    have = sum(p.shape[0] for p in parts)
    return jnp.concatenate(parts + [jnp.zeros((rows - have, width), F32)], 0).astype(BF16)


def project(x, w_t, w_pad, bias_col, v_row, k_mask, one_hot, rows, q_aug, k_aug, v_aug, k_t, v_t):
    width = w_t.shape[0] // 3
    heads = width // HEAD_DIM
    every = mm(w_t, x, 1, 1) + bias_col
    every = jnp.concatenate([every[:width] * HEAD_DIM**-0.5, every[width:]], 0).astype(BF16)
    for h in range(heads):
        q_aug[h, 0:HEAD_DIM, rows] = every[h * HEAD_DIM : (h + 1) * HEAD_DIM]
        q_aug[h, HEAD_DIM : HEAD_DIM + 16, rows] = one_hot
        q_aug[h, HEAD_DIM + 16 :, rows] = jnp.zeros((48, x.shape[0]), BF16)
        k_t[h, :, rows] = every[width + h * HEAD_DIM : width + (h + 1) * HEAD_DIM]
        v_t[h, :, rows] = every[2 * width + h * HEAD_DIM : 2 * width + (h + 1) * HEAD_DIM]
    both = mm(x, w_pad, 1, 1)
    for h in range(heads):
        k_aug[h, rows, :] = both[:, h * 128 : (h + 1) * 128].astype(BF16) + k_mask
        at = (heads + h) * 128
        v_aug[h, rows, :] = (both[:, at : at + 128] + v_row[:, h * 128 : (h + 1) * 128]).astype(BF16)


def attend(h, cols, q_aug, k_aug, v_t, stats):
    scores = mm(k_aug[h], q_aug[h, :, cols])
    peak = jnp.max(scores, 0, keepdims=True)
    raised = jnp.exp(scores - peak)
    summed = jnp.sum(raised, 0, keepdims=True)
    mixed = mm(v_t[h], raised.astype(BF16)) / summed
    stats[h, :, cols] = jnp.broadcast_to(peak + jnp.log(summed), (8, mixed.shape[1]))
    return mixed.astype(BF16)


def local_forward_kernel(
    x_ref, w_ref, bias_ref, vrow_ref, kmask_ref, hot_ref,
    mixed_ref, q_aug, k_aug, v_aug, k_t, v_t, stats, w_pad
):
    heads = q_aug.shape[0]
    width = heads * HEAD_DIM
    w_pad[...] = jnp.zeros_like(w_pad)
    for i in range(2):
        for h in range(heads):
            w_pad[(i * heads + h) * 128 : (i * heads + h) * 128 + HEAD_DIM] = w_ref[
                (i + 1) * width + h * HEAD_DIM : (i + 1) * width + (h + 1) * HEAD_DIM
            ]
    length = x_ref.shape[0]
    block = 384

    def step(i, _):
        rows = pl.ds(pl.multiple_of(i * block, block), block)
        project(
            x_ref[rows, :], w_ref[...], w_pad[...], bias_ref[...], vrow_ref[...], kmask_ref[rows, :],
            hot_ref[:, rows], rows, q_aug, k_aug, v_aug, k_t, v_t,
        )
        return 0

    lax.fori_loop(0, length // block, step, 0)

    def attend_step(i, _):
        cols = pl.ds(pl.multiple_of(i * block, block), block)
        for h in range(heads):
            mixed_ref[i, h * HEAD_DIM : (h + 1) * HEAD_DIM, :] = attend(h, cols, q_aug, k_aug, v_t, stats)
        return 0

    lax.fori_loop(0, length // block, attend_step, 0)


MESH = pl.DeviceIdType.MESH
CHUNKS = 3


class Place:
    def __init__(self):
        self.d, self.z = lax.axis_index("dp"), lax.axis_index("mp")
        d, z = self.d, self.z
        self.b = d % 2
        self.p = z + self.b * (3 - 2 * z)
        self.sib = d + 1 - 2 * self.b
        self.q = (d // 2) % 4
        self.base = d - d % 8
        self.primary = self.p < 2
        self.rb = z // 2
        self.row = d - self.b + self.rb
        self.pp = z + self.rb * (3 - 2 * z)
        self.far = (z + 2) % 4
        self.group = jnp.where(self.primary, z, self.far)

    def own_line(self, place):
        return place + self.b * (3 - 2 * place)

    def line(self, place):
        return place + self.rb * (3 - 2 * place)

    def chip(self, k):
        return self.base + 2 * ((self.q + k) % 4) + self.b

    def barrier(self):
        sem = pltpu.get_barrier_semaphore()
        others = [((self.d), (self.z + k) % 4) for k in (1, 2, 3)]
        others += [(self.sib, (self.z + k) % 4) for k in range(4)]
        others += [(self.chip(k), self.z) for k in (1, 2, 3)]
        others += [(self.base + 2 * ((self.q + k) % 4) + 1 - self.b, self.z) for k in (1, 2, 3)]
        for dp, mp in others:
            pl.semaphore_signal(sem, inc=1, device_id=(dp, mp), device_id_type=MESH)
        pl.semaphore_wait(sem, len(others))

    def send(self, src, dst, send_sem, recv_sem, dp, mp):
        pltpu.make_async_remote_copy(
            src_ref=src, dst_ref=dst, send_sem=send_sem, recv_sem=recv_sem, device_id=(dp, mp), device_id_type=MESH
        ).start()

    def sent(self, src, send_sem):
        pltpu.make_async_remote_copy(
            src_ref=src, dst_ref=src, send_sem=send_sem, recv_sem=send_sem, device_id=(self.sib, self.z), device_id_type=MESH
        ).wait_send()

    def got(self, dst, recv_sem):
        pltpu.make_async_remote_copy(
            src_ref=dst, dst_ref=dst, send_sem=recv_sem, recv_sem=recv_sem, device_id=(self.sib, self.z), device_id_type=MESH
        ).wait_recv()


def forward_kernel(
    frames, w_own, small_own, kmask_own, hot_own, w_up, w_down, w_out,
    x_all, w_t, mixed_heads, mixed_own, q_aug, k_aug, v_aug, k_t, stats, small_all, up_all, down_all, out_all,
    relay, v_t, w_pad, kmask, hot,
    small_s, small_r, mask_s, mask_r, wq_s, wq_r, x_s, x_r, relay_r, on_s, fwd_s, mix_s, mix_r, local,
    p1_s, p2_s, p3_s, w_r,
):
    at = Place()
    heads = q_aug.shape[0]
    width = heads * HEAD_DIM
    share = frames.shape[0]
    step_rows = share // CHUNKS
    quarter = w_own.shape[0] // 4
    at.barrier()
    primary = at.primary
    secondary = jnp.logical_not(primary)
    z = at.z

    def rows(ch):
        return pl.ds(ch * step_rows, step_rows)

    def piece(m, chip, core):
        if m == 2:
            n = w_out.shape[0] // 4
            half = w_out.shape[1] // 2
            return (pl.ds(pl.multiple_of(chip * n, 16), n), pl.ds(pl.multiple_of(core * half, 128), half))
        n = w_up.shape[0] // 8
        return (pl.ds(pl.multiple_of((2 * chip + core) * n, 16), n), slice(None))

    mats = ((w_up, up_all), (w_down, down_all), (w_out, out_all))

    wq_rows = pl.ds(pl.multiple_of(at.q * quarter, 16), quarter)
    first = jnp.where(at.p == 0, 1, at.p - 1)

    @pl.when(primary)
    def _():
        at.send(w_own.at[wq_rows], w_t.at[wq_rows], wq_s.at[0], wq_r.at[at.q], at.d, at.far)

    for ch in range(CHUNKS):
        @pl.when(at.p < 3)
        def _():
            at.send(frames.at[rows(ch)], x_all.at[z, rows(ch)], on_s.at[z, ch], x_r.at[z, ch], at.d, at.own_line(first))

        @pl.when(at.p == 3)
        def _():
            at.send(frames.at[rows(ch)], relay.at[rows(ch)], on_s.at[z, ch], relay_r.at[ch], at.d, at.own_line(2))

    @pl.when(primary)
    def _():
        at.send(kmask_own, kmask, mask_s.at[0], mask_r.at[0], at.sib, z)
        at.send(hot_own, hot, mask_s.at[1], mask_r.at[1], at.sib, z)
        pltpu.make_async_copy(kmask_own, kmask, local.at[0]).start()
        pltpu.make_async_copy(hot_own, hot, local.at[1]).start()
        pltpu.make_async_copy(w_own, w_t, local.at[2]).start()
        pltpu.make_async_copy(frames, x_all.at[z], local.at[3]).start()
        for ch in range(CHUNKS):
            at.send(frames.at[rows(ch)], x_all.at[z, rows(ch)], fwd_s.at[z, ch], x_r.at[z, ch], at.sib, z)

    for k in (1, 2, 3):
        to = (z + k) % 4
        at.send(small_own, small_all.at[z], small_s.at[k - 1], small_r.at[z], at.d, to)
    pltpu.make_async_copy(small_own, small_all.at[z], local.at[4]).start()
    for m, (src, dst) in enumerate(mats):
        pltpu.make_async_copy(src, dst.at[z], local.at[5 + m]).start()

    @pl.when(at.p == 2)
    def _():
        for ch in range(CHUNKS):
            at.got(relay.at[rows(ch)], relay_r.at[ch])
            at.send(relay.at[rows(ch)], x_all.at[at.own_line(3), rows(ch)], x_s.at[ch], x_r.at[at.own_line(3), ch], at.d, at.own_line(1))

    @pl.when(secondary)
    def _():
        at.got(w_t.at[wq_rows], wq_r.at[at.q])
        for k in (1, 2, 3):
            at.send(w_t.at[wq_rows], w_t.at[wq_rows], wq_s.at[k], wq_r.at[at.q], at.chip(k), z)
        at.got(kmask, mask_r.at[0])
        at.got(hot, mask_r.at[1])

    @pl.when(primary)
    def _():
        pltpu.make_async_copy(kmask_own, kmask, local.at[0]).wait()
        pltpu.make_async_copy(hot_own, hot, local.at[1]).wait()
        pltpu.make_async_copy(w_own, w_t, local.at[2]).wait()
        pltpu.make_async_copy(frames, x_all.at[z], local.at[3]).wait()

    pltpu.make_async_copy(small_own, small_all.at[z], local.at[4]).wait()
    for k in (1, 2, 3):
        at.got(small_all.at[(z + k) % 4], small_r.at[(z + k) % 4])

    @pl.when(secondary)
    def _():
        for k in (1, 2, 3):
            other = (at.q + k) % 4
            at.got(w_t.at[pl.ds(pl.multiple_of(other * quarter, 16), quarter)], wq_r.at[other])

    w_pad[...] = jnp.zeros_like(w_pad)
    for i in range(2):
        for h in range(heads):
            w_pad[(i * heads + h) * 128 : (i * heads + h) * 128 + HEAD_DIM] = w_t[
                (i + 1) * width + h * HEAD_DIM : (i + 1) * width + (h + 1) * HEAD_DIM
            ]

    def shard_of(k):
        place = jnp.where(at.pp == 0, k, jnp.where(k == 0, 1, jnp.where(k == 1, 2, jnp.where(k == 2, 0, 3))))
        return place, at.line(place)

    def gather_step(k, _):
        place, s = shard_of(k)
        for ch in range(CHUNKS):
            block = x_all.at[s, rows(ch)]

            @pl.when(jnp.logical_or(k > 0, secondary))
            def _():
                at.got(block, x_r.at[s, ch])

            @pl.when(jnp.logical_and(k > 0, primary))
            def _():
                @pl.when(jnp.logical_and(at.p == 1, place >= 2))
                def _():
                    at.send(block, block, on_s.at[s, ch], x_r.at[s, ch], at.d, at.own_line(0))

                at.send(block, block, fwd_s.at[s, ch], x_r.at[s, ch], at.sib, z)

        cols = pl.ds(pl.multiple_of(s * share, share), share)
        biases = jnp.transpose(small_all[at.group])
        project(
            x_all[s], w_t[...], w_pad[...], biases[: 3 * width, 1:2], small_all[at.group, 2:3, : heads * 128], kmask[cols, :],
            hot[:, cols], cols, q_aug, k_aug, v_aug, k_t, v_t,
        )
        return 0

    lax.fori_loop(0, 4, gather_step, 0)

    for m, (src, dst) in enumerate(mats):
        r, c = piece(m, at.q, at.b)
        for k in (1, 2, 3):
            at.send(src.at[r, c], dst.at[z, r, c], p1_s.at[m, k - 1], w_r.at[m, z, 2 * at.q + at.b], at.d, (z + k) % 4)

    def spread(m):
        dst = mats[m][1]
        r, c = piece(m, at.q, at.b)
        for k in (1, 2, 3):
            s = (z + k) % 4
            sem = w_r.at[m, s, 2 * at.q + at.b]
            at.got(dst.at[s, r, c], sem)
            for j in (1, 2, 3):
                at.send(dst.at[s, r, c], dst.at[s, r, c], p2_s.at[m, k - 1, j], sem, at.chip(j), z)
            at.send(dst.at[s, r, c], dst.at[s, r, c], p2_s.at[m, k - 1, 0], sem, at.sib, z)

    def attend_step(i, _):
        cols = pl.ds(pl.multiple_of(i * share, share), share)
        for h in range(heads):
            mixed_heads[i, h * HEAD_DIM : (h + 1) * HEAD_DIM, :] = attend(h, cols, q_aug, k_aug, v_t, stats)
        mine = jnp.logical_and(primary, i == z)
        block = mixed_own.at[pl.ds(pl.multiple_of(at.group * width, 64), width)]

        @pl.when(mine)
        def _():
            pltpu.make_async_copy(mixed_heads.at[i], block, mix_s.at[i]).start()

        @pl.when(jnp.logical_not(mine))
        def _():
            at.send(mixed_heads.at[i], block, mix_s.at[i], mix_r.at[at.group], at.row, i)

        @pl.when(i == 1)
        def _():
            spread(0)

        @pl.when(i == 3)
        def _():
            spread(1)
            spread(2)

        return 0

    lax.fori_loop(0, 4, attend_step, 0)

    for m, (_, dst) in enumerate(mats):
        for j in (1, 2, 3):
            chip = (at.q + j) % 4
            r, c = piece(m, chip, at.b)
            for k in (1, 2, 3):
                s = (z + k) % 4
                sem = w_r.at[m, s, 2 * chip + at.b]
                at.got(dst.at[s, r, c], sem)
                at.send(dst.at[s, r, c], dst.at[s, r, c], p3_s.at[m, j - 1, k - 1], sem, at.sib, z)

    for g in range(4):
        mine = jnp.logical_and(primary, z == g)
        block = mixed_own.at[pl.ds(g * width, width)]

        @pl.when(jnp.logical_not(mine))
        def _():
            at.got(block, mix_r.at[g])

    for m, (src, dst) in enumerate(mats):
        pltpu.make_async_copy(src, dst.at[z], local.at[5 + m]).wait()
        for j in range(4):
            chip = (at.q + j) % 4
            r, c = piece(m, chip, 1 - at.b)
            for k in (1, 2, 3):
                s = (z + k) % 4
                at.got(dst.at[s, r, c], w_r.at[m, s, 2 * chip + 1 - at.b])

    for i in range(4):
        mine = jnp.logical_and(primary, z == i)

        @pl.when(mine)
        def _():
            block = mixed_own.at[pl.ds(pl.multiple_of(at.group * width, 64), width)]
            pltpu.make_async_copy(mixed_heads.at[i], block, mix_s.at[i]).wait()

        @pl.when(jnp.logical_not(mine))
        def _():
            at.sent(mixed_heads.at[i], mix_s.at[i])

    for k in range(3):
        at.sent(small_own, small_s.at[k])
    for ch in range(CHUNKS):
        at.sent(frames.at[rows(ch)], on_s.at[z, ch])

        @pl.when(at.p == 2)
        def _():
            at.sent(relay.at[rows(ch)], x_s.at[ch])

        @pl.when(at.p == 1)
        def _():
            for place in (2, 3):
                at.sent(x_all.at[at.own_line(place), rows(ch)], on_s.at[at.own_line(place), ch])

        @pl.when(primary)
        def _():
            for s in range(4):
                at.sent(x_all.at[s, rows(ch)], fwd_s.at[s, ch])

    @pl.when(primary)
    def _():
        at.sent(kmask_own, mask_s.at[0])
        at.sent(hot_own, mask_s.at[1])
        at.sent(w_own.at[wq_rows], wq_s.at[0])

    @pl.when(secondary)
    def _():
        for k in (1, 2, 3):
            at.sent(w_t.at[wq_rows], wq_s.at[k])

    for m, (src, dst) in enumerate(mats):
        r, c = piece(m, at.q, at.b)
        for k in range(3):
            at.sent(src.at[r, c], p1_s.at[m, k])
            for j in range(4):
                at.sent(src.at[r, c], p2_s.at[m, k, j])
            for j in range(3):
                at.sent(src.at[r, c], p3_s.at[m, j, k])


def run_forward(frames, w_t, small, kmask, hot, w_up, w_down, w_out):
    share, d = frames.shape
    length = hot.shape[1]
    width = w_t.shape[0] // 3
    heads = width // HEAD_DIM
    f = w_up.shape[1]
    any_ = pl.BlockSpec(memory_space=pl.ANY)
    dma, V = pltpu.SemaphoreType.DMA, pltpu.VMEM
    return pl.pallas_call(
        forward_kernel,
        out_shape=(
            S((4, share, d)), S(w_t.shape), S((4, width, share)), S((4 * width, share)),
            S((heads, 128, length)), S((heads, length, 128)), S((heads, length, 128)), S((heads, HEAD_DIM, length)),
            S((heads, 8, length), F32), S((4, 8, d), F32), S((4, d, f)), S((4, f, d)), S((4, width, d)),
        ),
        in_specs=[VMEM] * 5 + [any_] * 3, out_specs=[VMEM] * 10 + [any_] * 3,
        scratch_shapes=[
            V((share, d), BF16), V((heads, HEAD_DIM, length), BF16), V((2 * heads * 128, d), BF16),
            V((length, 128), BF16), V((16, length), BF16),
            dma((3,)), dma((4,)), dma((2,)), dma((2,)), dma((4,)), dma((4,)), dma((CHUNKS,)), dma((4, CHUNKS)), dma((CHUNKS,)),
            dma((4, CHUNKS)), dma((4, CHUNKS)), dma((4,)), dma((4,)), dma((8,)),
            dma((3, 3)), dma((3, 3, 4)), dma((3, 3, 3)), dma((3, 4, 8)),
        ],
        compiler_params=pltpu.CompilerParams(vmem_limit_bytes=LIMIT, collective_id=0, has_side_effects=True),
        name="attention_forward",
    )(frames, w_t, small, kmask, hot, w_up, w_down, w_out)


def norm_stats(v):
    centered = v - jnp.mean(v, -1, keepdims=True)
    r = lax.rsqrt(jnp.mean(centered * centered, -1, keepdims=True) + 1e-05)
    return centered * r, r


def norm_back(c, gain, hat, r):
    e = c * gain
    return r * (e - jnp.mean(e, -1, keepdims=True) - hat * jnp.mean(e * hat, -1, keepdims=True))


def middle_kernel(
    skip_ref, mixed_ref, frames_ref, cot_ref, vec_ref, bup_ref, wout_ref, wup_ref, wdown_ref,
    layer_ref, gone_ref, gmixed_ref, normed_ref, act_ref, ginner_ref, gbranch_ref, gatt_ref, small_ref,
    slope_ref,
):
    skipped = skip_ref[0] == 1
    b_out, gain_one, shift_one, b_down, gain_two, shift_two = (vec_ref[i : i + 1, :] for i in range(6))
    frames = frames_ref[...].astype(F32)
    attended = mm(mixed_ref[...], wout_ref[...], 0, 0) + b_out
    hat_one, r_one = norm_stats(frames + attended)
    normed = hat_one * gain_one + shift_one
    normed_ref[...] = normed.astype(BF16)
    parts = wup_ref.shape[0]
    branch = jnp.zeros_like(normed)
    for s in range(parts):
        inner = mm(normed_ref[...], wup_ref[s]) + bup_ref[s : s + 1, :]
        cdf = 0.5 * (1.0 + lax.erf(inner * (0.5**0.5)))
        slope_ref[s] = cdf + inner * (jnp.exp(-0.5 * inner * inner) * 0.3989422804014327)
        act = (inner * cdf).astype(BF16)
        act_ref[s] = act
        branch = branch + mm(act, wdown_ref[s])
    hat_two, r_two = norm_stats(normed + (branch + b_down))
    result = hat_two * gain_two + shift_two
    cot = cot_ref[...].astype(F32)
    layer_ref[...] = jnp.where(skipped, frames, result).astype(BF16)
    grad_out = jnp.where(skipped, 0.0, cot)
    grad_two = norm_back(grad_out, gain_two, hat_two, r_two)
    gbranch = grad_two.astype(BF16)
    gbranch_ref[...] = gbranch
    small_ref[0:1, :] = jnp.sum(gbranch.astype(F32), 0, keepdims=True)
    small_ref[1:2, :] = jnp.sum(grad_out * hat_two, 0, keepdims=True)
    small_ref[2:3, :] = jnp.sum(grad_out, 0, keepdims=True)
    grad_normed = grad_two
    for s in range(parts):
        gact = mm(gbranch_ref[...], wdown_ref[s], 1, 1)
        ginner = (gact * slope_ref[s]).astype(BF16)
        ginner_ref[s] = ginner
        small_ref[6 + s : 7 + s, :] = jnp.sum(ginner.astype(F32), 0, keepdims=True)
        grad_normed = grad_normed + mm(ginner, wup_ref[s], 1, 1)
    grad_one = norm_back(grad_normed, gain_one, hat_one, r_one)
    gone_ref[...] = grad_one
    gatt = grad_one.astype(BF16)
    gatt_ref[...] = gatt
    small_ref[3:4, :] = jnp.sum(gatt.astype(F32), 0, keepdims=True)
    small_ref[4:5, :] = jnp.sum(grad_normed * hat_one, 0, keepdims=True)
    small_ref[5:6, :] = jnp.sum(grad_normed, 0, keepdims=True)
    gmixed_ref[...] = mm(wout_ref[...], gatt, 1, 1).astype(BF16)


def attend_back(h, i, cols, q_aug, k_aug, v_aug, k_t, do_aug, dq_acc, dk_acc, dv_acc):
    weights = jnp.exp(mm(k_aug[h], q_aug[h, :, cols]))
    rounded = weights.astype(BF16)
    dv_acc[h] += mm(do_aug[h, 0:HEAD_DIM, cols], rounded, 1, 1)
    grad = (weights * mm(v_aug[h], do_aug[h, :, cols])).astype(BF16)
    dk_acc[h] += mm(q_aug[h, 0:HEAD_DIM, cols], grad, 1, 1)
    return mm(k_t[h], grad)


def backward_kernel(
    x_ref, w_ref, gmixed_ref, mixed_ref, stats, q_in, k_aug, v_aug, k_t,
    wgrad_ref, part_ref, bias_ref, unused_ref, q_aug, do_aug, dk_acc, dv_acc, grads
):
    heads = q_aug.shape[0]
    width = heads * HEAD_DIM
    length = x_ref.shape[0]
    block = 384
    n = length // block

    def prepare(i, _):
        cols = pl.ds(pl.multiple_of(i * block, block), block)
        for h in range(heads):
            at = slice(h * HEAD_DIM, (h + 1) * HEAD_DIM)
            do = gmixed_ref[i, at, :]
            do_aug[h, 0:HEAD_DIM, cols] = do
            inner = jnp.sum(do.astype(F32) * mixed_ref[i, at, :].astype(F32), 0, keepdims=True)
            parts = split3(-inner)
            do_aug[h, HEAD_DIM : HEAD_DIM + 16, cols] = pad_rows(parts, 16, block)
            do_aug[h, HEAD_DIM + 16 :, cols] = jnp.zeros((48, block), BF16)
            q_aug[h, 0:HEAD_DIM, cols] = q_in[h, 0:HEAD_DIM, cols]
            hot = q_in[h, HEAD_DIM : HEAD_DIM + 16, cols].astype(F32)[0:4]
            parts = split3(-stats[h, 0:1, cols])
            q_aug[h, HEAD_DIM : HEAD_DIM + 16, cols] = pad_rows((hot,) + parts, 16, block)
            q_aug[h, HEAD_DIM + 16 :, cols] = jnp.zeros((48, block), BF16)
        return 0

    lax.fori_loop(0, n, prepare, 0)
    dk_acc[...] = jnp.zeros_like(dk_acc)
    dv_acc[...] = jnp.zeros_like(dv_acc)

    def step(i, _):
        cols = pl.ds(pl.multiple_of(i * block, block), block)
        for h in range(heads):
            dq = attend_back(h, i, cols, q_aug, k_aug, v_aug, k_t, do_aug, None, dk_acc, dv_acc)
            grads[h * HEAD_DIM : (h + 1) * HEAD_DIM, cols] = dq.astype(BF16) * jnp.bfloat16(HEAD_DIM**-0.5)
        return 0

    lax.fori_loop(0, n, step, 0)
    for h in range(heads):
        at = width + h * HEAD_DIM
        grads[at : at + HEAD_DIM, :] = dk_acc[h].astype(BF16)
        at = 2 * width + h * HEAD_DIM
        grads[at : at + HEAD_DIM, :] = dv_acc[h].astype(BF16)
    wgrad_ref[...] = mm(grads[...], x_ref[...]).astype(BF16)
    bias_ref[...] = mm(jnp.ones((8, length), BF16), grads[...], 1, 1)

    def out_step(i, _):
        cols = pl.ds(pl.multiple_of(i * block, block), block)
        part_ref[cols, :] = mm(grads[:, cols], w_ref[...], 0, 0).astype(BF16)
        return 0

    lax.fori_loop(0, n, out_step, 0)


def weights_kernel(normed_ref, act_ref, ginner_ref, gbranch_ref, gatt_ref, mixed_ref, gup_ref, gdown_ref, gout_ref):
    for s in range(act_ref.shape[0]):
        gdown_ref[s] = mm(act_ref[s], gbranch_ref[...], 0, 0).astype(BF16)
        gup_ref[s] = mm(normed_ref[...], ginner_ref[s], 0, 0).astype(BF16)
    gout_ref[...] = mm(mixed_ref[...], gatt_ref[...]).astype(BF16)


def S(shape, dtype=BF16):
    return jax.ShapeDtypeStruct(shape, dtype)


def shards(
    frames, cotangent, segments, padding, skip_flag, w_query, b_query, w_key, w_value, b_value,
    w_out, b_out, gain_one, shift_one, w_up, b_up, w_down, b_down, gain_two, shift_two,
):
    mp = lax.axis_size("mp")
    share, d = frames.shape[1:]
    length = segments.shape[1]
    width = w_query.shape[1]
    heads = width // HEAD_DIM
    params = pltpu.CompilerParams(vmem_limit_bytes=LIMIT)
    scale = HEAD_DIM**-0.5
    own = frames[0]
    w_t = jnp.concatenate([w_query.T, w_key.T, w_value.T], 0)
    bias_col = jnp.concatenate([b_query, jnp.zeros_like(b_query), b_value])[:, None]
    v_row = jnp.concatenate(
        [b_value.reshape(heads, HEAD_DIM), jnp.ones((heads, 3)), jnp.zeros((heads, 61))], 1
    ).reshape(1, heads * 128)
    seg, pad = segments[0], padding[0]
    ids = jnp.arange(4)
    ok = (seg[:, None] == ids[None]) & (pad[:, None] == 1)
    k_mask = jnp.concatenate(
        [jnp.zeros((length, 64)), jnp.where(ok, 0.0, -1e30), jnp.ones((length, 3)), jnp.zeros((length, 57))], 1
    ).astype(BF16)
    hot = jnp.concatenate([(seg[None] == ids[:, None]).astype(BF16), jnp.zeros((12, length), BF16)], 0)

    everything = lax.all_gather(own, "mp", axis=0, tiled=True)
    mixed, q_aug, k_aug, v_aug, k_t, v_t, stats = pl.pallas_call(
        local_forward_kernel,
        out_shape=(
            S((mp, width, share)), S((heads, 128, length)), S((heads, length, 128)), S((heads, length, 128)),
            S((heads, HEAD_DIM, length)), S((heads, HEAD_DIM, length)), S((heads, 8, length), F32),
        ),
        in_specs=[VMEM] * 6, out_specs=[VMEM] * 7,
        scratch_shapes=[pltpu.VMEM((2 * heads * 128, d), BF16)],
        compiler_params=params, name="local_forward",
    )(everything, w_t, bias_col, v_row, k_mask, hot)
    zero = jnp.zeros((d,), F32)
    bias_row = jnp.concatenate([b_query, jnp.zeros_like(b_query), b_value, jnp.zeros((d - 3 * width,), F32)])
    v_row2 = jnp.concatenate([v_row[0], jnp.zeros((d - heads * 128,), F32)])
    small = jnp.stack([b_up, bias_row, v_row2] + [zero] * 5)
    _, _, _, mixed_own, _, _, _, _, _, small_all, wup, wdown, wout = run_forward(
        own, w_t, small, k_mask, hot, w_up, w_down, w_out
    )
    wout = wout.reshape(mp * width, d)
    bup = small_all[:, 0]
    vec = jnp.stack([b_out, gain_one, shift_one, b_down, gain_two, shift_two] + [b_out] * 2)
    f = w_up.shape[1]
    layer, gone, gmixed, normed, act, ginner, gbranch, gatt, small = pl.pallas_call(
        middle_kernel,
        out_shape=(
            S((share, d)), S((share, d), F32), S((mp * width, share)), S((share, d)), S((mp, share, f)),
            S((mp, share, f)), S((share, d)), S((share, d)), S((16, d), F32),
        ),
        in_specs=[SMEM] + [VMEM] * 8, out_specs=[VMEM] * 9,
        scratch_shapes=[pltpu.VMEM((mp, share, f), F32)],
        compiler_params=params, name="feed_forward",
    )(skip_flag, mixed_own, own, cotangent[0], vec, bup, wout, wup, wdown)
    gup, gdown, gout = pl.pallas_call(
        weights_kernel,
        out_shape=(S((mp, d, f)), S((mp, f, d)), S((mp * width, d))),
        in_specs=[VMEM] * 6, out_specs=[VMEM] * 3, compiler_params=params, name="weight_grads",
    )(normed, act, ginner, gbranch, gatt, mixed_own)
    gmixed_heads = lax.all_to_all(gmixed.reshape(mp, width, share), "mp", 0, 0)
    wgrad, part, bias = pl.pallas_call(
        backward_kernel,
        out_shape=(S((3 * width, d)), S((length, d)), S((8, 3 * width), F32), S((16, 128), F32)),
        in_specs=[VMEM] * 9, out_specs=[VMEM] * 4,
        scratch_shapes=[
            pltpu.VMEM((heads, 128, length), BF16), pltpu.VMEM((heads, 128, length), BF16),
            pltpu.VMEM((heads, HEAD_DIM, length), F32), pltpu.VMEM((heads, HEAD_DIM, length), F32),
            pltpu.VMEM((3 * width, length), BF16),
        ],
        compiler_params=params, name="attention_backward",
    )(everything, w_t, gmixed_heads, mixed, stats, q_aug, k_aug, v_aug, k_t)[:3]
    dx = lax.psum_scatter(part, "mp", scatter_dimension=0, tiled=True).astype(F32)
    skipped = (skip_flag == 1)[0]
    frames_grad = jnp.where(skipped, cotangent[0].astype(F32), gone + dx).astype(BF16)
    wgrad = lax.psum(wgrad, "dp").astype(F32)
    bias = lax.psum(bias[0], "dp")
    gup = lax.psum(lax.psum_scatter(gup, "mp"), "dp").astype(F32)
    gdown = lax.psum(lax.psum_scatter(gdown, "mp"), "dp").astype(F32)
    gout = lax.psum(lax.psum_scatter(gout.reshape(mp, width, d), "mp"), "dp").astype(F32)
    small = lax.psum(small, ("dp", "mp"))
    z = lax.axis_index("mp")
    return (
        layer[None], frames_grad[None],
        wgrad[:width].T, bias[:width], wgrad[width : 2 * width].T, wgrad[2 * width :].T, bias[2 * width :],
        gout, small[3], small[4], small[5],
        gup, small[6 + z], gdown, small[0], small[1], small[2],
    )


def solution(mesh):
    split = (P("dp", "mp", None), P(None, "mp"), P("mp"), P("mp", None), P())
    row, col, one, top, rep = split
    return jax.shard_map(
        shards,
        mesh=mesh,
        in_specs=(row, row, P("dp", None), P("dp", None), P("dp"), col, one, col, col, one, top, rep, rep, rep, col, one, top, rep, rep, rep),
        out_specs=(row, row, col, one, col, col, one, top, rep, rep, rep, col, one, top, rep, rep, rep),
        check_vma=False,
    )
```

time: 735 us -> 552 us (0.75)
  waiting for transfers between devices: 474 us -> 230 us
  Pallas kernels: 0 us -> 214 us
  matrix products: 108 us -> 0 us
  other arithmetic: 39.6 us -> 14.4 us
  local copies, waits for them, and re-layouts: 33.4 us -> 11.7 us
  starting transfers between devices: 1 us -> 8.9 us
    pallas_call x0 -> x5, Pallas kernels: none -> 214 us  [the longest x1 137 us: run_forward(): pl.pallas_call(forward_kernel, out_shape=(S((4, share, d)), S(w_t.shape),...]
    all_gather x4 -> x1, waiting for transfers between devices: 203 us -> 0.01 us  [shards(): everything = lax.all_gather(own, 'mp', axis=0, tiled=True)]
    dot_general x39 -> x0, matrix products: 108 us -> none  [the longest x1 14.7 us: shards(): jnp.dot(normed_low, w_up, preferred_element_type=jnp.float32) + b_up]
    reduce_scatter x4, waiting for transfers between devices: 177 us -> 150 us  [the longest x1 88 us: shards(): gdown = lax.psum(lax.psum_scatter(gdown, 'mp'), 'dp').astype(F32)]
    psum x1, waiting for transfers between devices: 92.6 us -> 69.1 us  [shards(): wgrad = lax.psum(wgrad, 'dp').astype(F32)]
    reduce_sum x15 -> x0, other arithmetic: 20.7 us -> none  [the longest x3 7.79 us: one_block(): summed = jnp.sum(raised, -1, keepdims=True)]
    unnamed x115 -> x31, local copies, waits for them, and re-layouts: 20.5 us -> 2.95 us
    all_to_all x0 -> x1, waiting for transfers between devices: none -> 8.77 us  [shards(): gmixed_heads = lax.all_to_all(gmixed.reshape(mp, width, share), 'mp', 0, 0)]
  transfers between devices with their start and end apart: 9 -> 7, of which waited for: 8 -> 4; matrix products, arithmetic and copies ran while one was open for 3% -> 3% of each run, Pallas kernels for 0% -> 39%
where the time goes in v1:
time: 552 us; the launch traced here: 550 us
  waiting for transfers between devices  230 us (42%)
  Pallas kernels  214 us (39%)
  blocking collectives  55.6 us (10%)
  between operations  15 us (3%)
  other arithmetic  14.4 us (3%)
  local copies, waits for them, and re-layouts  11.7 us (2%)
  starting transfers between devices  8.9 us (2%)
    pallas_call x1, Pallas kernels, run_forward(): pl.pallas_call(forward_kernel, out_shape=(S((4, share, d)), S(w_t.shape),...  137 us
    reduce_scatter x1, waiting for transfers between devices, shards(): gdown = lax.psum(lax.psum_scatter(gdown, 'mp'), 'dp').astype(F32)  88 us
    psum x1, waiting for transfers between devices, shards(): wgrad = lax.psum(wgrad, 'dp').astype(F32)  69.1 us
    reduce_scatter x1, waiting for transfers between devices, shards(): gup = lax.psum(lax.psum_scatter(gup, 'mp'), 'dp').astype(F32)  62.5 us
    psum x1, blocking collectives, shards(): small = lax.psum(small, ('dp', 'mp'))  43.5 us
    pallas_call x1, Pallas kernels, shards(): pl.pallas_call(backward_kernel, out_shape=(S((3 * width, d)), S((length,...  27.3 us
    pallas_call x1, Pallas kernels, shards(): pl.pallas_call(local_forward_kernel, out_shape=(S((mp, width, share)), S(...  20.7 us
    pallas_call x1, Pallas kernels, shards(): pl.pallas_call(middle_kernel, out_shape=(S((share, d)), S((share, d), F32...  17.5 us
  transfers between devices with their start and end apart: 7, of which 4 were waited for; matrix products, arithmetic and copies ran while one was open for 3% of the time, Pallas kernels for 39%

profile of v1, /device:TPU:1, one launch (start us, length us, event | category | flops | bytes accessed | tf_op | source)
XLA Modules:
  0.0 550.0 jit_solution(11826237950553279402)
XLA Ops:
  7.2 0.7 all-gather.3.cloned.1.call-update
  8.2 0.8 reshape.59
  9.1 0.8 pad_maximum_fusion.1
  9.9 0.7 stack.38
  10.6 0.7 reduce
  12.0 0.7 compare_reduce_fusion
  12.7 2.1 pad_maximum_fusion.w_own.w_ref
  15.5 1.1 select_convert_fusion.1
  16.5 1.0 maximum_maximum_fusion.kmask_own.kmask_ref
  17.5 137.0 %attention_forward.1 = (bf16[4,384,768]{2,1,0:T(8,128)(2,1)}, bf16[576,768]{1,0:T(8,128)(2,1)}, bf16[4,192,384]{2,1,0:T(8,128)(2,1)}, bf16[768,384]{1,0:T(8,128)...) custom-call(bf16[384,768]{1,0:T(8,128)(2,1)} %bitcast.35, ...), custom_call_target="tpu_custom_call" | custom-call | tf_op jit(solution)/shard_map/attention_forward/pallas_call | solution.py:417
  154.6 0.9 copy.38
  157.5 17.5 %feed_forward.1 = (bf16[384,768]{1,0:T(8,128)(2,1)}, f32[384,768]{1,0:T(8,128)}, bf16[768,384]{1,0:T(8,128)(2,1)}, bf16[384,768]{1,0:T(8,128)(2,1)}, bf16[4,384,...) custom-call(s32[1]{0:T(128)S(6)} %copy.47.skip_ref, ...), custom_call_target="tpu_custom_call" | custom-call | tf_op jit(solution)/shard_map/feed_forward/pallas_call | solution.py:619
  175.0 11.6 %weight_grads.1 = (bf16[4,768,768]{2,1,0:T(8,128)(2,1)}, bf16[4,768,768]{2,1,0:T(8,128)(2,1)}, bf16[768,768]{1,0:T(8,128)(2,1)}) custom-call(bf16[384,768]{1,0:T(8,128)(2,1)} %get-tuple-element.60.normed_ref, bf16[4,384,768]{2,1,0:T(8,128)(2,1)} %get-tuple-element.61.act_ref, bf16[4,384,768]{2,1,0:T(8,128)(2,1)} %get-tuple-element.62.ginner_ref, ...), custom_call_target="tpu_custom_call" | custom-call | tf_op jit(solution)/shard_map/weight_grads/pallas_call | solution.py:629
  188.0 8.7 %all-to-all-start = ((bf16[4,192,384]{2,1,0:T(8,128)(2,1)}), bf16[4,192,384]{2,1,0:T(8,128)(2,1)S(1)}, u32[]{:S(2)}, u32[]{:S(2)}) async-start(bf16[4,192,384]{2,1,0:T(8,128)(2,1)} %bitcast.11), calls=%async_computation | async-start | bytes 1179648 | tf_op jit(solution)/shard_map/all_to_all | solution.py:634
  196.8 0.9 broadcast_in_dim.42.bias_ref
  198.2 20.7 %local_forward.1 = (bf16[4,192,384]{2,1,0:T(8,128)(2,1)}, bf16[3,128,1536]{2,1,0:T(8,128)(2,1)}, bf16[3,1536,128]{2,1,0:T(8,128)(2,1)}, bf16[3,1536,128]{2,1,0:T...) custom-call(bf16[1536,768]{1,0:T(8,128)(2,1)} %bitcast.33, ...), custom_call_target="tpu_custom_call" | custom-call | tf_op jit(solution)/shard_map/local_forward/pallas_call | solution.py:598
  218.9 8.8 %all-to-all-done.gmixed_ref = bf16[4,192,384]{2,1,0:T(8,128)(2,1)S(1)} async-done(((bf16[4,192,384]{2,1,0:T(8,128)(2,1)}), bf16[4,192,384]{2,1,0:T(8,128)(2,1)S(1)}, u32[]{:S(2)}, u32[]{:S(2)}) %all-to-all-start) | async-done | bytes 589856 | tf_op jit(solution)/shard_map/all_to_all | solution.py:634
  227.7 0.8 copy-done
  228.5 27.3 %attention_backward.1 = (bf16[576,768]{1,0:T(8,128)(2,1)}, bf16[1536,768]{1,0:T(8,128)(2,1)}, f32[8,576]{1,0:T(8,128)}, f32[16,128]{1,0:T(8,128)}) custom-call(bf16[1536,768]{1,0:T(8,128)(2,1)} %bitcast.34, bf16[576,768]{1,0:T(8,128)(2,1)} %pad_maximum_fusion.w_own.w_ref, bf16[4,192,384]{2,1,0:T(8,128)(2,1)} %copy-done, ...), custom_call_target="tpu_custom_call" | custom-call | tf_op jit(solution)/shard_map/attention_backward/pallas_call | solution.py:635
  255.9 62.5 %reduce-scatter.9.cloned.1.call-done = bf16[1,768,768]{2,1,0:T(8,128)(2,1)} async-done(((bf16[4,768,768]{2,1,0:T(8,128)(2,1)}), bf16[1,768,768]{2,1,0:T(8,128)(2,1)}) %reduce-scatter.9.cloned.1.call-update) | async-done | bytes 1179664 | tf_op jit(solution)/shard_map/reduce_scatter | solution.py:651
  318.4 88.0 %reduce-scatter.11.cloned.1.call-done = bf16[1,768,768]{2,1,0:T(8,128)(2,1)} async-done(((bf16[4,768,768]{2,1,0:T(8,128)(2,1)}), bf16[1,768,768]{2,1,0:T(8,128)(2,1)}) %reduce-scatter.11.cloned.1.call-update) | async-done | bytes 1179664 | tf_op jit(solution)/shard_map/reduce_scatter | solution.py:652
  406.4 0.8 copy-done.6
  407.2 43.5 %psum.45 = f32[16,768]{1,0:T(8,128)S(1)} all-reduce(f32[16,768]{1,0:T(8,128)S(1)} %copy-done.6), channel_id=1, replica_groups=mesh['dp'=8,'mp'=4] {'dp','mp'}, use_global_device_ids=true, to_apply=%region_5.6 | all-reduce | flops 12288 | bytes 98304 | tf_op jit(solution)/shard_map/psum | solution.py:654
  451.4 0.7 slice_reduce_fusion.6
  452.1 12.1 %psum.43 = f32[576]{0:T(1024)S(1)} all-reduce(f32[576]{0:T(1024)S(1)} %slice_reduce_fusion.6), channel_id=1, replica_groups=mesh['dp'=8,'mp'=4] {'dp'}, use_global_device_ids=true, to_apply=%region_2.3 | all-reduce | flops 576 | bytes 4608 | tf_op jit(solution)/shard_map/psum | solution.py:650
  464.7 2.1 fusion.1
  466.8 69.1 %all-reduce.5.cloned.1.call-done = (bf16[576,768]{1,0:T(8,128)(2,1)}, bf16[192,768]{1,0:T(8,128)(2,1)}, bf16[768,768]{1,0:T(8,128)(2,1)}, bf16[768,768]{1,0:T(8,128)(2,1)}) async-done(((bf16[576,768]{1,0:T(8,128)(2,1)}, bf16[192,768]{1,0:T(8,128)(2,1)}, bf16[768,768]{1,0:T(8,128)(2,1)}, bf16[768,768]{1,0:T(8,128)(2,1)}), (bf16[576,768]{1,0:T(8,128)(2,1)}, bf16[192,768]{1,0:T(8,128)(2,1)}, ...) | async-done | bytes 3538960 | tf_op jit(solution)/shard_map/psum | solution.py:649
  535.9 1.3 convert_element_type.26
  537.2 1.2 slice_bitcast_fusion
  539.1 1.6 convert_element_type.28
  540.7 1.6 convert_element_type.29
  542.3 0.9 convert_element_type.27
  (74 shorter events, 7.1 us)
Async XLA Ops:
  7.2 191.0 %all-gather.3.cloned.1.call-start = ((), (), s32[]{:S(2)}) async-start(), calls=%async_computation.9 | async-start | bytes 2949120 | tf_op jit(solution)/shard_map/all_gather | solution.py:597
  7.9 248.0 %reduce-scatter.7.cloned.1.call-start = ((), (), s32[]{:S(2)}) async-start(), calls=%async_computation.6 | async-start | bytes 1474560 | tf_op jit(solution)/shard_map/reduce_scatter | solution.py:653
  17.5 138.7 %copy-start.9 = (f32[768]{0:T(1024)S(1)}, f32[768]{0:T(1024)}, u32[]{:S(2)}) copy-start(f32[768]{0:T(1024)} %param.31) | copy-start | bytes 9220
  17.5 138.7 %copy-start.10 = (f32[768]{0:T(1024)S(1)}, f32[768]{0:T(1024)}, u32[]{:S(2)}) copy-start(f32[768]{0:T(1024)} %param.32) | copy-start | bytes 9220
  17.5 138.7 %copy-start.11 = (f32[768]{0:T(1024)S(1)}, f32[768]{0:T(1024)}, u32[]{:S(2)}) copy-start(f32[768]{0:T(1024)} %param.33) | copy-start | bytes 9220
  17.5 138.7 %copy-start.12 = (f32[768]{0:T(1024)S(1)}, f32[768]{0:T(1024)}, u32[]{:S(2)}) copy-start(f32[768]{0:T(1024)} %param.37) | copy-start | bytes 9220
  17.5 138.7 %copy-start.13 = (f32[768]{0:T(1024)S(1)}, f32[768]{0:T(1024)}, u32[]{:S(2)}) copy-start(f32[768]{0:T(1024)} %param.38) | copy-start | bytes 9220
  17.5 138.7 %copy-start.14 = (f32[768]{0:T(1024)S(1)}, f32[768]{0:T(1024)}, u32[]{:S(2)}) copy-start(f32[768]{0:T(1024)} %param.39) | copy-start | bytes 9220
  186.6 131.7 %reduce-scatter.9.cloned.1.call-start = ((), (), s32[]{:S(2)}) async-start(), calls=%async_computation.7 | async-start | bytes 5898240 | tf_op jit(solution)/shard_map/reduce_scatter | solution.py:651
  187.4 219.0 %reduce-scatter.11.cloned.1.call-start = ((), (), s32[]{:S(2)}) async-start(), calls=%async_computation.8 | async-start | bytes 5898240 | tf_op jit(solution)/shard_map/reduce_scatter | solution.py:652
  188.0 8.7 %copy-start.7 = (f32[192]{0:T(256)S(1)}, f32[192]{0:T(256)}, u32[]{:S(2)}) copy-start(f32[192]{0:T(256)} %param.29) | copy-start | bytes 2308
  188.0 8.7 %copy-start.8 = (f32[192]{0:T(256)S(1)}, f32[192]{0:T(256)}, u32[]{:S(2)}) copy-start(f32[192]{0:T(256)} %param.26) | copy-start | bytes 2308
  188.0 39.7 %all-to-all-start = ((bf16[4,192,384]{2,1,0:T(8,128)(2,1)}), bf16[4,192,384]{2,1,0:T(8,128)(2,1)S(1)}, u32[]{:S(2)}, u32[]{:S(2)}) async-start(bf16[4,192,384]{2,1,0:T(8,128)(2,1)} %bitcast.11), calls=%async_computation | async-start | bytes 1179648 | tf_op jit(solution)/shard_map/all_to_all | solution.py:634
  196.7 268.1 %reduce-scatter.5.cloned.1.call-start = ((), (), s32[]{:S(2)}) async-start(), calls=%async_computation.5 | async-start | bytes 2949120 | tf_op jit(solution)/shard_map/reduce_scatter | solution.py:646
  227.7 0.8 copy-start
  255.8 280.0 %all-reduce.5.cloned.1.call-start = ((), (), s32[]{:S(2)}) async-start(), calls=%async_computation.10 | async-start | bytes 7077888 | tf_op jit(solution)/shard_map/psum | solution.py:649
  406.4 0.8 copy-start.6
  406.4 58.4 %copy-start.1 = (bf16[1,384,768]{2,1,0:T(8,128)(2,1)S(1)}, bf16[1,384,768]{2,1,0:T(8,128)(2,1)}, u32[]{:S(2)}) copy-start(bf16[1,384,768]{2,1,0:T(8,128)(2,1)} %param.21) | copy-start | bytes 1769476
  406.4 58.4 %copy-start.2 = (f32[384,768]{1,0:T(8,128)S(1)}, f32[384,768]{1,0:T(8,128)}, u32[]{:S(2)}) copy-start(f32[384,768]{1,0:T(8,128)} %get-tuple-element.49) | copy-start | bytes 3538948
  537.1 1.9 copy-start.4
  539.1 1.7 copy-start.3
  540.7 1.6 copy-start.5
Sparse Core Ops, SparseCore 0:
  9.6 65.4 all-gather.2
  186.8 43.2 reduce-scatter.6
  232.4 85.9 reduce-scatter.8
  320.5 85.7 reduce-scatter.10
  409.1 49.2 reduce-scatter.4
  461.9 73.9 all-reduce.4

commit v2 on v1

--- a/solution.py
+++ b/solution.py
@@ -50,48 +50,15 @@
         v_aug[h, rows, :] = (both[:, at : at + 128] + v_row[:, h * 128 : (h + 1) * 128]).astype(BF16)
 
 
-def attend(h, cols, q_aug, k_aug, v_t, stats):
+def attend(h, cols, q_aug, k_aug, v_t):
     scores = mm(k_aug[h], q_aug[h, :, cols])
     peak = jnp.max(scores, 0, keepdims=True)
     raised = jnp.exp(scores - peak)
     summed = jnp.sum(raised, 0, keepdims=True)
     mixed = mm(v_t[h], raised.astype(BF16)) / summed
-    stats[h, :, cols] = jnp.broadcast_to(peak + jnp.log(summed), (8, mixed.shape[1]))
+    one_hot = q_aug[h, HEAD_DIM : HEAD_DIM + 16, cols].astype(F32)[0:4]
+    q_aug[h, HEAD_DIM : HEAD_DIM + 16, cols] = pad_rows((one_hot,) + split3(-(peak + jnp.log(summed))), 16, mixed.shape[1])
     return mixed.astype(BF16)
-
-
-def local_forward_kernel(
-    x_ref, w_ref, bias_ref, vrow_ref, kmask_ref, hot_ref,
-    mixed_ref, q_aug, k_aug, v_aug, k_t, v_t, stats, w_pad
-):
-    heads = q_aug.shape[0]
-    width = heads * HEAD_DIM
-    w_pad[...] = jnp.zeros_like(w_pad)
-    for i in range(2):
-        for h in range(heads):
-            w_pad[(i * heads + h) * 128 : (i * heads + h) * 128 + HEAD_DIM] = w_ref[
-                (i + 1) * width + h * HEAD_DIM : (i + 1) * width + (h + 1) * HEAD_DIM
-            ]
-    length = x_ref.shape[0]
-    block = 384
-
-    def step(i, _):
-        rows = pl.ds(pl.multiple_of(i * block, block), block)
-        project(
-            x_ref[rows, :], w_ref[...], w_pad[...], bias_ref[...], vrow_ref[...], kmask_ref[rows, :],
-            hot_ref[:, rows], rows, q_aug, k_aug, v_aug, k_t, v_t,
-        )
-        return 0
-
-    lax.fori_loop(0, length // block, step, 0)
-
-    def attend_step(i, _):
-        cols = pl.ds(pl.multiple_of(i * block, block), block)
-        for h in range(heads):
-            mixed_ref[i, h * HEAD_DIM : (h + 1) * HEAD_DIM, :] = attend(h, cols, q_aug, k_aug, v_t, stats)
-        return 0
-
-    lax.fori_loop(0, length // block, attend_step, 0)
 
 
 MESH = pl.DeviceIdType.MESH
@@ -123,12 +90,15 @@
     def chip(self, k):
         return self.base + 2 * ((self.q + k) % 4) + self.b
 
+    def other(self, k):
+        return self.base + 2 * ((self.q + k) % 4) + 1 - self.b
+
     def barrier(self):
         sem = pltpu.get_barrier_semaphore()
         others = [((self.d), (self.z + k) % 4) for k in (1, 2, 3)]
         others += [(self.sib, (self.z + k) % 4) for k in range(4)]
         others += [(self.chip(k), self.z) for k in (1, 2, 3)]
-        others += [(self.base + 2 * ((self.q + k) % 4) + 1 - self.b, self.z) for k in (1, 2, 3)]
+        others += [(self.other(k), self.z) for k in (1, 2, 3)]
         for dp, mp in others:
             pl.semaphore_signal(sem, inc=1, device_id=(dp, mp), device_id_type=MESH)
         pl.semaphore_wait(sem, len(others))
@@ -151,7 +121,7 @@
 
 def forward_kernel(
     frames, w_own, small_own, kmask_own, hot_own, w_up, w_down, w_out,
-    x_all, w_t, mixed_heads, mixed_own, q_aug, k_aug, v_aug, k_t, stats, small_all, up_all, down_all, out_all,
+    x_all, w_t, mixed_heads, mixed_own, q_aug, k_aug, v_aug, k_t, small_all, up_all, down_all, out_all,
     relay, v_t, w_pad, kmask, hot,
     small_s, small_r, mask_s, mask_r, wq_s, wq_r, x_s, x_r, relay_r, on_s, fwd_s, mix_s, mix_r, local,
     p1_s, p2_s, p3_s, w_r,
@@ -302,7 +272,7 @@
     def attend_step(i, _):
         cols = pl.ds(pl.multiple_of(i * share, share), share)
         for h in range(heads):
-            mixed_heads[i, h * HEAD_DIM : (h + 1) * HEAD_DIM, :] = attend(h, cols, q_aug, k_aug, v_t, stats)
+            mixed_heads[i, h * HEAD_DIM : (h + 1) * HEAD_DIM, :] = attend(h, cols, q_aug, k_aug, v_t)
         mine = jnp.logical_and(primary, i == z)
         block = mixed_own.at[pl.ds(pl.multiple_of(at.group * width, 64), width)]
 
@@ -419,9 +389,9 @@
         out_shape=(
             S((4, share, d)), S(w_t.shape), S((4, width, share)), S((4 * width, share)),
             S((heads, 128, length)), S((heads, length, 128)), S((heads, length, 128)), S((heads, HEAD_DIM, length)),
-            S((heads, 8, length), F32), S((4, 8, d), F32), S((4, d, f)), S((4, f, d)), S((4, width, d)),
+            S((4, 8, d), F32), S((4, d, f)), S((4, f, d)), S((4, width, d)),
         ),
-        in_specs=[VMEM] * 5 + [any_] * 3, out_specs=[VMEM] * 10 + [any_] * 3,
+        in_specs=[VMEM] * 5 + [any_] * 3, out_specs=[VMEM] * 9 + [any_] * 3,
         scratch_shapes=[
             V((share, d), BF16), V((heads, HEAD_DIM, length), BF16), V((2 * heads * 128, d), BF16),
             V((length, 128), BF16), V((16, length), BF16),
@@ -474,6 +444,7 @@
     grad_two = norm_back(grad_out, gain_two, hat_two, r_two)
     gbranch = grad_two.astype(BF16)
     gbranch_ref[...] = gbranch
+    small_ref[10:16, :] = jnp.zeros_like(small_ref[10:16, :])
     small_ref[0:1, :] = jnp.sum(gbranch.astype(F32), 0, keepdims=True)
     small_ref[1:2, :] = jnp.sum(grad_out * hat_two, 0, keepdims=True)
     small_ref[2:3, :] = jnp.sum(grad_out, 0, keepdims=True)
@@ -503,66 +474,439 @@
     return mm(k_t[h], grad)
 
 
+def total(first, *others):
+    out = first.astype(F32)
+    for other in others:
+        out = out + other.astype(F32)
+    return out
+
+
 def backward_kernel(
-    x_ref, w_ref, gmixed_ref, mixed_ref, stats, q_in, k_aug, v_aug, k_t,
-    wgrad_ref, part_ref, bias_ref, unused_ref, q_aug, do_aug, dk_acc, dv_acc, grads
+    skip_ref, gmixed, mixed_own, normed, act, ginner, gbranch, gatt, small, gone, cot,
+    x_all, w_t, mixed_heads, q_aug, k_aug, v_aug, k_t,
+    frames_grad, dw_out, up_out, down_out, out_out, small_out,
+    do_in, do_aug, dk_acc, dv_acc, grads,
+    big, away, core_in, plane_in, mid, z_in, bigo, core_ino, plane_ino, mido, z_ino,
+    part, sib_in, line_in, dw_own, dw_in, dw_mid, dw_z, small_mine, small_plane, small_mid, small_z,
+    gm_s, gm_r, ci_s, ci_r, pl_s, pl_r, z_s, z_r, ag_s, ag_r, agf_s,
+    part_s, part_r, line_s, line_r, dwp_s, dwp_r, dwz_s, dwz_r, dwo_s, dwo_r, dwf_s, sp_s, sp_r, sz_s, sz_r,
 ):
+    at = Place()
     heads = q_aug.shape[0]
     width = heads * HEAD_DIM
-    length = x_ref.shape[0]
-    block = 384
-    n = length // block
+    share = gatt.shape[0]
+    length = x_all.shape[0] * share
+    step_rows = share // CHUNKS
+    z, c, q = at.z, at.b, at.q
+    primary = at.primary
+    secondary = jnp.logical_not(primary)
+    at.barrier()
+
+    for g in range(4):
+        block = gmixed.at[pl.ds(g * width, width)]
+        near = at.b == g // 2
+        to_d = jnp.where(near, at.d, at.sib)
+        to_z = jnp.where(near, g, (g + 2) % 4)
+        mine = jnp.logical_and(near, z == g)
+
+        @pl.when(mine)
+        def _():
+            pltpu.make_async_copy(block, do_in.at[z], gm_s.at[g]).start()
+
+        @pl.when(jnp.logical_not(mine))
+        def _():
+            at.send(block, do_in.at[z], gm_s.at[g], gm_r.at[z], to_d, to_z)
+
+    n_big = 8
+    half = big.shape[1]
+    quarter = half // 4
+    halfo = bigo.shape[3]
+    quartero = bigo.shape[2] // 4
+    finals = (down_out, up_out, out_out)
+
+    def big_rows(chip):
+        return pl.ds(pl.multiple_of(chip * quarter, 16), quarter)
+
+    def out_rows(chip):
+        return pl.ds(pl.multiple_of(chip * quartero, 16), quartero)
+
+    def weight_job(j):
+        if j < n_big:
+            kind, s = j // 4, j % 4
+            made = mm(act[s], gbranch[...], 0, 0) if kind == 0 else mm(normed[...], ginner[s], 0, 0)
+            made = made.astype(BF16)
+            if j >= 4:
+                at.sent(away.at[j % 4], ci_s.at[j - 4])
+
+            @pl.when(c == 0)
+            def _():
+                big[j] = made[:half]
+                away[j % 4] = made[half:]
+
+            @pl.when(c == 1)
+            def _():
+                big[j] = made[half:]
+                away[j % 4] = made[:half]
+
+            at.send(away.at[j % 4], core_in.at[j], ci_s.at[j], ci_r.at[j], at.sib, z)
+        else:
+            for s in range(4):
+                made = mm(mixed_own[s * width : (s + 1) * width, :], gatt[...])
+                for i in range(2):
+                    bigo[i, s] = made[:, i * halfo : (i + 1) * halfo].astype(BF16)
+            at.send(bigo.at[1 - c], core_ino, ci_s.at[j], ci_r.at[j], at.sib, z)
+
+    def core_job(j):
+        if j < n_big:
+            at.got(core_in.at[j], ci_r.at[j])
+            big[j] = total(big[j], core_in[j]).astype(BF16)
+            for k in (1, 2, 3):
+                at.send(big.at[j, big_rows((q + k) % 4)], plane_in.at[3 - k, j], pl_s.at[j, k - 1], pl_r.at[j, 3 - k], at.chip(k), z)
+        else:
+            at.got(core_ino, ci_r.at[j])
+            bigo[c] = total(bigo[c], core_ino[...]).astype(BF16)
+            for k in (1, 2, 3):
+                at.send(bigo.at[c, :, out_rows((q + k) % 4)], plane_ino.at[3 - k], pl_s.at[j, k - 1], pl_r.at[j, 3 - k], at.chip(k), z)
+
+    def plane_job(j):
+        if j < n_big:
+            kind, s = j // 4, j % 4
+            for k in range(3):
+                at.got(plane_in.at[k, j], pl_r.at[j, k])
+            mid[j] = total(big[j, big_rows(q)], plane_in[0, j], plane_in[1, j], plane_in[2, j]).astype(BF16)
+
+            @pl.when(z != s)
+            def _():
+                slot = 3 - (s - z + 4) % 4
+                at.send(mid.at[j], z_in.at[slot, kind], z_s.at[j], z_r.at[kind, slot], at.d, s)
+        else:
+            for k in range(3):
+                at.got(plane_ino.at[k], pl_r.at[j, k])
+            mido[...] = total(bigo[c, :, out_rows(q)], plane_ino[0], plane_ino[1], plane_ino[2]).astype(BF16)
+            for s in range(4):
+                @pl.when(z != s)
+                def _():
+                    slot = 3 - (s - z + 4) % 4
+                    at.send(mido.at[s], z_ino.at[slot], z_s.at[j + s], z_r.at[2, slot], at.d, s)
+
+    def final_piece(kind, chip, core):
+        if kind < 2:
+            return finals[kind].at[pl.ds(pl.multiple_of(core * half + chip * quarter, 16), quarter)]
+        return out_out.at[out_rows(chip), pl.ds(pl.multiple_of(core * halfo, 128), halfo)]
+
+    def final_job(kind):
+        for k in range(3):
+            at.got(z_in.at[k, kind] if kind < 2 else z_ino.at[k], z_r.at[kind, k])
+        piece = final_piece(kind, q, c)
+        if kind < 2:
+            piece[...] = total(mid[4 * kind + z], z_in[0, kind], z_in[1, kind], z_in[2, kind]).astype(BF16)
+        else:
+            piece[...] = total(mido[z], z_ino[0], z_ino[1], z_ino[2]).astype(BF16)
+        sem = ag_r.at[kind, 2 * q + c]
+        for k in (1, 2, 3):
+            at.send(piece, piece, ag_s.at[kind, k], sem, at.chip(k), z)
+        at.send(piece, piece, ag_s.at[kind, 0], sem, at.sib, z)
+
+    def share_job(kind):
+        for k in (1, 2, 3):
+            chip = (q + k) % 4
+            piece = final_piece(kind, chip, c)
+            sem = ag_r.at[kind, 2 * chip + c]
+            at.got(piece, sem)
+            at.send(piece, piece, agf_s.at[kind, k - 1], sem, at.sib, z)
+
+    def end_job(kind):
+        for k in range(4):
+            chip = (q + k) % 4
+            at.got(final_piece(kind, chip, 1 - c), ag_r.at[kind, 2 * chip + 1 - c])
+
+    for j in range(n_big + 1):
+        weight_job(j)
+        if j >= 2:
+            core_job(j - 2)
+    core_job(n_big - 1)
+    core_job(n_big)
+
+    for s in range(4):
+        mine = jnp.logical_and(primary, z == s)
+
+        @pl.when(mine)
+        def _():
+            pltpu.make_async_copy(gmixed.at[pl.ds(s * width, width)], do_in.at[s], gm_s.at[s]).wait()
+
+        @pl.when(jnp.logical_not(mine))
+        def _():
+            at.got(do_in.at[s], gm_r.at[s])
 
     def prepare(i, _):
-        cols = pl.ds(pl.multiple_of(i * block, block), block)
+        cols = pl.ds(pl.multiple_of(i * share, share), share)
         for h in range(heads):
-            at = slice(h * HEAD_DIM, (h + 1) * HEAD_DIM)
-            do = gmixed_ref[i, at, :]
+            hs = slice(h * HEAD_DIM, (h + 1) * HEAD_DIM)
+            do = do_in[i, hs, :]
             do_aug[h, 0:HEAD_DIM, cols] = do
-            inner = jnp.sum(do.astype(F32) * mixed_ref[i, at, :].astype(F32), 0, keepdims=True)
-            parts = split3(-inner)
-            do_aug[h, HEAD_DIM : HEAD_DIM + 16, cols] = pad_rows(parts, 16, block)
-            do_aug[h, HEAD_DIM + 16 :, cols] = jnp.zeros((48, block), BF16)
-            q_aug[h, 0:HEAD_DIM, cols] = q_in[h, 0:HEAD_DIM, cols]
-            hot = q_in[h, HEAD_DIM : HEAD_DIM + 16, cols].astype(F32)[0:4]
-            parts = split3(-stats[h, 0:1, cols])
-            q_aug[h, HEAD_DIM : HEAD_DIM + 16, cols] = pad_rows((hot,) + parts, 16, block)
-            q_aug[h, HEAD_DIM + 16 :, cols] = jnp.zeros((48, block), BF16)
+            inner = jnp.sum(do.astype(F32) * mixed_heads[i, hs, :].astype(F32), 0, keepdims=True)
+            do_aug[h, HEAD_DIM : HEAD_DIM + 16, cols] = pad_rows(split3(-inner), 16, share)
+            do_aug[h, HEAD_DIM + 16 :, cols] = jnp.zeros((48, share), BF16)
         return 0
 
-    lax.fori_loop(0, n, prepare, 0)
+    lax.fori_loop(0, 4, prepare, 0)
     dk_acc[...] = jnp.zeros_like(dk_acc)
     dv_acc[...] = jnp.zeros_like(dv_acc)
 
-    def step(i, _):
-        cols = pl.ds(pl.multiple_of(i * block, block), block)
+    def attention_step(i, _):
+        cols = pl.ds(pl.multiple_of(i * share, share), share)
         for h in range(heads):
             dq = attend_back(h, i, cols, q_aug, k_aug, v_aug, k_t, do_aug, None, dk_acc, dv_acc)
-            grads[h * HEAD_DIM : (h + 1) * HEAD_DIM, cols] = dq.astype(BF16) * jnp.bfloat16(HEAD_DIM**-0.5)
+            grads[h * HEAD_DIM : (h + 1) * HEAD_DIM, cols] = (dq.astype(BF16).astype(F32) * HEAD_DIM**-0.5).astype(BF16)
+        for n in range(4):
+            @pl.when(i == n)
+            def _():
+                for j in (2 * n, 2 * n + 1):
+                    plane_job(j)
         return 0
 
-    lax.fori_loop(0, n, step, 0)
+    lax.fori_loop(0, 4, attention_step, 0)
     for h in range(heads):
-        at = width + h * HEAD_DIM
-        grads[at : at + HEAD_DIM, :] = dk_acc[h].astype(BF16)
-        at = 2 * width + h * HEAD_DIM
-        grads[at : at + HEAD_DIM, :] = dv_acc[h].astype(BF16)
-    wgrad_ref[...] = mm(grads[...], x_ref[...]).astype(BF16)
-    bias_ref[...] = mm(jnp.ones((8, length), BF16), grads[...], 1, 1)
-
-    def out_step(i, _):
-        cols = pl.ds(pl.multiple_of(i * block, block), block)
-        part_ref[cols, :] = mm(grads[:, cols], w_ref[...], 0, 0).astype(BF16)
+        grads[width + h * HEAD_DIM : width + (h + 1) * HEAD_DIM, :] = dk_acc[h].astype(BF16)
+        grads[2 * width + h * HEAD_DIM : 2 * width + (h + 1) * HEAD_DIM, :] = dv_acc[h].astype(BF16)
+
+
+    small_mine[...] = small[...]
+    small_mine[pl.ds(10 + at.group, 1), 0 : 3 * width] = mm(jnp.ones((8, length), BF16), grads[...], 1, 1)[0:1]
+    at.send(small_mine, small_plane.at[0], sp_s.at[0], sp_r.at[0], at.sib, z)
+    for k in (1, 2, 3):
+        at.send(small_mine, small_plane.at[4 - k], sp_s.at[k], sp_r.at[4 - k], at.chip(k), z)
+        at.send(small_mine, small_plane.at[7 - k], sp_s.at[3 + k], sp_r.at[7 - k], at.other(k), z)
+
+    def rows(ch):
+        return pl.ds(ch * step_rows, step_rows)
+
+    def order(k):
+        return jnp.where(at.pp == 0, 3 - k, (4 - k) % 4)
+
+    def part_job(s):
+        part[s] = mm(grads[:, pl.ds(pl.multiple_of(s * share, share), share)], w_t[...], 0, 0).astype(BF16)
+
+        @pl.when(secondary)
+        def _():
+            for ch in range(CHUNKS):
+                at.send(part.at[s, rows(ch)], sib_in.at[s, rows(ch)], part_s.at[s, ch], part_r.at[s, ch], at.sib, z)
+
+    def line_job(place):
+        s = at.line(place)
+        for ch in range(CHUNKS):
+            here = (s, rows(ch))
+
+            @pl.when(jnp.logical_and(primary, place != at.p))
+            def _():
+                at.got(sib_in.at[here], part_r.at[s, ch])
+
+                @pl.when(jnp.logical_and(at.p == 1, place >= 2))
+                def _():
+                    at.got(line_in.at[here], line_r.at[s, ch])
+                    part[here] = total(part[here], sib_in[here], line_in[here]).astype(BF16)
+                    at.send(part.at[here], line_in.at[here], line_s.at[s, ch], line_r.at[s, ch], at.d, at.own_line(2))
+
+                @pl.when(jnp.logical_or(at.p == 0, place == 0))
+                def _():
+                    part[here] = total(part[here], sib_in[here]).astype(BF16)
+                    at.send(part.at[here], line_in.at[here], line_s.at[s, ch], line_r.at[s, ch], at.d, at.own_line(1 - at.p))
+
+    def part_step(k, _):
+        part_job(at.line(order(k)))
+
+        @pl.when(k > 0)
+        def _():
+            line_job(order(k - 1))
+
         return 0
 
-    lax.fori_loop(0, n, out_step, 0)
-
-
-def weights_kernel(normed_ref, act_ref, ginner_ref, gbranch_ref, gatt_ref, mixed_ref, gup_ref, gdown_ref, gout_ref):
-    for s in range(act_ref.shape[0]):
-        gdown_ref[s] = mm(act_ref[s], gbranch_ref[...], 0, 0).astype(BF16)
-        gup_ref[s] = mm(normed_ref[...], ginner_ref[s], 0, 0).astype(BF16)
-    gout_ref[...] = mm(mixed_ref[...], gatt_ref[...]).astype(BF16)
+    lax.fori_loop(0, 4, part_step, 0)
+    line_job(order(3))
+
+    made = mm(grads[:, 0:share], x_all[0])
+    for s in range(1, 4):
+        made = made + mm(grads[:, s * share : (s + 1) * share], x_all[s])
+    made = made.astype(BF16)
+    fourth = made.shape[0] // 4
+    for i in range(4):
+        dw_own[i] = made[i * fourth : (i + 1) * fourth]
+    for k in (1, 2, 3):
+        at.send(dw_own.at[(q + k) % 4], dw_in.at[3 - k], dwp_s.at[k - 1], dwp_r.at[3 - k], at.chip(k), z)
+
+    plane_job(n_big)
+    for k in range(7):
+        at.got(small_plane.at[k], sp_r.at[k])
+    small_mid[...] = total(small_mine[...], *(small_plane[k] for k in range(7)))
+    for k in (1, 2, 3):
+        at.send(small_mid, small_z.at[3 - k], sz_s.at[k - 1], sz_r.at[3 - k], at.d, (z + k) % 4)
+
+    final_job(0)
+
+    @pl.when(at.p == 2)
+    def _():
+        s = at.own_line(3)
+        for ch in range(CHUNKS):
+            here = (s, rows(ch))
+            at.got(line_in.at[here], line_r.at[s, ch])
+            at.send(line_in.at[here], line_in.at[here], line_s.at[s, ch], line_r.at[s, ch], at.d, s)
+
+    def dw_rows(i):
+        return pl.ds(pl.multiple_of(i * fourth, 16), fourth)
+
+    for k in range(3):
+        at.got(dw_in.at[k], dwp_r.at[k])
+    dw_mid[...] = total(dw_own[q], dw_in[0], dw_in[1], dw_in[2]).astype(BF16)
+
+    @pl.when(secondary)
+    def _():
+        at.send(dw_mid, dw_z, dwz_s.at[0], dwz_r.at[0], at.d, at.far)
+
+    final_job(1)
+    final_job(2)
+    share_job(0)
+
+    @pl.when(primary)
+    def _():
+        at.got(dw_z, dwz_r.at[0])
+        piece = dw_out.at[dw_rows(q)]
+        piece[...] = total(dw_mid[...], dw_z[...]).astype(BF16)
+        for k in (1, 2, 3):
+            at.send(piece, piece, dwo_s.at[k], dwo_r.at[q], at.chip(k), z)
+        at.send(piece, piece, dwo_s.at[0], dwo_r.at[q], at.sib, z)
+
+    for k in range(3):
+        at.got(small_z.at[k], sz_r.at[k])
+    small_out[...] = total(small_mid[...], small_z[0], small_z[1], small_z[2])
+
+    skipped = skip_ref[0] == 1
+    for ch in range(CHUNKS):
+        at.got(line_in.at[z, rows(ch)], line_r.at[z, ch])
+
+    @pl.when(primary)
+    def _():
+        for ch in range(CHUNKS):
+            at.got(sib_in.at[z, rows(ch)], part_r.at[z, ch])
+        grad = gone[...] + total(part[z], sib_in[z], line_in[z])
+        frames_grad[...] = jnp.where(skipped, cot[...].astype(F32), grad).astype(BF16)
+
+    @pl.when(secondary)
+    def _():
+        grad = gone[...] + line_in[z].astype(F32)
+        frames_grad[...] = jnp.where(skipped, cot[...].astype(F32), grad).astype(BF16)
+
+    share_job(1)
+    share_job(2)
+
+    @pl.when(primary)
+    def _():
+        for k in (1, 2, 3):
+            i = (q + k) % 4
+            piece = dw_out.at[dw_rows(i)]
+            at.got(piece, dwo_r.at[i])
+            at.send(piece, piece, dwf_s.at[k - 1], dwo_r.at[i], at.sib, z)
+
+    @pl.when(secondary)
+    def _():
+        for i in range(4):
+            at.got(dw_out.at[dw_rows(i)], dwo_r.at[i])
+
+    for kind in range(3):
+        end_job(kind)
+
+    for g in range(4):
+        mine = jnp.logical_and(primary, z == g)
+
+        @pl.when(jnp.logical_not(mine))
+        def _():
+            at.sent(gmixed.at[pl.ds(g * width, width)], gm_s.at[g])
+
+    for j in range(n_big):
+        if j >= 4:
+            at.sent(core_in.at[j], ci_s.at[j])
+        for k in range(3):
+            at.sent(plane_in.at[k, j], pl_s.at[j, k])
+
+        @pl.when(z != j % 4)
+        def _():
+            at.sent(mid.at[j], z_s.at[j])
+
+    at.sent(core_ino, ci_s.at[n_big])
+    for k in range(3):
+        at.sent(plane_ino.at[k], pl_s.at[n_big, k])
+    for s in range(4):
+        @pl.when(z != s)
+        def _():
+            at.sent(mido.at[s], z_s.at[n_big + s])
+
+    for kind in range(3):
+        for k in range(4):
+            at.sent(final_piece(kind, q, c), ag_s.at[kind, k])
+        for k in range(3):
+            at.sent(final_piece(kind, q, c), agf_s.at[kind, k])
+    for k in range(7):
+        at.sent(small_mine, sp_s.at[k])
+    for k in range(3):
+        at.sent(small_mid, sz_s.at[k])
+        at.sent(dw_mid, dwp_s.at[k])
+
+    @pl.when(secondary)
+    def _():
+        at.sent(dw_mid, dwz_s.at[0])
+        for s in range(4):
+            for ch in range(CHUNKS):
+                at.sent(part.at[s, rows(ch)], part_s.at[s, ch])
+
+    @pl.when(primary)
+    def _():
+        for k in range(4):
+            at.sent(dw_mid, dwo_s.at[k])
+        for k in range(3):
+            at.sent(dw_mid, dwf_s.at[k])
+        for k in (1, 2, 3):
+            for ch in range(CHUNKS):
+                s = at.line((at.p + k) % 4)
+                at.sent(part.at[s, rows(ch)], line_s.at[s, ch])
+
+    @pl.when(at.p == 2)
+    def _():
+        for ch in range(CHUNKS):
+            at.sent(line_in.at[at.own_line(3), rows(ch)], line_s.at[at.own_line(3), ch])
+
+
+def run_backward(skip, gmixed, mixed_own, normed, act, ginner, gbranch, gatt, small, gone, cot,
+                 x_all, w_t, mixed_heads, q_aug, k_aug, v_aug, k_t):
+    share, d = gatt.shape
+    f = act.shape[2]
+    heads, _, length = q_aug.shape
+    width = heads * HEAD_DIM
+    dma, V = pltpu.SemaphoreType.DMA, pltpu.VMEM
+    hd, hf, ho = d // 2, f // 2, d // 2
+    return pl.pallas_call(
+        backward_kernel,
+        out_shape=(
+            S((share, d)), S((3 * width, d)), S((d, f)), S((f, d)), S((width, d)), S((16, d), F32),
+        ),
+        in_specs=[SMEM] + [VMEM] * 17, out_specs=[VMEM] * 6,
+        scratch_shapes=[
+            V((4, width, share), BF16), V((heads, 128, length), BF16),
+            V((heads, HEAD_DIM, length), F32), V((heads, HEAD_DIM, length), F32), V((3 * width, length), BF16),
+            V((8, hd, d), BF16), V((4, hd, d), BF16), V((8, hd, d), BF16), V((3, 8, hd // 4, d), BF16), V((8, hd // 4, d), BF16),
+            V((3, 2, hd // 4, d), BF16),
+            V((2, 4, width, ho), BF16), V((4, width, ho), BF16), V((3, 4, width // 4, ho), BF16), V((4, width // 4, ho), BF16),
+            V((3, width // 4, ho), BF16),
+            V((4, share, d), BF16), V((4, share, d), BF16), V((4, share, d), BF16),
+            V((4, 3 * width // 4, d), BF16), V((3, 3 * width // 4, d), BF16), V((3 * width // 4, d), BF16), V((3 * width // 4, d), BF16),
+            V((16, d), F32), V((7, 16, d), F32), V((16, d), F32), V((3, 16, d), F32),
+            dma((4,)), dma((4,)), dma((9,)), dma((9,)), dma((9, 3)), dma((9, 3)), dma((12,)), dma((3, 3)),
+            dma((3, 4)), dma((3, 8)), dma((3, 3)),
+            dma((4, CHUNKS)), dma((4, CHUNKS)), dma((4, CHUNKS)), dma((4, CHUNKS)), dma((3,)), dma((3,)), dma((1,)), dma((1,)),
+            dma((4,)), dma((4,)), dma((3,)), dma((7,)), dma((7,)), dma((3,)), dma((3,)),
+        ],
+        compiler_params=pltpu.CompilerParams(vmem_limit_bytes=LIMIT, collective_id=1, has_side_effects=True),
+        name="attention_backward",
+    )(skip, gmixed, mixed_own, normed, act, ginner, gbranch, gatt, small, gone, cot,
+      x_all, w_t, mixed_heads, q_aug, k_aug, v_aug, k_t)
 
 
 def S(shape, dtype=BF16):
@@ -582,7 +926,6 @@
     scale = HEAD_DIM**-0.5
     own = frames[0]
     w_t = jnp.concatenate([w_query.T, w_key.T, w_value.T], 0)
-    bias_col = jnp.concatenate([b_query, jnp.zeros_like(b_query), b_value])[:, None]
     v_row = jnp.concatenate(
         [b_value.reshape(heads, HEAD_DIM), jnp.ones((heads, 3)), jnp.zeros((heads, 61))], 1
     ).reshape(1, heads * 128)
@@ -594,22 +937,11 @@
     ).astype(BF16)
     hot = jnp.concatenate([(seg[None] == ids[:, None]).astype(BF16), jnp.zeros((12, length), BF16)], 0)
 
-    everything = lax.all_gather(own, "mp", axis=0, tiled=True)
-    mixed, q_aug, k_aug, v_aug, k_t, v_t, stats = pl.pallas_call(
-        local_forward_kernel,
-        out_shape=(
-            S((mp, width, share)), S((heads, 128, length)), S((heads, length, 128)), S((heads, length, 128)),
-            S((heads, HEAD_DIM, length)), S((heads, HEAD_DIM, length)), S((heads, 8, length), F32),
-        ),
-        in_specs=[VMEM] * 6, out_specs=[VMEM] * 7,
-        scratch_shapes=[pltpu.VMEM((2 * heads * 128, d), BF16)],
-        compiler_params=params, name="local_forward",
-    )(everything, w_t, bias_col, v_row, k_mask, hot)
     zero = jnp.zeros((d,), F32)
     bias_row = jnp.concatenate([b_query, jnp.zeros_like(b_query), b_value, jnp.zeros((d - 3 * width,), F32)])
-    v_row2 = jnp.concatenate([v_row[0], jnp.zeros((d - heads * 128,), F32)])
-    small = jnp.stack([b_up, bias_row, v_row2] + [zero] * 5)
-    _, _, _, mixed_own, _, _, _, _, _, small_all, wup, wdown, wout = run_forward(
+    v_row = jnp.concatenate([v_row[0], jnp.zeros((d - heads * 128,), F32)])
+    small = jnp.stack([b_up, bias_row, v_row] + [zero] * 5)
+    x_all, w_t, mixed, mixed_own, q_aug, k_aug, v_aug, k_t, small_all, wup, wdown, wout = run_forward(
         own, w_t, small, k_mask, hot, w_up, w_down, w_out
     )
     wout = wout.reshape(mp * width, d)
@@ -626,36 +958,22 @@
         scratch_shapes=[pltpu.VMEM((mp, share, f), F32)],
         compiler_params=params, name="feed_forward",
     )(skip_flag, mixed_own, own, cotangent[0], vec, bup, wout, wup, wdown)
-    gup, gdown, gout = pl.pallas_call(
-        weights_kernel,
-        out_shape=(S((mp, d, f)), S((mp, f, d)), S((mp * width, d))),
-        in_specs=[VMEM] * 6, out_specs=[VMEM] * 3, compiler_params=params, name="weight_grads",
-    )(normed, act, ginner, gbranch, gatt, mixed_own)
-    gmixed_heads = lax.all_to_all(gmixed.reshape(mp, width, share), "mp", 0, 0)
-    wgrad, part, bias = pl.pallas_call(
-        backward_kernel,
-        out_shape=(S((3 * width, d)), S((length, d)), S((8, 3 * width), F32), S((16, 128), F32)),
-        in_specs=[VMEM] * 9, out_specs=[VMEM] * 4,
-        scratch_shapes=[
-            pltpu.VMEM((heads, 128, length), BF16), pltpu.VMEM((heads, 128, length), BF16),
-            pltpu.VMEM((heads, HEAD_DIM, length), F32), pltpu.VMEM((heads, HEAD_DIM, length), F32),
-            pltpu.VMEM((3 * width, length), BF16),
-        ],
-        compiler_params=params, name="attention_backward",
-    )(everything, w_t, gmixed_heads, mixed, stats, q_aug, k_aug, v_aug, k_t)[:3]
-    dx = lax.psum_scatter(part, "mp", scatter_dimension=0, tiled=True).astype(F32)
-    skipped = (skip_flag == 1)[0]
-    frames_grad = jnp.where(skipped, cotangent[0].astype(F32), gone + dx).astype(BF16)
-    wgrad = lax.psum(wgrad, "dp").astype(F32)
-    bias = lax.psum(bias[0], "dp")
-    gup = lax.psum(lax.psum_scatter(gup, "mp"), "dp").astype(F32)
-    gdown = lax.psum(lax.psum_scatter(gdown, "mp"), "dp").astype(F32)
-    gout = lax.psum(lax.psum_scatter(gout.reshape(mp, width, d), "mp"), "dp").astype(F32)
-    small = lax.psum(small, ("dp", "mp"))
+    frames_grad, wgrad, gup, gdown, gout, small = run_backward(
+        skip_flag, gmixed, mixed_own, normed, act, ginner, gbranch, gatt, small, gone, cotangent[0],
+        x_all, w_t, mixed, q_aug, k_aug, v_aug, k_t,
+    )
+    dp = lax.axis_size("dp")
+    if dp > 8:
+        groups = [list(range(i, dp, 8)) for i in range(8)]
+        wgrad, gup, gdown, gout, small = (
+            lax.psum(v.astype(F32), "dp", axis_index_groups=groups) for v in (wgrad, gup, gdown, gout, small)
+        )
+    wgrad, gup, gdown, gout = (v.astype(F32) for v in (wgrad, gup, gdown, gout))
     z = lax.axis_index("mp")
+    bias = small[10 + z]
     return (
         layer[None], frames_grad[None],
-        wgrad[:width].T, bias[:width], wgrad[width : 2 * width].T, wgrad[2 * width :].T, bias[2 * width :],
+        wgrad[:width].T, bias[:width], wgrad[width : 2 * width].T, wgrad[2 * width :].T, bias[2 * width : 3 * width],
         gout, small[3], small[4], small[5],
         gup, small[6 + z], gdown, small[0], small[1], small[2],
     )

time: 552 us -> 285 us (0.52)
  the two profiles are of different devices: /device:TPU:1 before, /device:TPU:9 now
where the time goes in v2:
time: 285 us; the launch traced here: 280 us
  Pallas kernels  257 us (90%)
  other arithmetic  11.6 us (4%)
  local copies, waits for them, and re-layouts  9.16 us (3%)
    pallas_call x1, Pallas kernels, run_backward(): pl.pallas_call(backward_kernel, out_shape=(S((share, d)), S((3 * width, d...  135 us
    pallas_call x1, Pallas kernels, run_forward(): pl.pallas_call(forward_kernel, out_shape=(S((4, share, d)), S(w_t.shape),...  105 us
    pallas_call x1, Pallas kernels, shards(): pl.pallas_call(middle_kernel, out_shape=(S((share, d)), S((share, d), F32...  17.5 us

profile of v2, /device:TPU:9, one launch (start us, length us, event | category | flops | bytes accessed | tf_op | source)
XLA Modules:
  0.0 280.0 jit_solution(7854820985063492999)
XLA Ops:
  0.7 0.0 copy-start.4
  0.7 0.7 reduce
  1.4 0.7 compare_reduce_fusion
  2.1 1.1 select_convert_fusion
  3.3 0.1 pad.5.clone
  3.4 0.1 pad.6.clone
  3.4 1.0 maximum_maximum_fusion.kmask_own
  4.4 0.6 pad_convert_fusion.hot_own
  5.0 2.1 pad_maximum_fusion.w_own
  7.1 0.1 reshape.52
  7.2 0.1 pad.8.clone
  7.3 0.1 pad.9.clone
  7.4 0.1 pad_maximum_fusion.1
  7.5 0.6 stack.42.small_own
  8.2 0.0 copy-start.10
  8.2 0.0 copy-start.11
  8.2 105.1 %attention_forward.1 = (bf16[4,384,768]{2,1,0:T(8,128)(2,1)}, bf16[576,768]{1,0:T(8,128)(2,1)}, bf16[4,192,384]{2,1,0:T(8,128)(2,1)}, bf16[768,384]{1,0:T(8,128)...) custom-call(bf16[384,768]{1,0:T(8,128)(2,1)} %bitcast.20, ...), custom_call_target="tpu_custom_call" | custom-call | tf_op jit(solution)/shard_map/attention_forward/pallas_call | solution.py:387
  113.4 0.9 copy.37
  114.3 0.6 slice_bitcast_fusion.3.bup_ref
  115.7 0.6 stack.49.vec_ref
  116.3 17.5 %feed_forward.1 = (bf16[384,768]{1,0:T(8,128)(2,1)}, f32[384,768]{1,0:T(8,128)}, bf16[768,384]{1,0:T(8,128)(2,1)}, bf16[384,768]{1,0:T(8,128)(2,1)}, bf16[4,384,...) custom-call(s32[1]{0:T(128)S(6)} %copy.39.skip_ref, ...), custom_call_target="tpu_custom_call" | custom-call | tf_op jit(solution)/shard_map/feed_forward/pallas_call | solution.py:951
  133.8 134.6 %attention_backward.1 = (bf16[384,768]{1,0:T(8,128)(2,1)}, bf16[576,768]{1,0:T(8,128)(2,1)}, bf16[768,768]{1,0:T(8,128)(2,1)}, bf16[768,768]{1,0:T(8,128)(2,1)},...) custom-call(s32[1]{0:T(128)S(6)} %copy.39.skip_ref, bf16[768,384]{1,0:T(8,128)(2,1)} %get-tuple-element.50.gmixed, ...), custom_call_target="tpu_custom_call" | custom-call | tf_op jit(solution)/shard_map/attention_backward/pallas_call | solution.py:885
  268.4 1.3 convert_element_type.14
  269.7 1.2 slice_bitcast_fusion
  270.9 0.7 copy-done.1
  271.6 1.6 convert_element_type.16
  273.2 0.1 copy-done
  273.3 1.6 convert_element_type.17
  274.8 0.9 convert_element_type.15
  275.7 1.7 slice_reduce_fusion
  277.4 1.4 fusion.1
  278.7 0.8 copy.40
  (42 shorter events, 0.1 us)
Async XLA Ops:
  0.7 6.5 %copy-start.4 = (f32[192]{0:T(256)S(1)}, f32[192]{0:T(256)}, u32[]{:S(2)}) copy-start(f32[192]{0:T(256)} %param.29) | copy-start | bytes 2308
  0.7 6.8 %copy-start.12 = (f32[192]{0:T(256)S(1)}, f32[192]{0:T(256)}, u32[]{:S(2)}) copy-start(f32[192]{0:T(256)} %param.26) | copy-start | bytes 2308
  0.7 6.8 %copy-start.5 = (f32[768]{0:T(1024)S(1)}, f32[768]{0:T(1024)}, u32[]{:S(2)}) copy-start(f32[768]{0:T(1024)} %param.35) | copy-start | bytes 9220
  8.2 107.4 %copy-start.6 = (f32[768]{0:T(1024)S(1)}, f32[768]{0:T(1024)}, u32[]{:S(2)}) copy-start(f32[768]{0:T(1024)} %param.31) | copy-start | bytes 9220
  8.2 107.4 %copy-start.7 = (f32[768]{0:T(1024)S(1)}, f32[768]{0:T(1024)}, u32[]{:S(2)}) copy-start(f32[768]{0:T(1024)} %param.32) | copy-start | bytes 9220
  8.2 107.4 %copy-start.8 = (f32[768]{0:T(1024)S(1)}, f32[768]{0:T(1024)}, u32[]{:S(2)}) copy-start(f32[768]{0:T(1024)} %param.33) | copy-start | bytes 9220
  8.2 107.4 %copy-start.9 = (f32[768]{0:T(1024)S(1)}, f32[768]{0:T(1024)}, u32[]{:S(2)}) copy-start(f32[768]{0:T(1024)} %param.37) | copy-start | bytes 9220
  8.2 107.4 %copy-start.10 = (f32[768]{0:T(1024)S(1)}, f32[768]{0:T(1024)}, u32[]{:S(2)}) copy-start(f32[768]{0:T(1024)} %param.38) | copy-start | bytes 9220
  8.2 107.5 %copy-start.11 = (f32[768]{0:T(1024)S(1)}, f32[768]{0:T(1024)}, u32[]{:S(2)}) copy-start(f32[768]{0:T(1024)} %param.39) | copy-start | bytes 9220
  269.7 1.9 copy-start.1
  271.6 1.7 copy-start
  273.3 1.6 copy-start.3
  273.3 5.5 %copy-start.2 = (bf16[384,768]{1,0:T(8,128)(2,1)S(1)}, bf16[384,768]{1,0:T(8,128)(2,1)}, u32[]{:S(2)}) copy-start(bf16[384,768]{1,0:T(8,128)(2,1)} %get-tuple-element.65) | copy-start | bytes 1769476

commit v3 on v2

--- a/solution.py
+++ b/solution.py
@@ -16,6 +16,10 @@
 
 def mm(a, b, ca=1, cb=0):
     return lax.dot_general(a, b, (((ca,), (cb,)), ((), ())), preferred_element_type=F32)
+
+
+def row_of(ref):
+    return ref[...].reshape(1, ref.shape[0])
 
 
 def split3(v):
@@ -74,6 +78,13 @@
         self.sib = d + 1 - 2 * self.b
         self.q = (d // 2) % 4
         self.base = d - d % 8
+        q = self.q
+        turn, over = q + 1 - 2 * (q % 2), (q + 2) % 4
+        self.near_chip = turn + self.b * (over - turn)
+        self.across_chip = over + self.b * (turn - over)
+        self.opposite_chip = 3 - q
+        self.near = self.base + 2 * self.near_chip + self.b
+        self.across = self.base + 2 * self.across_chip + self.b
         self.primary = self.p < 2
         self.rb = z // 2
         self.row = d - self.b + self.rb
@@ -120,11 +131,11 @@
 
 
 def forward_kernel(
-    frames, w_own, small_own, kmask_own, hot_own, w_up, w_down, w_out,
+    frames, w_query, w_key, w_value, b_query, b_value, b_up, segments, padding, w_up, w_down, w_out,
     x_all, w_t, mixed_heads, mixed_own, q_aug, k_aug, v_aug, k_t, small_all, up_all, down_all, out_all,
-    relay, v_t, w_pad, kmask, hot,
+    relay, v_t, w_pad, kmask, hot, w_own, small_own, kmask_own, hot_own,
     small_s, small_r, mask_s, mask_r, wq_s, wq_r, x_s, x_r, relay_r, on_s, fwd_s, mix_s, mix_r, local,
-    p1_s, p2_s, p3_s, w_r,
+    line_s, near_s, far_s, core_s, w_r,
 ):
     at = Place()
     heads = q_aug.shape[0]
@@ -132,6 +143,16 @@
     share = frames.shape[0]
     step_rows = share // CHUNKS
     quarter = w_own.shape[0] // 4
+    for i, w in enumerate((w_query, w_key, w_value)):
+        w_own[i * width : (i + 1) * width] = w[...]
+    small_own[...] = jnp.zeros_like(small_own)
+    small_own[0:1, :] = row_of(b_up)
+    small_own[1:2, 0:width] = row_of(b_query)
+    values = row_of(b_value)
+    small_own[1:2, 2 * width : 3 * width] = values
+    for h in range(heads):
+        small_own[2:3, h * 128 : h * 128 + HEAD_DIM] = values[:, h * HEAD_DIM : (h + 1) * HEAD_DIM]
+        small_own[2:3, h * 128 + HEAD_DIM : h * 128 + HEAD_DIM + 3] = jnp.ones((1, 3), F32)
     at.barrier()
     primary = at.primary
     secondary = jnp.logical_not(primary)
@@ -150,6 +171,8 @@
 
     mats = ((w_up, up_all), (w_down, down_all), (w_out, out_all))
 
+    for k in (1, 2, 3):
+        at.send(small_own, small_all.at[z], small_s.at[k - 1], small_r.at[z], at.d, (z + k) % 4)
     wq_rows = pl.ds(pl.multiple_of(at.q * quarter, 16), quarter)
     first = jnp.where(at.p == 0, 1, at.p - 1)
 
@@ -168,35 +191,103 @@
 
     @pl.when(primary)
     def _():
+        for i in range(4):
+            cols = slice(i * share, (i + 1) * share)
+            seg, pad = segments[:, cols], padding[:, cols]
+            row = lax.broadcasted_iota(jnp.int32, (128, share), 0)
+            told = jnp.logical_and(row - HEAD_DIM == seg, pad == 1)
+            mask = jnp.where(row < HEAD_DIM, 0.0, jnp.where(row < HEAD_DIM + 4, jnp.where(told, 0.0, -1e30), jnp.where(row < HEAD_DIM + 7, 1.0, 0.0)))
+            kmask_own[cols, :] = mask.T.astype(BF16)
+            hot_own[:, cols] = jnp.where(row[:16] == seg, 1.0, 0.0).astype(BF16)
         at.send(kmask_own, kmask, mask_s.at[0], mask_r.at[0], at.sib, z)
         at.send(hot_own, hot, mask_s.at[1], mask_r.at[1], at.sib, z)
+        for ch in range(CHUNKS):
+            at.send(frames.at[rows(ch)], x_all.at[z, rows(ch)], fwd_s.at[z, ch], x_r.at[z, ch], at.sib, z)
+        pltpu.make_async_copy(w_own, w_t, local.at[2]).start()
+        pltpu.make_async_copy(frames, x_all.at[z], local.at[3]).start()
         pltpu.make_async_copy(kmask_own, kmask, local.at[0]).start()
         pltpu.make_async_copy(hot_own, hot, local.at[1]).start()
-        pltpu.make_async_copy(w_own, w_t, local.at[2]).start()
-        pltpu.make_async_copy(frames, x_all.at[z], local.at[3]).start()
-        for ch in range(CHUNKS):
-            at.send(frames.at[rows(ch)], x_all.at[z, rows(ch)], fwd_s.at[z, ch], x_r.at[z, ch], at.sib, z)
-
-    for k in (1, 2, 3):
-        to = (z + k) % 4
-        at.send(small_own, small_all.at[z], small_s.at[k - 1], small_r.at[z], at.d, to)
+
     pltpu.make_async_copy(small_own, small_all.at[z], local.at[4]).start()
-    for m, (src, dst) in enumerate(mats):
-        pltpu.make_async_copy(src, dst.at[z], local.at[5 + m]).start()
-
-    @pl.when(at.p == 2)
-    def _():
-        for ch in range(CHUNKS):
+
+    def weights_first(m):
+        src, dst = mats[m]
+        r, c = piece(m, at.q, at.b)
+        sem = w_r.at[m, z, 2 * at.q + at.b]
+
+        @pl.when(z < 3)
+        def _():
+            at.send(src.at[r, c], dst.at[z, r, c], line_s.at[m, z, 0], sem, at.d, z + 1)
+
+        @pl.when(z > 0)
+        def _():
+            at.send(src.at[r, c], dst.at[z, r, c], line_s.at[m, z, 1], sem, at.d, z - 1)
+
+    def shard_at(n):
+        low = z // 2
+        near = z + low * (3 - 2 * z)
+        s = jnp.where(near == 0, n + 1, 2 if n == 0 else (0 if n == 1 else 3))
+        return s + low * (3 - 2 * s)
+
+    def weights_line(m, n):
+        dst = mats[m][1]
+        s = shard_at(n)
+        r, c = piece(m, at.q, at.b)
+        block = dst.at[s, r, c]
+        sem = w_r.at[m, s, 2 * at.q + at.b]
+        at.got(block, sem)
+
+        @pl.when(jnp.logical_and(s < z, z < 3))
+        def _():
+            at.send(block, block, line_s.at[m, s, 0], sem, at.d, z + 1)
+
+        @pl.when(jnp.logical_and(s > z, z > 0))
+        def _():
+            at.send(block, block, line_s.at[m, s, 1], sem, at.d, z - 1)
+
+        at.send(block, block, near_s.at[m, s], sem, at.near, z)
+        at.send(block, block, far_s.at[m, s, 0], sem, at.across, z)
+        at.send(block, block, core_s.at[m, s, 0], sem, at.sib, z)
+
+    def weights_near(m, n):
+        dst = mats[m][1]
+        s = shard_at(n)
+        r, c = piece(m, at.near_chip, at.b)
+        block = dst.at[s, r, c]
+        sem = w_r.at[m, s, 2 * at.near_chip + at.b]
+        at.got(block, sem)
+        at.send(block, block, far_s.at[m, s, 1], sem, at.across, z)
+        at.send(block, block, core_s.at[m, s, 1], sem, at.sib, z)
+
+    def weights_across(m, n):
+        dst = mats[m][1]
+        s = shard_at(n)
+        for i, chip in ((2, at.across_chip), (3, at.opposite_chip)):
+            r, c = piece(m, chip, at.b)
+            block = dst.at[s, r, c]
+            sem = w_r.at[m, s, 2 * chip + at.b]
+            at.got(block, sem)
+            at.send(block, block, core_s.at[m, s, i], sem, at.sib, z)
+
+    for m in range(3):
+        weights_first(m)
+
+    def relay_job(ch):
+        @pl.when(at.p == 2)
+        def _():
             at.got(relay.at[rows(ch)], relay_r.at[ch])
             at.send(relay.at[rows(ch)], x_all.at[at.own_line(3), rows(ch)], x_s.at[ch], x_r.at[at.own_line(3), ch], at.d, at.own_line(1))
+
+    relay_job(0)
 
     @pl.when(secondary)
     def _():
         at.got(w_t.at[wq_rows], wq_r.at[at.q])
         for k in (1, 2, 3):
             at.send(w_t.at[wq_rows], w_t.at[wq_rows], wq_s.at[k], wq_r.at[at.q], at.chip(k), z)
-        at.got(kmask, mask_r.at[0])
-        at.got(hot, mask_r.at[1])
+
+    for ch in range(1, CHUNKS):
+        relay_job(ch)
 
     @pl.when(primary)
     def _():
@@ -211,6 +302,8 @@
 
     @pl.when(secondary)
     def _():
+        at.got(kmask, mask_r.at[0])
+        at.got(hot, mask_r.at[1])
         for k in (1, 2, 3):
             other = (at.q + k) % 4
             at.got(w_t.at[pl.ds(pl.multiple_of(other * quarter, 16), quarter)], wq_r.at[other])
@@ -222,12 +315,20 @@
                 (i + 1) * width + h * HEAD_DIM : (i + 1) * width + (h + 1) * HEAD_DIM
             ]
 
-    def shard_of(k):
+    A, B, C = weights_line, weights_near, weights_across
+    early = {1: ((A, 0, 0), (A, 1, 0), (A, 2, 0),), 2: ((A, 0, 1), (A, 1, 1), (A, 2, 1), (B, 0, 0), (B, 1, 0), (B, 2, 0),), 3: ((A, 0, 2), (C, 0, 0), (C, 1, 0), (C, 2, 0),)}
+    jobs = {0: ((A, 1, 2), (B, 0, 1),), 1: ((A, 2, 2), (B, 1, 1),), 2: ((B, 2, 1), (C, 0, 1),), 3: ((C, 1, 1), (B, 0, 2),), 4: ((C, 2, 1), (B, 1, 2),), 5: ((B, 2, 2),), 6: ((C, 0, 2),), 7: ((C, 1, 2),), 8: ((C, 2, 2),)}
+
+    def run_jobs(table, now):
+        for when, todo in table.items():
+            @pl.when(now == when)
+            def _():
+                for job, m, n in todo:
+                    job(m, n)
+
+    def gather_step(k, _):
         place = jnp.where(at.pp == 0, k, jnp.where(k == 0, 1, jnp.where(k == 1, 2, jnp.where(k == 2, 0, 3))))
-        return place, at.line(place)
-
-    def gather_step(k, _):
-        place, s = shard_of(k)
+        s = at.line(place)
         for ch in range(CHUNKS):
             block = x_all.at[s, rows(ch)]
 
@@ -243,6 +344,7 @@
 
                 at.send(block, block, fwd_s.at[s, ch], x_r.at[s, ch], at.sib, z)
 
+        run_jobs(early, k)
         cols = pl.ds(pl.multiple_of(s * share, share), share)
         biases = jnp.transpose(small_all[at.group])
         project(
@@ -253,59 +355,28 @@
 
     lax.fori_loop(0, 4, gather_step, 0)
 
-    for m, (src, dst) in enumerate(mats):
-        r, c = piece(m, at.q, at.b)
-        for k in (1, 2, 3):
-            at.send(src.at[r, c], dst.at[z, r, c], p1_s.at[m, k - 1], w_r.at[m, z, 2 * at.q + at.b], at.d, (z + k) % 4)
-
-    def spread(m):
-        dst = mats[m][1]
-        r, c = piece(m, at.q, at.b)
-        for k in (1, 2, 3):
-            s = (z + k) % 4
-            sem = w_r.at[m, s, 2 * at.q + at.b]
-            at.got(dst.at[s, r, c], sem)
-            for j in (1, 2, 3):
-                at.send(dst.at[s, r, c], dst.at[s, r, c], p2_s.at[m, k - 1, j], sem, at.chip(j), z)
-            at.send(dst.at[s, r, c], dst.at[s, r, c], p2_s.at[m, k - 1, 0], sem, at.sib, z)
-
-    def attend_step(i, _):
+    def attend_step(t, _):
+        turn, h = t // heads, t % heads
+        i = (z + jnp.where(turn == 0, 2, jnp.where(turn == 1, 1, jnp.where(turn == 2, 3, 0)))) % 4
         cols = pl.ds(pl.multiple_of(i * share, share), share)
-        for h in range(heads):
-            mixed_heads[i, h * HEAD_DIM : (h + 1) * HEAD_DIM, :] = attend(h, cols, q_aug, k_aug, v_t)
+        mixed_heads[i, pl.ds(pl.multiple_of(h * HEAD_DIM, HEAD_DIM), HEAD_DIM), :] = attend(h, cols, q_aug, k_aug, v_t)
         mine = jnp.logical_and(primary, i == z)
         block = mixed_own.at[pl.ds(pl.multiple_of(at.group * width, 64), width)]
 
-        @pl.when(mine)
+        @pl.when(jnp.logical_and(h == heads - 1, mine))
         def _():
             pltpu.make_async_copy(mixed_heads.at[i], block, mix_s.at[i]).start()
 
-        @pl.when(jnp.logical_not(mine))
+        @pl.when(jnp.logical_and(h == heads - 1, jnp.logical_not(mine)))
         def _():
             at.send(mixed_heads.at[i], block, mix_s.at[i], mix_r.at[at.group], at.row, i)
 
-        @pl.when(i == 1)
-        def _():
-            spread(0)
-
-        @pl.when(i == 3)
-        def _():
-            spread(1)
-            spread(2)
-
+        run_jobs(jobs, t)
         return 0
 
-    lax.fori_loop(0, 4, attend_step, 0)
-
-    for m, (_, dst) in enumerate(mats):
-        for j in (1, 2, 3):
-            chip = (at.q + j) % 4
-            r, c = piece(m, chip, at.b)
-            for k in (1, 2, 3):
-                s = (z + k) % 4
-                sem = w_r.at[m, s, 2 * chip + at.b]
-                at.got(dst.at[s, r, c], sem)
-                at.send(dst.at[s, r, c], dst.at[s, r, c], p3_s.at[m, j - 1, k - 1], sem, at.sib, z)
+    lax.fori_loop(0, 4 * heads, attend_step, 0)
+    for job, m, n in jobs.get(99, ()):
+        job(m, n)
 
     for g in range(4):
         mine = jnp.logical_and(primary, z == g)
@@ -315,8 +386,7 @@
         def _():
             at.got(block, mix_r.at[g])
 
-    for m, (src, dst) in enumerate(mats):
-        pltpu.make_async_copy(src, dst.at[z], local.at[5 + m]).wait()
+    for m, (_, dst) in enumerate(mats):
         for j in range(4):
             chip = (at.q + j) % 4
             r, c = piece(m, chip, 1 - at.b)
@@ -368,18 +438,29 @@
 
     for m, (src, dst) in enumerate(mats):
         r, c = piece(m, at.q, at.b)
-        for k in range(3):
-            at.sent(src.at[r, c], p1_s.at[m, k])
-            for j in range(4):
-                at.sent(src.at[r, c], p2_s.at[m, k, j])
-            for j in range(3):
-                at.sent(src.at[r, c], p3_s.at[m, j, k])
-
-
-def run_forward(frames, w_t, small, kmask, hot, w_up, w_down, w_out):
+        block = src.at[r, c]
+        for s in range(4):
+            @pl.when(jnp.logical_and(s <= z, z < 3))
+            def _():
+                at.sent(block, line_s.at[m, s, 0])
+
+            @pl.when(jnp.logical_and(s >= z, z > 0))
+            def _():
+                at.sent(block, line_s.at[m, s, 1])
+
+            @pl.when(s != z)
+            def _():
+                at.sent(block, near_s.at[m, s])
+                for i in range(2):
+                    at.sent(block, far_s.at[m, s, i])
+                for i in range(4):
+                    at.sent(block, core_s.at[m, s, i])
+
+
+def run_forward(frames, w_query, w_key, w_value, b_query, b_value, b_up, segments, padding, w_up, w_down, w_out):
     share, d = frames.shape
-    length = hot.shape[1]
-    width = w_t.shape[0] // 3
+    length = segments.shape[1]
+    width = w_query.shape[0]
     heads = width // HEAD_DIM
     f = w_up.shape[1]
     any_ = pl.BlockSpec(memory_space=pl.ANY)
@@ -387,21 +468,22 @@
     return pl.pallas_call(
         forward_kernel,
         out_shape=(
-            S((4, share, d)), S(w_t.shape), S((4, width, share)), S((4 * width, share)),
+            S((4, share, d)), S((3 * width, d)), S((4, width, share)), S((4 * width, share)),
             S((heads, 128, length)), S((heads, length, 128)), S((heads, length, 128)), S((heads, HEAD_DIM, length)),
             S((4, 8, d), F32), S((4, d, f)), S((4, f, d)), S((4, width, d)),
         ),
-        in_specs=[VMEM] * 5 + [any_] * 3, out_specs=[VMEM] * 9 + [any_] * 3,
+        in_specs=[VMEM] * 9 + [any_] * 3, out_specs=[VMEM] * 9 + [any_] * 3,
         scratch_shapes=[
             V((share, d), BF16), V((heads, HEAD_DIM, length), BF16), V((2 * heads * 128, d), BF16),
             V((length, 128), BF16), V((16, length), BF16),
+            V((3 * width, d), BF16), V((8, d), F32), V((length, 128), BF16), V((16, length), BF16),
             dma((3,)), dma((4,)), dma((2,)), dma((2,)), dma((4,)), dma((4,)), dma((CHUNKS,)), dma((4, CHUNKS)), dma((CHUNKS,)),
             dma((4, CHUNKS)), dma((4, CHUNKS)), dma((4,)), dma((4,)), dma((8,)),
-            dma((3, 3)), dma((3, 3, 4)), dma((3, 3, 3)), dma((3, 4, 8)),
+            dma((3, 4, 2)), dma((3, 4)), dma((3, 4, 2)), dma((3, 4, 4)), dma((3, 4, 8)),
         ],
         compiler_params=pltpu.CompilerParams(vmem_limit_bytes=LIMIT, collective_id=0, has_side_effects=True),
         name="attention_forward",
-    )(frames, w_t, small, kmask, hot, w_up, w_down, w_out)
+    )(frames, w_query, w_key, w_value, b_query, b_value, b_up, segments, padding, w_up, w_down, w_out)
 
 
 def norm_stats(v):
@@ -416,25 +498,45 @@
 
 
 def middle_kernel(
-    skip_ref, mixed_ref, frames_ref, cot_ref, vec_ref, bup_ref, wout_ref, wup_ref, wdown_ref,
+    skip_ref, mixed_ref, frames_ref, cot_ref, b_out, gain_one, shift_one, b_down, gain_two, shift_two, bup_ref, w_out, w_up, w_down, out_all, up_all, down_all,
     layer_ref, gone_ref, gmixed_ref, normed_ref, act_ref, ginner_ref, gbranch_ref, gatt_ref, small_ref,
-    slope_ref,
+    slope_ref, wout_ref, wup_ref, wdown_ref, sems,
 ):
+    z = lax.axis_index("mp")
+    mats = ((w_out, out_all, wout_ref), (w_up, up_all, wup_ref), (w_down, down_all, wdown_ref))
+    for m, (own, everyone, dst) in enumerate(mats):
+        for s in range(4):
+            @pl.when(z == s)
+            def _():
+                pltpu.make_async_copy(own, dst.at[s], sems.at[m, s]).start()
+
+            @pl.when(z != s)
+            def _():
+                pltpu.make_async_copy(everyone.at[s], dst.at[s], sems.at[m, s]).start()
+
+    def arrive(m, s):
+        pltpu.make_async_copy(mats[m][0], mats[m][2].at[s], sems.at[m, s]).wait()
+
     skipped = skip_ref[0] == 1
-    b_out, gain_one, shift_one, b_down, gain_two, shift_two = (vec_ref[i : i + 1, :] for i in range(6))
+    b_out, gain_one, shift_one, b_down, gain_two, shift_two = (row_of(v) for v in (b_out, gain_one, shift_one, b_down, gain_two, shift_two))
     frames = frames_ref[...].astype(F32)
-    attended = mm(mixed_ref[...], wout_ref[...], 0, 0) + b_out
+    for s in range(4):
+        arrive(0, s)
+    all_out = wout_ref[...].reshape(mixed_ref.shape[0], frames.shape[1])
+    attended = mm(mixed_ref[...], all_out, 0, 0) + b_out
     hat_one, r_one = norm_stats(frames + attended)
     normed = hat_one * gain_one + shift_one
     normed_ref[...] = normed.astype(BF16)
     parts = wup_ref.shape[0]
     branch = jnp.zeros_like(normed)
     for s in range(parts):
-        inner = mm(normed_ref[...], wup_ref[s]) + bup_ref[s : s + 1, :]
+        arrive(1, s)
+        inner = mm(normed_ref[...], wup_ref[s]) + bup_ref[s, 0:1, :]
         cdf = 0.5 * (1.0 + lax.erf(inner * (0.5**0.5)))
         slope_ref[s] = cdf + inner * (jnp.exp(-0.5 * inner * inner) * 0.3989422804014327)
         act = (inner * cdf).astype(BF16)
         act_ref[s] = act
+        arrive(2, s)
         branch = branch + mm(act, wdown_ref[s])
     hat_two, r_two = norm_stats(normed + (branch + b_down))
     result = hat_two * gain_two + shift_two
@@ -462,7 +564,7 @@
     small_ref[3:4, :] = jnp.sum(gatt.astype(F32), 0, keepdims=True)
     small_ref[4:5, :] = jnp.sum(grad_normed * hat_one, 0, keepdims=True)
     small_ref[5:6, :] = jnp.sum(grad_normed, 0, keepdims=True)
-    gmixed_ref[...] = mm(wout_ref[...], gatt, 1, 1).astype(BF16)
+    gmixed_ref[...] = mm(all_out, gatt, 1, 1).astype(BF16)
 
 
 def attend_back(h, i, cols, q_aug, k_aug, v_aug, k_t, do_aug, dq_acc, dk_acc, dv_acc):
@@ -486,9 +588,9 @@
     x_all, w_t, mixed_heads, q_aug, k_aug, v_aug, k_t,
     frames_grad, dw_out, up_out, down_out, out_out, small_out,
     do_in, do_aug, dk_acc, dv_acc, grads,
-    big, away, core_in, plane_in, mid, z_in, bigo, core_ino, plane_ino, mido, z_ino,
+    big, away, core_in, near_in, across_in, mid, z_in, bigo, core_ino, near_ino, across_ino, mido, z_ino,
     part, sib_in, line_in, dw_own, dw_in, dw_mid, dw_z, small_mine, small_plane, small_mid, small_z,
-    gm_s, gm_r, ci_s, ci_r, pl_s, pl_r, z_s, z_r, ag_s, ag_r, agf_s,
+    gm_s, gm_r, ci_s, ci_r, nr_s, nr_r, ac_s, ac_r, z_s, z_r, ag_s, ag_r,
     part_s, part_r, line_s, line_r, dwp_s, dwp_r, dwz_s, dwz_r, dwo_s, dwo_r, dwf_s, sp_s, sp_r, sz_s, sz_r,
 ):
     at = Place()
@@ -557,32 +659,42 @@
             at.send(bigo.at[1 - c], core_ino, ci_s.at[j], ci_r.at[j], at.sib, z)
 
     def core_job(j):
+        at.got(core_in.at[j] if j < n_big else core_ino, ci_r.at[j])
         if j < n_big:
-            at.got(core_in.at[j], ci_r.at[j])
             big[j] = total(big[j], core_in[j]).astype(BF16)
-            for k in (1, 2, 3):
-                at.send(big.at[j, big_rows((q + k) % 4)], plane_in.at[3 - k, j], pl_s.at[j, k - 1], pl_r.at[j, 3 - k], at.chip(k), z)
         else:
-            at.got(core_ino, ci_r.at[j])
             bigo[c] = total(bigo[c], core_ino[...]).astype(BF16)
-            for k in (1, 2, 3):
-                at.send(bigo.at[c, :, out_rows((q + k) % 4)], plane_ino.at[3 - k], pl_s.at[j, k - 1], pl_r.at[j, 3 - k], at.chip(k), z)
+        for i, chip in enumerate((at.near_chip, at.opposite_chip)):
+            if j < n_big:
+                at.send(big.at[j, big_rows(chip)], near_in.at[i, j], nr_s.at[j, i], nr_r.at[j, i], at.near, z)
+            else:
+                at.send(bigo.at[c, :, out_rows(chip)], near_ino.at[i], nr_s.at[j, i], nr_r.at[j, i], at.near, z)
+
+    def near_job(j):
+        if j < n_big:
+            for i in range(2):
+                at.got(near_in.at[i, j], nr_r.at[j, i])
+            near_in[1, j] = total(big[j, big_rows(at.across_chip)], near_in[1, j]).astype(BF16)
+            at.send(near_in.at[1, j], across_in.at[j], ac_s.at[j], ac_r.at[j], at.across, z)
+        else:
+            for i in range(2):
+                at.got(near_ino.at[i], nr_r.at[j, i])
+            near_ino[1] = total(bigo[c, :, out_rows(at.across_chip)], near_ino[1]).astype(BF16)
+            at.send(near_ino.at[1], across_ino, ac_s.at[j], ac_r.at[j], at.across, z)
 
     def plane_job(j):
         if j < n_big:
             kind, s = j // 4, j % 4
-            for k in range(3):
-                at.got(plane_in.at[k, j], pl_r.at[j, k])
-            mid[j] = total(big[j, big_rows(q)], plane_in[0, j], plane_in[1, j], plane_in[2, j]).astype(BF16)
+            at.got(across_in.at[j], ac_r.at[j])
+            mid[j] = total(big[j, big_rows(q)], near_in[0, j], across_in[j]).astype(BF16)
 
             @pl.when(z != s)
             def _():
                 slot = 3 - (s - z + 4) % 4
                 at.send(mid.at[j], z_in.at[slot, kind], z_s.at[j], z_r.at[kind, slot], at.d, s)
         else:
-            for k in range(3):
-                at.got(plane_ino.at[k], pl_r.at[j, k])
-            mido[...] = total(bigo[c, :, out_rows(q)], plane_ino[0], plane_ino[1], plane_ino[2]).astype(BF16)
+            at.got(across_ino, ac_r.at[j])
+            mido[...] = total(bigo[c, :, out_rows(q)], near_ino[0], across_ino[...]).astype(BF16)
             for s in range(4):
                 @pl.when(z != s)
                 def _():
@@ -603,17 +715,23 @@
         else:
             piece[...] = total(mido[z], z_ino[0], z_ino[1], z_ino[2]).astype(BF16)
         sem = ag_r.at[kind, 2 * q + c]
-        for k in (1, 2, 3):
-            at.send(piece, piece, ag_s.at[kind, k], sem, at.chip(k), z)
-        at.send(piece, piece, ag_s.at[kind, 0], sem, at.sib, z)
+        at.send(piece, piece, ag_s.at[kind, 0], sem, at.near, z)
+        at.send(piece, piece, ag_s.at[kind, 1], sem, at.across, z)
+        at.send(piece, piece, ag_s.at[kind, 2], sem, at.sib, z)
+
+    def pass_job(kind):
+        piece = final_piece(kind, at.near_chip, c)
+        sem = ag_r.at[kind, 2 * at.near_chip + c]
+        at.got(piece, sem)
+        at.send(piece, piece, ag_s.at[kind, 3], sem, at.across, z)
+        at.send(piece, piece, ag_s.at[kind, 4], sem, at.sib, z)
 
     def share_job(kind):
-        for k in (1, 2, 3):
-            chip = (q + k) % 4
+        for i, chip in enumerate((at.across_chip, at.opposite_chip)):
             piece = final_piece(kind, chip, c)
             sem = ag_r.at[kind, 2 * chip + c]
             at.got(piece, sem)
-            at.send(piece, piece, agf_s.at[kind, k - 1], sem, at.sib, z)
+            at.send(piece, piece, ag_s.at[kind, 5 + i], sem, at.sib, z)
 
     def end_job(kind):
         for k in range(4):
@@ -627,18 +745,23 @@
     core_job(n_big - 1)
     core_job(n_big)
 
-    for s in range(4):
-        mine = jnp.logical_and(primary, z == s)
+    def block_of(turn):
+        low = z // 2
+        near = z + low * (3 - 2 * z)
+        s = jnp.where(near == 0, turn, jnp.where(turn == 0, 1, jnp.where(turn == 1, 2, jnp.where(turn == 2, 0, 3))))
+        return s + low * (3 - 2 * s)
+
+    def prepare(i):
+        mine = jnp.logical_and(primary, z == i)
 
         @pl.when(mine)
         def _():
-            pltpu.make_async_copy(gmixed.at[pl.ds(s * width, width)], do_in.at[s], gm_s.at[s]).wait()
+            pltpu.make_async_copy(gmixed.at[pl.ds(pl.multiple_of(i * width, 64), width)], do_in.at[i], gm_s.at[i]).wait()
 
         @pl.when(jnp.logical_not(mine))
         def _():
-            at.got(do_in.at[s], gm_r.at[s])
-
-    def prepare(i, _):
+            at.got(do_in.at[i], gm_r.at[i])
+
         cols = pl.ds(pl.multiple_of(i * share, share), share)
         for h in range(heads):
             hs = slice(h * HEAD_DIM, (h + 1) * HEAD_DIM)
@@ -647,25 +770,38 @@
             inner = jnp.sum(do.astype(F32) * mixed_heads[i, hs, :].astype(F32), 0, keepdims=True)
             do_aug[h, HEAD_DIM : HEAD_DIM + 16, cols] = pad_rows(split3(-inner), 16, share)
             do_aug[h, HEAD_DIM + 16 :, cols] = jnp.zeros((48, share), BF16)
-        return 0
-
-    lax.fori_loop(0, 4, prepare, 0)
+
     dk_acc[...] = jnp.zeros_like(dk_acc)
     dv_acc[...] = jnp.zeros_like(dv_acc)
 
-    def attention_step(i, _):
+    N, M, Q = near_job, plane_job, final_job
+    jobs = {-1: ((N, 0), (N, 1),), 0: ((N, 2), (M, 0),), 1: ((M, 1),), 2: ((N, 3), (M, 2),), 4: ((N, 4), (M, 3),), 6: ((N, 5), (M, 4),), 8: ((N, 6), (M, 5), (Q, 0),), 10: ((N, 7), (M, 6),)}
+
+    def attention_step(t, _):
+        i, h = block_of(t // heads), t % heads
+
+        @pl.when(h == 0)
+        def _():
+            prepare(i)
+
         cols = pl.ds(pl.multiple_of(i * share, share), share)
-        for h in range(heads):
-            dq = attend_back(h, i, cols, q_aug, k_aug, v_aug, k_t, do_aug, None, dk_acc, dv_acc)
-            grads[h * HEAD_DIM : (h + 1) * HEAD_DIM, cols] = (dq.astype(BF16).astype(F32) * HEAD_DIM**-0.5).astype(BF16)
-        for n in range(4):
-            @pl.when(i == n)
-            def _():
-                for j in (2 * n, 2 * n + 1):
-                    plane_job(j)
+        dq = attend_back(h, i, cols, q_aug, k_aug, v_aug, k_t, do_aug, None, dk_acc, dv_acc)
+        hs = pl.ds(pl.multiple_of(h * HEAD_DIM, HEAD_DIM), HEAD_DIM)
+        grads[hs, cols] = (dq.astype(BF16).astype(F32) * HEAD_DIM**-0.5).astype(BF16)
+        for when, todo in jobs.items():
+            if 0 <= when < 99:
+                @pl.when(t == when)
+                def _():
+                    for job, j in todo:
+                        job(j)
+
         return 0
 
-    lax.fori_loop(0, 4, attention_step, 0)
+    for job, j in jobs.get(-1, ()):
+        job(j)
+    lax.fori_loop(0, 4 * heads, attention_step, 0)
+    for job, j in jobs.get(99, ()):
+        job(j)
     for h in range(heads):
         grads[width + h * HEAD_DIM : width + (h + 1) * HEAD_DIM, :] = dk_acc[h].astype(BF16)
         grads[2 * width + h * HEAD_DIM : 2 * width + (h + 1) * HEAD_DIM, :] = dv_acc[h].astype(BF16)
@@ -712,17 +848,16 @@
                     part[here] = total(part[here], sib_in[here]).astype(BF16)
                     at.send(part.at[here], line_in.at[here], line_s.at[s, ch], line_r.at[s, ch], at.d, at.own_line(1 - at.p))
 
-    def part_step(k, _):
+    for k in range(4):
         part_job(at.line(order(k)))
-
-        @pl.when(k > 0)
-        def _():
-            line_job(order(k - 1))
-
-        return 0
-
-    lax.fori_loop(0, 4, part_step, 0)
-    line_job(order(3))
+        if k > 0:
+            @pl.when(jnp.logical_or(at.p == 0, k == 1))
+            def _():
+                line_job(order(k - 1))
+
+    @pl.when(at.p == 0)
+    def _():
+        line_job(order(3))
 
     made = mm(grads[:, 0:share], x_all[0])
     for s in range(1, 4):
@@ -731,53 +866,74 @@
     fourth = made.shape[0] // 4
     for i in range(4):
         dw_own[i] = made[i * fourth : (i + 1) * fourth]
-    for k in (1, 2, 3):
-        at.send(dw_own.at[(q + k) % 4], dw_in.at[3 - k], dwp_s.at[k - 1], dwp_r.at[3 - k], at.chip(k), z)
-
-    plane_job(n_big)
-    for k in range(7):
-        at.got(small_plane.at[k], sp_r.at[k])
-    small_mid[...] = total(small_mine[...], *(small_plane[k] for k in range(7)))
-    for k in (1, 2, 3):
-        at.send(small_mid, small_z.at[3 - k], sz_s.at[k - 1], sz_r.at[3 - k], at.d, (z + k) % 4)
-
-    final_job(0)
-
-    @pl.when(at.p == 2)
-    def _():
-        s = at.own_line(3)
-        for ch in range(CHUNKS):
-            here = (s, rows(ch))
-            at.got(line_in.at[here], line_r.at[s, ch])
-            at.send(line_in.at[here], line_in.at[here], line_s.at[s, ch], line_r.at[s, ch], at.d, s)
+    at.send(dw_own.at[at.near_chip], dw_in.at[0], dwp_s.at[0], dwp_r.at[0], at.near, z)
+    at.send(dw_own.at[at.opposite_chip], dw_in.at[1], dwp_s.at[1], dwp_r.at[1], at.near, z)
 
     def dw_rows(i):
         return pl.ds(pl.multiple_of(i * fourth, 16), fourth)
 
-    for k in range(3):
-        at.got(dw_in.at[k], dwp_r.at[k])
-    dw_mid[...] = total(dw_own[q], dw_in[0], dw_in[1], dw_in[2]).astype(BF16)
-
-    @pl.when(secondary)
-    def _():
-        at.send(dw_mid, dw_z, dwz_s.at[0], dwz_r.at[0], at.d, at.far)
-
-    final_job(1)
-    final_job(2)
-    share_job(0)
-
-    @pl.when(primary)
-    def _():
-        at.got(dw_z, dwz_r.at[0])
-        piece = dw_out.at[dw_rows(q)]
-        piece[...] = total(dw_mid[...], dw_z[...]).astype(BF16)
+    def small_sum(_):
+        for k in range(7):
+            at.got(small_plane.at[k], sp_r.at[k])
+        small_mid[...] = total(small_mine[...], *(small_plane[k] for k in range(7)))
         for k in (1, 2, 3):
-            at.send(piece, piece, dwo_s.at[k], dwo_r.at[q], at.chip(k), z)
-        at.send(piece, piece, dwo_s.at[0], dwo_r.at[q], at.sib, z)
-
-    for k in range(3):
-        at.got(small_z.at[k], sz_r.at[k])
-    small_out[...] = total(small_mid[...], small_z[0], small_z[1], small_z[2])
+            at.send(small_mid, small_z.at[3 - k], sz_s.at[k - 1], sz_r.at[3 - k], at.d, (z + k) % 4)
+
+    def small_end(_):
+        for k in range(3):
+            at.got(small_z.at[k], sz_r.at[k])
+        small_out[...] = total(small_mid[...], small_z[0], small_z[1], small_z[2])
+
+    def onward(k):
+        @pl.when(at.p == 1)
+        def _():
+            line_job(order(k))
+
+        if k == 1:
+            @pl.when(at.p == 2)
+            def _():
+                s = at.own_line(3)
+                for ch in range(CHUNKS):
+                    here = (s, rows(ch))
+                    at.got(line_in.at[here], line_r.at[s, ch])
+                    at.send(line_in.at[here], line_in.at[here], line_s.at[s, ch], line_r.at[s, ch], at.d, s)
+
+    def dw_across(_):
+        for k in range(2):
+            at.got(dw_in.at[k], dwp_r.at[k])
+        dw_in[1] = total(dw_own[at.across_chip], dw_in[1]).astype(BF16)
+        at.send(dw_in.at[1], dw_in.at[2], dwp_s.at[2], dwp_r.at[2], at.across, z)
+
+    def dw_plane(_):
+        at.got(dw_in.at[2], dwp_r.at[2])
+        dw_mid[...] = total(dw_own[q], dw_in[0], dw_in[2]).astype(BF16)
+
+        @pl.when(secondary)
+        def _():
+            at.send(dw_mid, dw_z, dwz_s.at[0], dwz_r.at[0], at.d, at.far)
+
+    def dw_final(_):
+        @pl.when(primary)
+        def _():
+            at.got(dw_z, dwz_r.at[0])
+            piece = dw_out.at[dw_rows(q)]
+            piece[...] = total(dw_mid[...], dw_z[...]).astype(BF16)
+            at.send(piece, piece, dwo_s.at[0], dwo_r.at[q], at.near, z)
+            at.send(piece, piece, dwo_s.at[1], dwo_r.at[q], at.across, z)
+            at.send(piece, piece, dwo_s.at[2], dwo_r.at[q], at.sib, z)
+
+    def dw_pass(_):
+        @pl.when(primary)
+        def _():
+            i = at.near_chip
+            piece = dw_out.at[dw_rows(i)]
+            at.got(piece, dwo_r.at[i])
+            at.send(piece, piece, dwo_s.at[3], dwo_r.at[i], at.across, z)
+            at.send(piece, piece, dwf_s.at[0], dwo_r.at[i], at.sib, z)
+
+    N, M, Q, U, V = near_job, plane_job, final_job, pass_job, share_job
+    for job, j in ((M, 7), (N, 8), (small_sum, 0), (dw_across, 0), (dw_plane, 0), (onward, 1), (M, 8), (onward, 2), (dw_final, 0), (Q, 1), (U, 0), (dw_pass, 0), (onward, 3), (V, 0), (Q, 2), (U, 1), (small_end, 0), (U, 2), (V, 1), (V, 2)):
+        job(j)
 
     skipped = skip_ref[0] == 1
     for ch in range(CHUNKS):
@@ -795,16 +951,13 @@
         grad = gone[...] + line_in[z].astype(F32)
         frames_grad[...] = jnp.where(skipped, cot[...].astype(F32), grad).astype(BF16)
 
-    share_job(1)
-    share_job(2)
 
     @pl.when(primary)
     def _():
-        for k in (1, 2, 3):
-            i = (q + k) % 4
+        for k, i in ((1, at.across_chip), (2, at.opposite_chip)):
             piece = dw_out.at[dw_rows(i)]
             at.got(piece, dwo_r.at[i])
-            at.send(piece, piece, dwf_s.at[k - 1], dwo_r.at[i], at.sib, z)
+            at.send(piece, piece, dwf_s.at[k], dwo_r.at[i], at.sib, z)
 
     @pl.when(secondary)
     def _():
@@ -824,26 +977,26 @@
     for j in range(n_big):
         if j >= 4:
             at.sent(core_in.at[j], ci_s.at[j])
-        for k in range(3):
-            at.sent(plane_in.at[k, j], pl_s.at[j, k])
+        for k in range(2):
+            at.sent(near_in.at[k, j], nr_s.at[j, k])
+        at.sent(across_in.at[j], ac_s.at[j])
 
         @pl.when(z != j % 4)
         def _():
             at.sent(mid.at[j], z_s.at[j])
 
     at.sent(core_ino, ci_s.at[n_big])
-    for k in range(3):
-        at.sent(plane_ino.at[k], pl_s.at[n_big, k])
+    for k in range(2):
+        at.sent(near_ino.at[k], nr_s.at[n_big, k])
+    at.sent(across_ino, ac_s.at[n_big])
     for s in range(4):
         @pl.when(z != s)
         def _():
             at.sent(mido.at[s], z_s.at[n_big + s])
 
     for kind in range(3):
-        for k in range(4):
+        for k in range(7):
             at.sent(final_piece(kind, q, c), ag_s.at[kind, k])
-        for k in range(3):
-            at.sent(final_piece(kind, q, c), agf_s.at[kind, k])
     for k in range(7):
         at.sent(small_mine, sp_s.at[k])
     for k in range(3):
@@ -891,15 +1044,15 @@
         scratch_shapes=[
             V((4, width, share), BF16), V((heads, 128, length), BF16),
             V((heads, HEAD_DIM, length), F32), V((heads, HEAD_DIM, length), F32), V((3 * width, length), BF16),
-            V((8, hd, d), BF16), V((4, hd, d), BF16), V((8, hd, d), BF16), V((3, 8, hd // 4, d), BF16), V((8, hd // 4, d), BF16),
+            V((8, hd, d), BF16), V((4, hd, d), BF16), V((8, hd, d), BF16), V((2, 8, hd // 4, d), BF16), V((8, hd // 4, d), BF16), V((8, hd // 4, d), BF16),
             V((3, 2, hd // 4, d), BF16),
-            V((2, 4, width, ho), BF16), V((4, width, ho), BF16), V((3, 4, width // 4, ho), BF16), V((4, width // 4, ho), BF16),
+            V((2, 4, width, ho), BF16), V((4, width, ho), BF16), V((2, 4, width // 4, ho), BF16), V((4, width // 4, ho), BF16), V((4, width // 4, ho), BF16),
             V((3, width // 4, ho), BF16),
             V((4, share, d), BF16), V((4, share, d), BF16), V((4, share, d), BF16),
             V((4, 3 * width // 4, d), BF16), V((3, 3 * width // 4, d), BF16), V((3 * width // 4, d), BF16), V((3 * width // 4, d), BF16),
             V((16, d), F32), V((7, 16, d), F32), V((16, d), F32), V((3, 16, d), F32),
-            dma((4,)), dma((4,)), dma((9,)), dma((9,)), dma((9, 3)), dma((9, 3)), dma((12,)), dma((3, 3)),
-            dma((3, 4)), dma((3, 8)), dma((3, 3)),
+            dma((4,)), dma((4,)), dma((9,)), dma((9,)), dma((9, 2)), dma((9, 2)), dma((9,)), dma((9,)), dma((12,)), dma((3, 3)),
+            dma((3, 7)), dma((3, 8)),
             dma((4, CHUNKS)), dma((4, CHUNKS)), dma((4, CHUNKS)), dma((4, CHUNKS)), dma((3,)), dma((3,)), dma((1,)), dma((1,)),
             dma((4,)), dma((4,)), dma((3,)), dma((7,)), dma((7,)), dma((3,)), dma((3,)),
         ],
@@ -907,6 +1060,23 @@
         name="attention_backward",
     )(skip, gmixed, mixed_own, normed, act, ginner, gbranch, gatt, small, gone, cot,
       x_all, w_t, mixed_heads, q_aug, k_aug, v_aug, k_t)
+
+
+def last_kernel(dw, up, down, out, small, *outs):
+    z = lax.axis_index("mp")
+    d_query, d_key, d_value, d_up, d_down, d_out, b_query, b_value, b_up = outs[:9]
+    width = d_out.shape[0]
+    for i, target in enumerate((d_query, d_key, d_value)):
+        target[...] = dw[i * width : (i + 1) * width].astype(F32)
+    d_up[...] = up[...].astype(F32)
+    d_down[...] = down[...].astype(F32)
+    d_out[...] = out[...].astype(F32)
+    bias = small[pl.ds(10 + z, 1), :]
+    b_query[...] = bias[:, 0:width].reshape(width)
+    b_value[...] = bias[:, 2 * width : 3 * width].reshape(width)
+    b_up[...] = small[pl.ds(6 + z, 1), :].reshape(small.shape[1])
+    for i, target in enumerate(outs[9:]):
+        target[...] = small[i : i + 1, :].reshape(small.shape[1])
 
 
 def S(shape, dtype=BF16):
@@ -923,30 +1093,10 @@
     width = w_query.shape[1]
     heads = width // HEAD_DIM
     params = pltpu.CompilerParams(vmem_limit_bytes=LIMIT)
-    scale = HEAD_DIM**-0.5
     own = frames[0]
-    w_t = jnp.concatenate([w_query.T, w_key.T, w_value.T], 0)
-    v_row = jnp.concatenate(
-        [b_value.reshape(heads, HEAD_DIM), jnp.ones((heads, 3)), jnp.zeros((heads, 61))], 1
-    ).reshape(1, heads * 128)
-    seg, pad = segments[0], padding[0]
-    ids = jnp.arange(4)
-    ok = (seg[:, None] == ids[None]) & (pad[:, None] == 1)
-    k_mask = jnp.concatenate(
-        [jnp.zeros((length, 64)), jnp.where(ok, 0.0, -1e30), jnp.ones((length, 3)), jnp.zeros((length, 57))], 1
-    ).astype(BF16)
-    hot = jnp.concatenate([(seg[None] == ids[:, None]).astype(BF16), jnp.zeros((12, length), BF16)], 0)
-
-    zero = jnp.zeros((d,), F32)
-    bias_row = jnp.concatenate([b_query, jnp.zeros_like(b_query), b_value, jnp.zeros((d - 3 * width,), F32)])
-    v_row = jnp.concatenate([v_row[0], jnp.zeros((d - heads * 128,), F32)])
-    small = jnp.stack([b_up, bias_row, v_row] + [zero] * 5)
     x_all, w_t, mixed, mixed_own, q_aug, k_aug, v_aug, k_t, small_all, wup, wdown, wout = run_forward(
-        own, w_t, small, k_mask, hot, w_up, w_down, w_out
+        own, w_query.T, w_key.T, w_value.T, b_query, b_value, b_up, segments, padding, w_up, w_down, w_out
     )
-    wout = wout.reshape(mp * width, d)
-    bup = small_all[:, 0]
-    vec = jnp.stack([b_out, gain_one, shift_one, b_down, gain_two, shift_two] + [b_out] * 2)
     f = w_up.shape[1]
     layer, gone, gmixed, normed, act, ginner, gbranch, gatt, small = pl.pallas_call(
         middle_kernel,
@@ -954,10 +1104,13 @@
             S((share, d)), S((share, d), F32), S((mp * width, share)), S((share, d)), S((mp, share, f)),
             S((mp, share, f)), S((share, d)), S((share, d)), S((16, d), F32),
         ),
-        in_specs=[SMEM] + [VMEM] * 8, out_specs=[VMEM] * 9,
-        scratch_shapes=[pltpu.VMEM((mp, share, f), F32)],
+        in_specs=[SMEM] + [VMEM] * 10 + [pl.BlockSpec(memory_space=pl.ANY)] * 6, out_specs=[VMEM] * 9,
+        scratch_shapes=[
+            pltpu.VMEM((mp, share, f), F32), pltpu.VMEM((mp, width, d), BF16), pltpu.VMEM((mp, d, f), BF16),
+            pltpu.VMEM((mp, f, d), BF16), pltpu.SemaphoreType.DMA((3, 4)),
+        ],
         compiler_params=params, name="feed_forward",
-    )(skip_flag, mixed_own, own, cotangent[0], vec, bup, wout, wup, wdown)
+    )(skip_flag, mixed_own, own, cotangent[0], b_out, gain_one, shift_one, b_down, gain_two, shift_two, small_all, w_out, w_up, w_down, wout, wup, wdown)
     frames_grad, wgrad, gup, gdown, gout, small = run_backward(
         skip_flag, gmixed, mixed_own, normed, act, ginner, gbranch, gatt, small, gone, cotangent[0],
         x_all, w_t, mixed, q_aug, k_aug, v_aug, k_t,
@@ -968,14 +1121,18 @@
         wgrad, gup, gdown, gout, small = (
             lax.psum(v.astype(F32), "dp", axis_index_groups=groups) for v in (wgrad, gup, gdown, gout, small)
         )
-    wgrad, gup, gdown, gout = (v.astype(F32) for v in (wgrad, gup, gdown, gout))
-    z = lax.axis_index("mp")
-    bias = small[10 + z]
+    d_query, d_key, d_value, d_up, d_down, d_out, b_q, b_v, b_u, *rest = pl.pallas_call(
+        last_kernel,
+        out_shape=tuple(
+            S(s, F32) for s in [(width, d)] * 3 + [(d, f), (f, d), (width, d), (width,), (width,), (f,)] + [(d,)] * 6
+        ),
+        in_specs=[VMEM] * 5, out_specs=[VMEM] * 15, compiler_params=params, name="outputs",
+    )(wgrad, gup, gdown, gout, small)
+    b_down_grad, gain_two_grad, shift_two_grad, b_out_grad, gain_one_grad, shift_one_grad = rest
     return (
-        layer[None], frames_grad[None],
-        wgrad[:width].T, bias[:width], wgrad[width : 2 * width].T, wgrad[2 * width :].T, bias[2 * width : 3 * width],
-        gout, small[3], small[4], small[5],
-        gup, small[6 + z], gdown, small[0], small[1], small[2],
+        layer[None], frames_grad[None], d_query.T, b_q, d_key.T, d_value.T, b_v,
+        d_out, b_out_grad, gain_one_grad, shift_one_grad,
+        d_up, b_u, d_down, b_down_grad, gain_two_grad, shift_two_grad,
     )
 
 

time: 285 us -> 222 us (0.78)
  the two profiles are of different devices: /device:TPU:9 before, /device:TPU:1 now
where the time goes in v3:
time: 222 us; the launch traced here: 219 us
  Pallas kernels  216 us (97%)
    pallas_call x1, Pallas kernels, run_backward(): pl.pallas_call(backward_kernel, out_shape=(S((share, d)), S((3 * width, d...  110 us
    pallas_call x1, Pallas kernels, run_forward(): pl.pallas_call(forward_kernel, out_shape=(S((4, share, d)), S((3 * width,...  83.3 us
    pallas_call x1, Pallas kernels, shards(): pl.pallas_call(middle_kernel, out_shape=(S((share, d)), S((share, d), F32...  18.4 us
    pallas_call x1, Pallas kernels, shards(): pl.pallas_call(last_kernel, out_shape=tuple((S(s, F32) for s in [(width,...  5.08 us

profile of v3, /device:TPU:1, one launch (start us, length us, event | category | flops | bytes accessed | tf_op | source)
XLA Modules:
  0.0 219.0 jit_solution(5941748908924378172)
XLA Ops:
  1.3 83.3 %attention_forward.1 = (bf16[4,384,768]{2,1,0:T(8,128)(2,1)}, bf16[576,768]{1,0:T(8,128)(2,1)}, bf16[4,192,384]{2,1,0:T(8,128)(2,1)}, bf16[768,384]{1,0:T(8,128)...) custom-call(bf16[384,768]{1,0:T(8,128)(2,1)} %bitcast.10, ...), custom_call_target="tpu_custom_call" | custom-call | tf_op jit(solution)/shard_map/attention_forward/pallas_call | solution.py:468
  84.6 18.4 %feed_forward.1 = (bf16[384,768]{1,0:T(8,128)(2,1)}, f32[384,768]{1,0:T(8,128)}, bf16[768,384]{1,0:T(8,128)(2,1)}, bf16[384,768]{1,0:T(8,128)(2,1)}, bf16[4,384,...) custom-call(s32[1]{0:T(128)S(6)} %copy.38.skip_ref, ...), custom_call_target="tpu_custom_call" | custom-call | tf_op jit(solution)/shard_map/feed_forward/pallas_call | solution.py:1101
  103.0 109.6 %attention_backward.1 = (bf16[384,768]{1,0:T(8,128)(2,1)}, bf16[576,768]{1,0:T(8,128)(2,1)}, bf16[768,768]{1,0:T(8,128)(2,1)}, bf16[768,768]{1,0:T(8,128)(2,1)},...) custom-call(s32[1]{0:T(128)S(6)} %copy.38.skip_ref, bf16[768,384]{1,0:T(8,128)(2,1)} %get-tuple-element.65.gmixed, ...), custom_call_target="tpu_custom_call" | custom-call | tf_op jit(solution)/shard_map/attention_backward/pallas_call | solution.py:1038
  212.6 0.0 copy-start
  212.6 5.1 %outputs.1 = (f32[192,768]{1,0:T(8,128)}, f32[192,768]{1,0:T(8,128)}, f32[192,768]{1,0:T(8,128)}, f32[768,768]{1,0:T(8,128)}, f32[768,768]{1,0:T(8,128)}, /*inde...) custom-call(bf16[576,768]{1,0:T(8,128)(2,1)} %get-tuple-element.81.d, ...), custom_call_target="tpu_custom_call" | custom-call | tf_op jit(solution)/shard_map/outputs/pallas_call | solution.py:1124
  217.7 0.0 copy-done
  217.7 0.8 copy.39
Async XLA Ops:
  212.6 5.1 %copy-start = (bf16[384,768]{1,0:T(8,128)(2,1)S(1)}, bf16[384,768]{1,0:T(8,128)(2,1)}, u32[]{:S(2)}) copy-start(bf16[384,768]{1,0:T(8,128)(2,1)} %get-tuple-element.80) | copy-start | bytes 1769476

commit v4 on v3

--- a/solution.py
+++ b/solution.py
@@ -63,6 +63,81 @@
     one_hot = q_aug[h, HEAD_DIM : HEAD_DIM + 16, cols].astype(F32)[0:4]
     q_aug[h, HEAD_DIM : HEAD_DIM + 16, cols] = pad_rows((one_hot,) + split3(-(peak + jnp.log(summed))), 16, mixed.shape[1])
     return mixed.astype(BF16)
+
+
+def norm_stats(v):
+    centered = v - jnp.mean(v, -1, keepdims=True)
+    r = lax.rsqrt(jnp.mean(centered * centered, -1, keepdims=True) + 1e-05)
+    return centered * r, r
+
+
+def norm_back(c, gain, hat, r):
+    e = c * gain
+    return r * (e - jnp.mean(e, -1, keepdims=True) - hat * jnp.mean(e * hat, -1, keepdims=True))
+
+
+def feed_forward(
+    skip_ref, mixed_ref, frames_ref, cot_ref, b_out, gain_one, shift_one, b_down, gain_two, shift_two, small_all,
+    wout_ref, wup_ref, wdown_ref, arrive, leave, outside,
+    layer_ref, gone_ref, gmixed_ref, normed_ref, act_ref, ginner_ref, gbranch_ref, gatt_ref, small_ref, slope_ref,
+):
+    skipped = skip_ref[0] == 1
+    mixed_h, layer_h, gone_h, gmixed_h, normed_h, act_h, ginner_h, gbranch_h, gatt_h = outside
+    b_out, gain_one, shift_one, b_down, gain_two, shift_two = (row_of(v) for v in (b_out, gain_one, shift_one, b_down, gain_two, shift_two))
+    frames = frames_ref[...].astype(F32)
+    arrive(2)
+    all_out = wout_ref[...].reshape(mixed_ref.shape[0], frames.shape[1])
+    attended = mm(mixed_ref[...], all_out, 0, 0) + b_out
+    hat_one, r_one = norm_stats(frames + attended)
+    normed = hat_one * gain_one + shift_one
+    normed_ref[...] = normed.astype(BF16)
+    leave(7, mixed_ref, mixed_h)
+    leave(8, normed_ref, normed_h)
+    parts = wup_ref.shape[0]
+    arrive(0)
+    for s in range(parts):
+        inner = mm(normed_ref[...], wup_ref[s]) + small_all[s, 0:1, :]
+        cdf = 0.5 * (1.0 + lax.erf(inner * (0.5**0.5)))
+        slope_ref[s] = cdf + inner * (jnp.exp(-0.5 * inner * inner) * 0.3989422804014327)
+        act_ref[s] = (inner * cdf).astype(BF16)
+        leave(9, act_ref, act_h, s)
+    arrive(1)
+    branch = mm(act_ref[0], wdown_ref[0])
+    for s in range(1, parts):
+        branch = branch + mm(act_ref[s], wdown_ref[s])
+    hat_two, r_two = norm_stats(normed + (branch + b_down))
+    result = hat_two * gain_two + shift_two
+    cot = cot_ref[...].astype(F32)
+    layer_ref[...] = jnp.where(skipped, frames, result).astype(BF16)
+    grad_out = jnp.where(skipped, 0.0, cot)
+    grad_two = norm_back(grad_out, gain_two, hat_two, r_two)
+    gbranch = grad_two.astype(BF16)
+    gbranch_ref[...] = gbranch
+    leave(13, layer_ref, layer_h)
+    leave(14, gbranch_ref, gbranch_h)
+    small_ref[10:16, :] = jnp.zeros_like(small_ref[10:16, :])
+    small_ref[0:1, :] = jnp.sum(gbranch.astype(F32), 0, keepdims=True)
+    small_ref[1:2, :] = jnp.sum(grad_out * hat_two, 0, keepdims=True)
+    small_ref[2:3, :] = jnp.sum(grad_out, 0, keepdims=True)
+    grad_normed = grad_two
+    for s in range(parts):
+        gact = mm(gbranch_ref[...], wdown_ref[s], 1, 1)
+        ginner = (gact * slope_ref[s]).astype(BF16)
+        ginner_ref[s] = ginner
+        leave(15, ginner_ref, ginner_h, s)
+        small_ref[6 + s : 7 + s, :] = jnp.sum(ginner.astype(F32), 0, keepdims=True)
+        grad_normed = grad_normed + mm(ginner, wup_ref[s], 1, 1)
+    grad_one = norm_back(grad_normed, gain_one, hat_one, r_one)
+    gone_ref[...] = grad_one
+    gatt = grad_one.astype(BF16)
+    gatt_ref[...] = gatt
+    leave(19, gone_ref, gone_h)
+    leave(20, gatt_ref, gatt_h)
+    small_ref[3:4, :] = jnp.sum(gatt.astype(F32), 0, keepdims=True)
+    small_ref[4:5, :] = jnp.sum(grad_normed * hat_one, 0, keepdims=True)
+    small_ref[5:6, :] = jnp.sum(grad_normed, 0, keepdims=True)
+    gmixed_ref[...] = mm(all_out, gatt, 1, 1).astype(BF16)
+    leave(21, gmixed_ref, gmixed_h)
 
 
 MESH = pl.DeviceIdType.MESH
@@ -131,8 +206,13 @@
 
 
 def forward_kernel(
-    frames, w_query, w_key, w_value, b_query, b_value, b_up, segments, padding, w_up, w_down, w_out,
-    x_all, w_t, mixed_heads, mixed_own, q_aug, k_aug, v_aug, k_t, small_all, up_all, down_all, out_all,
+    skip, frames, cot, w_query, w_key, w_value, b_query, b_value, b_up, b_out, gain_one, shift_one, b_down, gain_two, shift_two,
+    segments, padding, w_up, w_down, w_out,
+    x_all_h, w_t_h, mixed_heads_h, mixed_own_h, q_aug_h, k_aug_h, v_aug_h, k_t_h,
+    layer_h, gone_h, gmixed_h, normed_h, act_h, ginner_h, gbranch_h, gatt_h, small_sums,
+    x_all, w_t, mixed_heads, mixed_own, q_aug, k_aug, v_aug, k_t,
+    layer, gone, gmixed, normed, act, ginner, gbranch, gatt, out_sems,
+    small_all, up_all, down_all, out_all, slope,
     relay, v_t, w_pad, kmask, hot, w_own, small_own, kmask_own, hot_own,
     small_s, small_r, mask_s, mask_r, wq_s, wq_r, x_s, x_r, relay_r, on_s, fwd_s, mix_s, mix_r, local,
     line_s, near_s, far_s, core_s, w_r,
@@ -271,6 +351,8 @@
 
     for m in range(3):
         weights_first(m)
+    for m, (src, dst) in enumerate(mats):
+        pltpu.make_async_copy(src, dst.at[z], local.at[5 + m]).start()
 
     def relay_job(ch):
         @pl.when(at.p == 2)
@@ -316,8 +398,8 @@
             ]
 
     A, B, C = weights_line, weights_near, weights_across
-    early = {1: ((A, 0, 0), (A, 1, 0), (A, 2, 0),), 2: ((A, 0, 1), (A, 1, 1), (A, 2, 1), (B, 0, 0), (B, 1, 0), (B, 2, 0),), 3: ((A, 0, 2), (C, 0, 0), (C, 1, 0), (C, 2, 0),)}
-    jobs = {0: ((A, 1, 2), (B, 0, 1),), 1: ((A, 2, 2), (B, 1, 1),), 2: ((B, 2, 1), (C, 0, 1),), 3: ((C, 1, 1), (B, 0, 2),), 4: ((C, 2, 1), (B, 1, 2),), 5: ((B, 2, 2),), 6: ((C, 0, 2),), 7: ((C, 1, 2),), 8: ((C, 2, 2),)}
+    early = {1: ((A, 0, 0), (A, 2, 0), (A, 1, 0),), 2: ((A, 0, 1), (A, 2, 1), (A, 1, 1), (B, 0, 0), (B, 2, 0), (B, 1, 0),), 3: ((A, 0, 2), (C, 0, 0), (C, 2, 0), (C, 1, 0),)}
+    jobs = {0: ((A, 2, 2), (B, 0, 1),), 1: ((B, 2, 1), (A, 1, 2),), 3: ((C, 0, 1), (B, 1, 1),), 4: ((C, 2, 1), (B, 0, 2),), 5: ((B, 2, 2), (C, 1, 1),), 7: ((C, 0, 2), (C, 2, 2),), 9: ((B, 1, 2),)}
 
     def run_jobs(table, now):
         for when, todo in table.items():
@@ -378,15 +460,36 @@
     for job, m, n in jobs.get(99, ()):
         job(m, n)
 
-    for g in range(4):
-        mine = jnp.logical_and(primary, z == g)
-        block = mixed_own.at[pl.ds(g * width, width)]
-
-        @pl.when(jnp.logical_not(mine))
-        def _():
-            at.got(block, mix_r.at[g])
-
-    for m, (_, dst) in enumerate(mats):
+    def leave(i, src, dst, part=None):
+        if part is not None:
+            src, dst, i = src.at[part], dst.at[part], i + part
+        left.append((src, dst, out_sems.at[i]))
+        pltpu.make_async_copy(src, dst, out_sems.at[i]).start()
+
+    left = []
+    for i, (src, dst) in enumerate((
+        (x_all, x_all_h), (w_t, w_t_h), (mixed_heads, mixed_heads_h), (q_aug, q_aug_h), (k_aug, k_aug_h), (v_aug, v_aug_h), (k_t, k_t_h),
+    )):
+        leave(i, src, dst)
+
+    def arrive(m):
+        if m == 2:
+            for g in range(4):
+                mine = jnp.logical_and(primary, z == g)
+                block = mixed_own.at[pl.ds(g * width, width)]
+
+                @pl.when(mine)
+                def _():
+                    pltpu.make_async_copy(mixed_heads.at[g], block, mix_s.at[g]).wait()
+
+                @pl.when(jnp.logical_not(mine))
+                def _():
+                    at.got(block, mix_r.at[g])
+
+        for job, m2, n in {0: ((C, 1, 2),)}.get(m, ()):
+            job(m2, n)
+        src, dst = mats[m]
+        pltpu.make_async_copy(src, dst.at[z], local.at[5 + m]).wait()
         for j in range(4):
             chip = (at.q + j) % 4
             r, c = piece(m, chip, 1 - at.b)
@@ -394,13 +497,17 @@
                 s = (z + k) % 4
                 at.got(dst.at[s, r, c], w_r.at[m, s, 2 * chip + 1 - at.b])
 
+    feed_forward(
+        skip, mixed_own, frames, cot, b_out, gain_one, shift_one, b_down, gain_two, shift_two, small_all,
+        out_all, up_all, down_all, arrive, leave,
+        (mixed_own_h, layer_h, gone_h, gmixed_h, normed_h, act_h, ginner_h, gbranch_h, gatt_h),
+        layer, gone, gmixed, normed, act, ginner, gbranch, gatt, small_sums, slope,
+    )
+    for src, dst, sem in left:
+        pltpu.make_async_copy(src, dst, sem).wait()
+
     for i in range(4):
         mine = jnp.logical_and(primary, z == i)
-
-        @pl.when(mine)
-        def _():
-            block = mixed_own.at[pl.ds(pl.multiple_of(at.group * width, 64), width)]
-            pltpu.make_async_copy(mixed_heads.at[i], block, mix_s.at[i]).wait()
 
         @pl.when(jnp.logical_not(mine))
         def _():
@@ -457,7 +564,10 @@
                     at.sent(block, core_s.at[m, s, i])
 
 
-def run_forward(frames, w_query, w_key, w_value, b_query, b_value, b_up, segments, padding, w_up, w_down, w_out):
+def run_forward(
+    skip, frames, cot, w_query, w_key, w_value, b_query, b_value, b_up, b_out, gain_one, shift_one, b_down, gain_two, shift_two,
+    segments, padding, w_up, w_down, w_out,
+):
     share, d = frames.shape
     length = segments.shape[1]
     width = w_query.shape[0]
@@ -470,10 +580,16 @@
         out_shape=(
             S((4, share, d)), S((3 * width, d)), S((4, width, share)), S((4 * width, share)),
             S((heads, 128, length)), S((heads, length, 128)), S((heads, length, 128)), S((heads, HEAD_DIM, length)),
-            S((4, 8, d), F32), S((4, d, f)), S((4, f, d)), S((4, width, d)),
+            S((share, d)), S((share, d), F32), S((4 * width, share)), S((share, d)), S((4, share, f)),
+            S((4, share, f)), S((share, d)), S((share, d)), S((16, d), F32),
         ),
-        in_specs=[VMEM] * 9 + [any_] * 3, out_specs=[VMEM] * 9 + [any_] * 3,
+        in_specs=[SMEM] + [VMEM] * 16 + [any_] * 3, out_specs=[any_] * 16 + [VMEM],
         scratch_shapes=[
+            V((4, share, d), BF16), V((3 * width, d), BF16), V((4, width, share), BF16), V((4 * width, share), BF16),
+            V((heads, 128, length), BF16), V((heads, length, 128), BF16), V((heads, length, 128), BF16), V((heads, HEAD_DIM, length), BF16),
+            V((share, d), BF16), V((share, d), F32), V((4 * width, share), BF16), V((share, d), BF16), V((4, share, f), BF16),
+            V((4, share, f), BF16), V((share, d), BF16), V((share, d), BF16), dma((22,)),
+            V((4, 8, d), F32), V((4, d, f), BF16), V((4, f, d), BF16), V((4, width, d), BF16), V((4, share, f), F32),
             V((share, d), BF16), V((heads, HEAD_DIM, length), BF16), V((2 * heads * 128, d), BF16),
             V((length, 128), BF16), V((16, length), BF16),
             V((3 * width, d), BF16), V((8, d), F32), V((length, 128), BF16), V((16, length), BF16),
@@ -482,98 +598,17 @@
             dma((3, 4, 2)), dma((3, 4)), dma((3, 4, 2)), dma((3, 4, 4)), dma((3, 4, 8)),
         ],
         compiler_params=pltpu.CompilerParams(vmem_limit_bytes=LIMIT, collective_id=0, has_side_effects=True),
-        name="attention_forward",
-    )(frames, w_query, w_key, w_value, b_query, b_value, b_up, segments, padding, w_up, w_down, w_out)
-
-
-def norm_stats(v):
-    centered = v - jnp.mean(v, -1, keepdims=True)
-    r = lax.rsqrt(jnp.mean(centered * centered, -1, keepdims=True) + 1e-05)
-    return centered * r, r
-
-
-def norm_back(c, gain, hat, r):
-    e = c * gain
-    return r * (e - jnp.mean(e, -1, keepdims=True) - hat * jnp.mean(e * hat, -1, keepdims=True))
-
-
-def middle_kernel(
-    skip_ref, mixed_ref, frames_ref, cot_ref, b_out, gain_one, shift_one, b_down, gain_two, shift_two, bup_ref, w_out, w_up, w_down, out_all, up_all, down_all,
-    layer_ref, gone_ref, gmixed_ref, normed_ref, act_ref, ginner_ref, gbranch_ref, gatt_ref, small_ref,
-    slope_ref, wout_ref, wup_ref, wdown_ref, sems,
-):
-    z = lax.axis_index("mp")
-    mats = ((w_out, out_all, wout_ref), (w_up, up_all, wup_ref), (w_down, down_all, wdown_ref))
-    for m, (own, everyone, dst) in enumerate(mats):
-        for s in range(4):
-            @pl.when(z == s)
-            def _():
-                pltpu.make_async_copy(own, dst.at[s], sems.at[m, s]).start()
-
-            @pl.when(z != s)
-            def _():
-                pltpu.make_async_copy(everyone.at[s], dst.at[s], sems.at[m, s]).start()
-
-    def arrive(m, s):
-        pltpu.make_async_copy(mats[m][0], mats[m][2].at[s], sems.at[m, s]).wait()
-
-    skipped = skip_ref[0] == 1
-    b_out, gain_one, shift_one, b_down, gain_two, shift_two = (row_of(v) for v in (b_out, gain_one, shift_one, b_down, gain_two, shift_two))
-    frames = frames_ref[...].astype(F32)
-    for s in range(4):
-        arrive(0, s)
-    all_out = wout_ref[...].reshape(mixed_ref.shape[0], frames.shape[1])
-    attended = mm(mixed_ref[...], all_out, 0, 0) + b_out
-    hat_one, r_one = norm_stats(frames + attended)
-    normed = hat_one * gain_one + shift_one
-    normed_ref[...] = normed.astype(BF16)
-    parts = wup_ref.shape[0]
-    branch = jnp.zeros_like(normed)
-    for s in range(parts):
-        arrive(1, s)
-        inner = mm(normed_ref[...], wup_ref[s]) + bup_ref[s, 0:1, :]
-        cdf = 0.5 * (1.0 + lax.erf(inner * (0.5**0.5)))
-        slope_ref[s] = cdf + inner * (jnp.exp(-0.5 * inner * inner) * 0.3989422804014327)
-        act = (inner * cdf).astype(BF16)
-        act_ref[s] = act
-        arrive(2, s)
-        branch = branch + mm(act, wdown_ref[s])
-    hat_two, r_two = norm_stats(normed + (branch + b_down))
-    result = hat_two * gain_two + shift_two
-    cot = cot_ref[...].astype(F32)
-    layer_ref[...] = jnp.where(skipped, frames, result).astype(BF16)
-    grad_out = jnp.where(skipped, 0.0, cot)
-    grad_two = norm_back(grad_out, gain_two, hat_two, r_two)
-    gbranch = grad_two.astype(BF16)
-    gbranch_ref[...] = gbranch
-    small_ref[10:16, :] = jnp.zeros_like(small_ref[10:16, :])
-    small_ref[0:1, :] = jnp.sum(gbranch.astype(F32), 0, keepdims=True)
-    small_ref[1:2, :] = jnp.sum(grad_out * hat_two, 0, keepdims=True)
-    small_ref[2:3, :] = jnp.sum(grad_out, 0, keepdims=True)
-    grad_normed = grad_two
-    for s in range(parts):
-        gact = mm(gbranch_ref[...], wdown_ref[s], 1, 1)
-        ginner = (gact * slope_ref[s]).astype(BF16)
-        ginner_ref[s] = ginner
-        small_ref[6 + s : 7 + s, :] = jnp.sum(ginner.astype(F32), 0, keepdims=True)
-        grad_normed = grad_normed + mm(ginner, wup_ref[s], 1, 1)
-    grad_one = norm_back(grad_normed, gain_one, hat_one, r_one)
-    gone_ref[...] = grad_one
-    gatt = grad_one.astype(BF16)
-    gatt_ref[...] = gatt
-    small_ref[3:4, :] = jnp.sum(gatt.astype(F32), 0, keepdims=True)
-    small_ref[4:5, :] = jnp.sum(grad_normed * hat_one, 0, keepdims=True)
-    small_ref[5:6, :] = jnp.sum(grad_normed, 0, keepdims=True)
-    gmixed_ref[...] = mm(all_out, gatt, 1, 1).astype(BF16)
-
-
-def attend_back(h, i, cols, q_aug, k_aug, v_aug, k_t, do_aug, dq_acc, dk_acc, dv_acc):
-    weights = jnp.exp(mm(k_aug[h], q_aug[h, :, cols]))
-    rounded = weights.astype(BF16)
-    dv_acc[h] += mm(do_aug[h, 0:HEAD_DIM, cols], rounded, 1, 1)
-    grad = (weights * mm(v_aug[h], do_aug[h, :, cols])).astype(BF16)
-    dk_acc[h] += mm(q_aug[h, 0:HEAD_DIM, cols], grad, 1, 1)
-    return mm(k_t[h], grad)
+        name="forward",
+    )(skip, frames, cot, w_query, w_key, w_value, b_query, b_value, b_up, b_out, gain_one, shift_one, b_down, gain_two, shift_two,
+      segments, padding, w_up, w_down, w_out)
+
+
+def attend_back(h, keys, queries, q_aug, k_aug, v_aug, k_t, do_aug, dk_acc, dv_acc):
+    weights = jnp.exp(mm(k_aug[h, keys, :], q_aug[h, :, queries]))
+    dv_acc[h, :, keys] += mm(do_aug[h, 0:HEAD_DIM, queries], weights.astype(BF16), 1, 1)
+    grad = (weights * mm(v_aug[h, keys, :], do_aug[h, :, queries])).astype(BF16)
+    dk_acc[h, :, keys] += mm(q_aug[h, 0:HEAD_DIM, queries], grad, 1, 1)
+    return mm(k_t[h, :, keys], grad)
 
 
 def total(first, *others):
@@ -584,12 +619,13 @@
 
 
 def backward_kernel(
-    skip_ref, gmixed, mixed_own, normed, act, ginner, gbranch, gatt, small, gone, cot,
-    x_all, w_t, mixed_heads, q_aug, k_aug, v_aug, k_t,
+    skip_ref, gmixed, mixed_own_h, normed_h, act_h, ginner_h, gbranch_h, gatt_h, small, gone_h, cot_h,
+    x_all, w_t_h, mixed_heads_h, q_aug_h, k_aug_h, v_aug_h, k_t_h,
     frames_grad, dw_out, up_out, down_out, out_out, small_out,
-    do_in, do_aug, dk_acc, dv_acc, grads,
+    mixed_own, normed, act, ginner, gbranch, gatt, gone, cot, w_t, mixed_heads, q_aug, k_aug, v_aug, k_t, load_sems,
+    do_in, do_aug, dk_acc, dv_acc, dq_acc, dq_keep, grads, x_sem,
     big, away, core_in, near_in, across_in, mid, z_in, bigo, core_ino, near_ino, across_ino, mido, z_ino,
-    part, sib_in, line_in, dw_own, dw_in, dw_mid, dw_z, small_mine, small_plane, small_mid, small_z,
+    sib_in, line_in, dw_own, dw_in, dw_mid, dw_z, small_mine, small_plane, small_mid, small_z,
     gm_s, gm_r, ci_s, ci_r, nr_s, nr_r, ac_s, ac_r, z_s, z_r, ag_s, ag_r,
     part_s, part_r, line_s, line_r, dwp_s, dwp_r, dwz_s, dwz_r, dwo_s, dwo_r, dwf_s, sp_s, sp_r, sz_s, sz_r,
 ):
@@ -597,11 +633,22 @@
     heads = q_aug.shape[0]
     width = heads * HEAD_DIM
     share = gatt.shape[0]
-    length = x_all.shape[0] * share
+    length = q_aug.shape[2]
     step_rows = share // CHUNKS
     z, c, q = at.z, at.b, at.q
     primary = at.primary
     secondary = jnp.logical_not(primary)
+    loads = []
+    for src, dst in ((gbranch_h, gbranch), (act_h, act), (normed_h, normed), (ginner_h, ginner), (mixed_own_h, mixed_own), (gatt_h, gatt),
+                     (mixed_heads_h, mixed_heads), (q_aug_h, q_aug), (k_aug_h, k_aug), (v_aug_h, v_aug), (k_t_h, k_t), (w_t_h, w_t),
+                     (gone_h, gone), (cot_h, cot)):
+        pltpu.make_async_copy(src, dst, load_sems.at[len(loads)]).start()
+        loads.append((src, dst))
+
+    def loaded(*numbers):
+        for n in numbers:
+            pltpu.make_async_copy(*loads[n], load_sems.at[n]).wait()
+
     at.barrier()
 
     for g in range(4):
@@ -633,6 +680,12 @@
         return pl.ds(pl.multiple_of(chip * quartero, 16), quartero)
 
     def weight_job(j):
+        if j == 0:
+            loaded(0, 1)
+        if j == n_big // 2:
+            loaded(2, 3)
+        if j == n_big:
+            loaded(4, 5)
         if j < n_big:
             kind, s = j // 4, j % 4
             made = mm(act[s], gbranch[...], 0, 0) if kind == 0 else mm(normed[...], ginner[s], 0, 0)
@@ -744,12 +797,11 @@
             core_job(j - 2)
     core_job(n_big - 1)
     core_job(n_big)
-
-    def block_of(turn):
-        low = z // 2
-        near = z + low * (3 - 2 * z)
-        s = jnp.where(near == 0, turn, jnp.where(turn == 0, 1, jnp.where(turn == 1, 2, jnp.where(turn == 2, 0, 3))))
-        return s + low * (3 - 2 * s)
+    x_here, part = core_in.at[0:4], core_in.at[4:8]
+    pltpu.make_async_copy(x_all, x_here, x_sem.at[0]).start()
+
+    late = at.rb
+    side = length // 2
 
     def prepare(i):
         mine = jnp.logical_and(primary, z == i)
@@ -771,25 +823,42 @@
             do_aug[h, HEAD_DIM : HEAD_DIM + 16, cols] = pad_rows(split3(-inner), 16, share)
             do_aug[h, HEAD_DIM + 16 :, cols] = jnp.zeros((48, share), BF16)
 
+    def half_row(n):
+        return pl.ds(pl.multiple_of(n * side, side), side)
+
     dk_acc[...] = jnp.zeros_like(dk_acc)
     dv_acc[...] = jnp.zeros_like(dv_acc)
 
-    N, M, Q = near_job, plane_job, final_job
-    jobs = {-1: ((N, 0), (N, 1),), 0: ((N, 2), (M, 0),), 1: ((M, 1),), 2: ((N, 3), (M, 2),), 4: ((N, 4), (M, 3),), 6: ((N, 5), (M, 4),), 8: ((N, 6), (M, 5), (Q, 0),), 10: ((N, 7), (M, 6),)}
+    N, M, Q, U, V = near_job, plane_job, final_job, pass_job, share_job
+    jobs = {-1: ((N, 0), (N, 1),), 0: ((N, 2), (M, 0),), 1: ((M, 1),), 2: ((N, 3), (M, 2),), 4: ((N, 4), (M, 3),), 6: ((N, 5), (M, 4),), 8: ((N, 6), (M, 5),), 50: ((Q, 0),), 10: ((N, 7), (M, 6),)}
 
     def attention_step(t, _):
-        i, h = block_of(t // heads), t % heads
-
-        @pl.when(h == 0)
-        def _():
-            prepare(i)
-
-        cols = pl.ds(pl.multiple_of(i * share, share), share)
-        dq = attend_back(h, i, cols, q_aug, k_aug, v_aug, k_t, do_aug, None, dk_acc, dv_acc)
+        last = t >= 3 * heads
+        h = jnp.where(last, t - 3 * heads, t // 3)
+        turn = jnp.where(last, 3, t % 3)
+        keys = half_row(jnp.where(jnp.logical_or(turn == 0, last), late, 1 - late))
+        queries = half_row(jnp.where(turn < 2, 1 - late, late))
+        dq = attend_back(h, keys, queries, q_aug, k_aug, v_aug, k_t, do_aug, dk_acc, dv_acc)
         hs = pl.ds(pl.multiple_of(h * HEAD_DIM, HEAD_DIM), HEAD_DIM)
-        grads[hs, cols] = (dq.astype(BF16).astype(F32) * HEAD_DIM**-0.5).astype(BF16)
+
+        @pl.when(turn == 0)
+        def _():
+            dq_acc[...] = dq
+
+        @pl.when(turn == 1)
+        def _():
+            grads[hs, queries] = ((dq_acc[...] + dq).astype(BF16).astype(F32) * HEAD_DIM**-0.5).astype(BF16)
+
+        @pl.when(turn == 2)
+        def _():
+            dq_keep[h] = dq
+
+        @pl.when(turn == 3)
+        def _():
+            grads[hs, queries] = ((dq_keep[h] + dq).astype(BF16).astype(F32) * HEAD_DIM**-0.5).astype(BF16)
+
         for when, todo in jobs.items():
-            if 0 <= when < 99:
+            if 0 <= when < 4 * heads:
                 @pl.when(t == when)
                 def _():
                     for job, j in todo:
@@ -797,15 +866,72 @@
 
         return 0
 
+    def rows(ch):
+        return pl.ds(ch * step_rows, step_rows)
+
+    def part_job(s):
+        part[s] = mm(grads[:, pl.ds(pl.multiple_of(s * share, share), share)], w_t[...], 0, 0).astype(BF16)
+
+        @pl.when(secondary)
+        def _():
+            for ch in range(CHUNKS):
+                at.send(part.at[s, rows(ch)], sib_in.at[s, rows(ch)], part_s.at[s, ch], part_r.at[s, ch], at.sib, z)
+
+    def line_job(place):
+        s = at.line(place)
+        for ch in range(CHUNKS):
+            here = (s, rows(ch))
+
+            @pl.when(jnp.logical_and(primary, place != at.p))
+            def _():
+                at.got(sib_in.at[here], part_r.at[s, ch])
+
+                @pl.when(jnp.logical_and(at.p == 1, place >= 2))
+                def _():
+                    at.got(line_in.at[here], line_r.at[s, ch])
+                    part[here] = total(part[here], sib_in[here], line_in[here]).astype(BF16)
+                    at.send(part.at[here], line_in.at[here], line_s.at[s, ch], line_r.at[s, ch], at.d, at.own_line(2))
+
+                @pl.when(jnp.logical_or(at.p == 0, place == 0))
+                def _():
+                    part[here] = total(part[here], sib_in[here]).astype(BF16)
+                    at.send(part.at[here], line_in.at[here], line_s.at[s, ch], line_r.at[s, ch], at.d, at.own_line(1 - at.p))
+
+    def finish(n):
+        cols = half_row(n)
+        for h in range(heads):
+            grads[width + h * HEAD_DIM : width + (h + 1) * HEAD_DIM, cols] = dk_acc[h, :, cols].astype(BF16)
+            grads[2 * width + h * HEAD_DIM : 2 * width + (h + 1) * HEAD_DIM, cols] = dv_acc[h, :, cols].astype(BF16)
+
+    loaded(6, 7, 8, 9, 10, 11)
+    for i in range(4):
+        prepare(i)
     for job, j in jobs.get(-1, ()):
         job(j)
-    lax.fori_loop(0, 4 * heads, attention_step, 0)
-    for job, j in jobs.get(99, ()):
+    lax.fori_loop(0, 3 * heads, attention_step, 0)
+    finish(1 - late)
+    for place in (3, 2):
+        part_job(at.line(place))
+
+    @pl.when(at.p == 0)
+    def _():
+        line_job(3)
+        line_job(2)
+
+    for job, j in jobs.get(50, ()):
         job(j)
-    for h in range(heads):
-        grads[width + h * HEAD_DIM : width + (h + 1) * HEAD_DIM, :] = dk_acc[h].astype(BF16)
-        grads[2 * width + h * HEAD_DIM : 2 * width + (h + 1) * HEAD_DIM, :] = dv_acc[h].astype(BF16)
-
+    lax.fori_loop(3 * heads, 4 * heads, attention_step, 0)
+    finish(late)
+    for place in (0, 1):
+        part_job(at.line(place))
+
+    @pl.when(at.p == 0)
+    def _():
+        line_job(1)
+
+    @pl.when(at.p == 1)
+    def _():
+        line_job(0)
 
     small_mine[...] = small[...]
     small_mine[pl.ds(10 + at.group, 1), 0 : 3 * width] = mm(jnp.ones((8, length), BF16), grads[...], 1, 1)[0:1]
@@ -814,54 +940,10 @@
         at.send(small_mine, small_plane.at[4 - k], sp_s.at[k], sp_r.at[4 - k], at.chip(k), z)
         at.send(small_mine, small_plane.at[7 - k], sp_s.at[3 + k], sp_r.at[7 - k], at.other(k), z)
 
-    def rows(ch):
-        return pl.ds(ch * step_rows, step_rows)
-
-    def order(k):
-        return jnp.where(at.pp == 0, 3 - k, (4 - k) % 4)
-
-    def part_job(s):
-        part[s] = mm(grads[:, pl.ds(pl.multiple_of(s * share, share), share)], w_t[...], 0, 0).astype(BF16)
-
-        @pl.when(secondary)
-        def _():
-            for ch in range(CHUNKS):
-                at.send(part.at[s, rows(ch)], sib_in.at[s, rows(ch)], part_s.at[s, ch], part_r.at[s, ch], at.sib, z)
-
-    def line_job(place):
-        s = at.line(place)
-        for ch in range(CHUNKS):
-            here = (s, rows(ch))
-
-            @pl.when(jnp.logical_and(primary, place != at.p))
-            def _():
-                at.got(sib_in.at[here], part_r.at[s, ch])
-
-                @pl.when(jnp.logical_and(at.p == 1, place >= 2))
-                def _():
-                    at.got(line_in.at[here], line_r.at[s, ch])
-                    part[here] = total(part[here], sib_in[here], line_in[here]).astype(BF16)
-                    at.send(part.at[here], line_in.at[here], line_s.at[s, ch], line_r.at[s, ch], at.d, at.own_line(2))
-
-                @pl.when(jnp.logical_or(at.p == 0, place == 0))
-                def _():
-                    part[here] = total(part[here], sib_in[here]).astype(BF16)
-                    at.send(part.at[here], line_in.at[here], line_s.at[s, ch], line_r.at[s, ch], at.d, at.own_line(1 - at.p))
-
-    for k in range(4):
-        part_job(at.line(order(k)))
-        if k > 0:
-            @pl.when(jnp.logical_or(at.p == 0, k == 1))
-            def _():
-                line_job(order(k - 1))
-
-    @pl.when(at.p == 0)
-    def _():
-        line_job(order(3))
-
-    made = mm(grads[:, 0:share], x_all[0])
+    pltpu.make_async_copy(x_all, x_here, x_sem.at[0]).wait()
+    made = mm(grads[:, 0:share], x_here[0])
     for s in range(1, 4):
-        made = made + mm(grads[:, s * share : (s + 1) * share], x_all[s])
+        made = made + mm(grads[:, s * share : (s + 1) * share], x_here[s])
     made = made.astype(BF16)
     fourth = made.shape[0] // 4
     for i in range(4):
@@ -884,12 +966,12 @@
             at.got(small_z.at[k], sz_r.at[k])
         small_out[...] = total(small_mid[...], small_z[0], small_z[1], small_z[2])
 
-    def onward(k):
+    def onward(place):
         @pl.when(at.p == 1)
         def _():
-            line_job(order(k))
-
-        if k == 1:
+            line_job(place)
+
+        if place == 3:
             @pl.when(at.p == 2)
             def _():
                 s = at.own_line(3)
@@ -931,11 +1013,11 @@
             at.send(piece, piece, dwo_s.at[3], dwo_r.at[i], at.across, z)
             at.send(piece, piece, dwf_s.at[0], dwo_r.at[i], at.sib, z)
 
-    N, M, Q, U, V = near_job, plane_job, final_job, pass_job, share_job
-    for job, j in ((M, 7), (N, 8), (small_sum, 0), (dw_across, 0), (dw_plane, 0), (onward, 1), (M, 8), (onward, 2), (dw_final, 0), (Q, 1), (U, 0), (dw_pass, 0), (onward, 3), (V, 0), (Q, 2), (U, 1), (small_end, 0), (U, 2), (V, 1), (V, 2)):
+    for job, j in ((onward, 3), (M, 7), (small_sum, 0), (dw_across, 0), (N, 8), (dw_plane, 0), (M, 8), (onward, 2), (dw_final, 0), (U, 0), (Q, 1), (dw_pass, 0), (U, 1), (Q, 2), (V, 0), (small_end, 0), (U, 2), (V, 1), (V, 2)):
         job(j)
 
     skipped = skip_ref[0] == 1
+    loaded(12, 13)
     for ch in range(CHUNKS):
         at.got(line_in.at[z, rows(ch)], line_r.at[z, ch])
 
@@ -1030,6 +1112,7 @@
 def run_backward(skip, gmixed, mixed_own, normed, act, ginner, gbranch, gatt, small, gone, cot,
                  x_all, w_t, mixed_heads, q_aug, k_aug, v_aug, k_t):
     share, d = gatt.shape
+    any_ = pl.BlockSpec(memory_space=pl.ANY)
     f = act.shape[2]
     heads, _, length = q_aug.shape
     width = heads * HEAD_DIM
@@ -1040,15 +1123,20 @@
         out_shape=(
             S((share, d)), S((3 * width, d)), S((d, f)), S((f, d)), S((width, d)), S((16, d), F32),
         ),
-        in_specs=[SMEM] + [VMEM] * 17, out_specs=[VMEM] * 6,
+        in_specs=[SMEM] + [any_] * 7 + [VMEM] + [any_] * 9, out_specs=[VMEM] * 6,
         scratch_shapes=[
+            V((4 * width, share), BF16), V((share, d), BF16), V((4, share, f), BF16), V((4, share, f), BF16), V((share, d), BF16),
+            V((share, d), BF16), V((share, d), F32), V((share, d), BF16), V((3 * width, d), BF16), V((4, width, share), BF16),
+            V((heads, 128, length), BF16), V((heads, length, 128), BF16), V((heads, length, 128), BF16),
+            V((heads, HEAD_DIM, length), BF16), dma((14,)),
             V((4, width, share), BF16), V((heads, 128, length), BF16),
-            V((heads, HEAD_DIM, length), F32), V((heads, HEAD_DIM, length), F32), V((3 * width, length), BF16),
+            V((heads, HEAD_DIM, length), F32), V((heads, HEAD_DIM, length), F32),
+            V((HEAD_DIM, length // 2), F32), V((heads, HEAD_DIM, length // 2), F32), V((3 * width, length), BF16), dma((1,)),
             V((8, hd, d), BF16), V((4, hd, d), BF16), V((8, hd, d), BF16), V((2, 8, hd // 4, d), BF16), V((8, hd // 4, d), BF16), V((8, hd // 4, d), BF16),
             V((3, 2, hd // 4, d), BF16),
             V((2, 4, width, ho), BF16), V((4, width, ho), BF16), V((2, 4, width // 4, ho), BF16), V((4, width // 4, ho), BF16), V((4, width // 4, ho), BF16),
             V((3, width // 4, ho), BF16),
-            V((4, share, d), BF16), V((4, share, d), BF16), V((4, share, d), BF16),
+            V((4, share, d), BF16), V((4, share, d), BF16),
             V((4, 3 * width // 4, d), BF16), V((3, 3 * width // 4, d), BF16), V((3 * width // 4, d), BF16), V((3 * width // 4, d), BF16),
             V((16, d), F32), V((7, 16, d), F32), V((16, d), F32), V((3, 16, d), F32),
             dma((4,)), dma((4,)), dma((9,)), dma((9,)), dma((9, 2)), dma((9, 2)), dma((9,)), dma((9,)), dma((12,)), dma((3, 3)),
@@ -1094,23 +1182,14 @@
     heads = width // HEAD_DIM
     params = pltpu.CompilerParams(vmem_limit_bytes=LIMIT)
     own = frames[0]
-    x_all, w_t, mixed, mixed_own, q_aug, k_aug, v_aug, k_t, small_all, wup, wdown, wout = run_forward(
-        own, w_query.T, w_key.T, w_value.T, b_query, b_value, b_up, segments, padding, w_up, w_down, w_out
+    f = w_up.shape[1]
+    (
+        x_all, w_t, mixed, mixed_own, q_aug, k_aug, v_aug, k_t,
+        layer, gone, gmixed, normed, act, ginner, gbranch, gatt, small,
+    ) = run_forward(
+        skip_flag, own, cotangent[0], w_query.T, w_key.T, w_value.T, b_query, b_value, b_up,
+        b_out, gain_one, shift_one, b_down, gain_two, shift_two, segments, padding, w_up, w_down, w_out,
     )
-    f = w_up.shape[1]
-    layer, gone, gmixed, normed, act, ginner, gbranch, gatt, small = pl.pallas_call(
-        middle_kernel,
-        out_shape=(
-            S((share, d)), S((share, d), F32), S((mp * width, share)), S((share, d)), S((mp, share, f)),
-            S((mp, share, f)), S((share, d)), S((share, d)), S((16, d), F32),
-        ),
-        in_specs=[SMEM] + [VMEM] * 10 + [pl.BlockSpec(memory_space=pl.ANY)] * 6, out_specs=[VMEM] * 9,
-        scratch_shapes=[
-            pltpu.VMEM((mp, share, f), F32), pltpu.VMEM((mp, width, d), BF16), pltpu.VMEM((mp, d, f), BF16),
-            pltpu.VMEM((mp, f, d), BF16), pltpu.SemaphoreType.DMA((3, 4)),
-        ],
-        compiler_params=params, name="feed_forward",
-    )(skip_flag, mixed_own, own, cotangent[0], b_out, gain_one, shift_one, b_down, gain_two, shift_two, small_all, w_out, w_up, w_down, wout, wup, wdown)
     frames_grad, wgrad, gup, gdown, gout, small = run_backward(
         skip_flag, gmixed, mixed_own, normed, act, ginner, gbranch, gatt, small, gone, cotangent[0],
         x_all, w_t, mixed, q_aug, k_aug, v_aug, k_t,

time: 222 us -> 208 us (0.937)
  Pallas kernels: 216 us -> 201 us
    pallas_call x1 -> x0, Pallas kernels: 18.4 us -> none  [shards(): pl.pallas_call(middle_kernel, out_shape=(S((share, d)), S((share, d), F32...]
    pallas_call x1, Pallas kernels: 83.3 us -> 93.3 us  [run_forward(): pl.pallas_call(forward_kernel, out_shape=(S((4, share, d)), S((3 * width,...]
    pallas_call x1, Pallas kernels: 110 us -> 102 us  [run_backward(): pl.pallas_call(backward_kernel, out_shape=(S((share, d)), S((3 * width, d...]
where the time goes in v4:
time: 208 us; the launch traced here: 205 us
  Pallas kernels  201 us (97%)
  local copies, waits for them, and re-layouts  2.08 us (1%)
    pallas_call x1, Pallas kernels, run_backward(): pl.pallas_call(backward_kernel, out_shape=(S((share, d)), S((3 * width, d...  102 us
    pallas_call x1, Pallas kernels, run_forward(): pl.pallas_call(forward_kernel, out_shape=(S((4, share, d)), S((3 * width,...  93.3 us
    pallas_call x1, Pallas kernels, shards(): pl.pallas_call(last_kernel, out_shape=tuple((S(s, F32) for s in [(width,...  5.08 us

profile of v4, /device:TPU:1, one launch (start us, length us, event | category | flops | bytes accessed | tf_op | source)
XLA Modules:
  0.0 204.5 jit_solution(7484118209293847392)
XLA Ops:
  1.3 93.3 %forward.1 = (bf16[4,384,768]{2,1,0:T(8,128)(2,1)}, bf16[576,768]{1,0:T(8,128)(2,1)}, bf16[4,192,384]{2,1,0:T(8,128)(2,1)}, bf16[768,384]{1,0:T(8,128)(2,1)}, bf...) custom-call(s32[1]{0:T(128)S(6)} %copy.39.skip.skip_ref, ...), custom_call_target="tpu_custom_call" | custom-call | tf_op jit(solution)/shard_map/forward/pallas_call | solution.py:578
  94.6 102.3 %attention_backward.1 = (bf16[384,768]{1,0:T(8,128)(2,1)}, bf16[576,768]{1,0:T(8,128)(2,1)}, bf16[768,768]{1,0:T(8,128)(2,1)}, bf16[768,768]{1,0:T(8,128)(2,1)},...) custom-call(s32[1]{0:T(128)S(6)} %copy.39.skip.skip_ref, bf16[768,384]{1,0:T(8,128)(2,1)} %get-tuple-element.56.gmixed, ...), custom_call_target="tpu_custom_call" | custom-call | tf_op jit(solution)/shard_map/attention_backward/pallas_call | solution.py:1121
  196.9 0.0 copy-start
  196.9 5.1 %outputs.1 = (f32[192,768]{1,0:T(8,128)}, f32[192,768]{1,0:T(8,128)}, f32[192,768]{1,0:T(8,128)}, f32[768,768]{1,0:T(8,128)}, f32[768,768]{1,0:T(8,128)}, /*inde...) custom-call(bf16[576,768]{1,0:T(8,128)(2,1)} %get-tuple-element.73.d, ...), custom_call_target="tpu_custom_call" | custom-call | tf_op jit(solution)/shard_map/outputs/pallas_call | solution.py:1203
  202.0 0.0 copy-start.1
  202.0 0.0 copy-done
  202.0 0.8 copy.40
  202.8 0.4 copy-done.1
  203.3 0.8 copy.41
Async XLA Ops:
  196.9 5.1 %copy-start = (bf16[384,768]{1,0:T(8,128)(2,1)S(1)}, bf16[384,768]{1,0:T(8,128)(2,1)}, u32[]{:S(2)}) copy-start(bf16[384,768]{1,0:T(8,128)(2,1)} %get-tuple-element.55) | copy-start | bytes 1769476
  202.0 1.3 copy-start.1

commit v5 on v4

--- a/solution.py
+++ b/solution.py
@@ -349,7 +349,7 @@
             at.got(block, sem)
             at.send(block, block, core_s.at[m, s, i], sem, at.sib, z)
 
-    for m in range(3):
+    for m in (2, 0, 1):
         weights_first(m)
     for m, (src, dst) in enumerate(mats):
         pltpu.make_async_copy(src, dst.at[z], local.at[5 + m]).start()
@@ -398,8 +398,8 @@
             ]
 
     A, B, C = weights_line, weights_near, weights_across
-    early = {1: ((A, 0, 0), (A, 2, 0), (A, 1, 0),), 2: ((A, 0, 1), (A, 2, 1), (A, 1, 1), (B, 0, 0), (B, 2, 0), (B, 1, 0),), 3: ((A, 0, 2), (C, 0, 0), (C, 2, 0), (C, 1, 0),)}
-    jobs = {0: ((A, 2, 2), (B, 0, 1),), 1: ((B, 2, 1), (A, 1, 2),), 3: ((C, 0, 1), (B, 1, 1),), 4: ((C, 2, 1), (B, 0, 2),), 5: ((B, 2, 2), (C, 1, 1),), 7: ((C, 0, 2), (C, 2, 2),), 9: ((B, 1, 2),)}
+    early = {1: ((A, 0, 0), (A, 0, 1), (A, 2, 0),), 2: ((A, 2, 1), (A, 1, 0), (A, 1, 1), (B, 0, 0), (B, 2, 0), (B, 1, 0),), 3: ((A, 0, 2), (C, 0, 0),)}
+    jobs = {0: ((C, 1, 0), (B, 0, 1),), 1: ((B, 2, 1), (A, 2, 2),), 2: ((C, 2, 0),), 3: ((C, 0, 1), (B, 1, 1),), 4: ((A, 1, 2), (B, 0, 2),), 5: ((C, 2, 1), (B, 2, 2), (C, 1, 1),), 7: ((C, 0, 2), (C, 2, 2),), 9: ((B, 1, 2),)}
 
     def run_jobs(table, now):
         for when, todo in table.items():

time: 208 us -> 206 us (level)
  no operation moved by 1% of the time
where the time goes in v5:
time: 206 us; the launch traced here: 203 us
  Pallas kernels  199 us (97%)
  local copies, waits for them, and re-layouts  2.08 us (1%)
    pallas_call x1, Pallas kernels, run_backward(): pl.pallas_call(backward_kernel, out_shape=(S((share, d)), S((3 * width, d...  102 us
    pallas_call x1, Pallas kernels, run_forward(): pl.pallas_call(forward_kernel, out_shape=(S((4, share, d)), S((3 * width,...  92.2 us
    pallas_call x1, Pallas kernels, shards(): pl.pallas_call(last_kernel, out_shape=tuple((S(s, F32) for s in [(width,...  5.08 us

profile of v5, /device:TPU:1, one launch (start us, length us, event | category | flops | bytes accessed | tf_op | source)
XLA Modules:
  0.0 203.0 jit_solution(8732241320742688874)
XLA Ops:
  1.3 92.2 %forward.1 = (bf16[4,384,768]{2,1,0:T(8,128)(2,1)}, bf16[576,768]{1,0:T(8,128)(2,1)}, bf16[4,192,384]{2,1,0:T(8,128)(2,1)}, bf16[768,384]{1,0:T(8,128)(2,1)}, bf...) custom-call(s32[1]{0:T(128)S(6)} %copy.39.skip.skip_ref, ...), custom_call_target="tpu_custom_call" | custom-call | tf_op jit(solution)/shard_map/forward/pallas_call | solution.py:578
  93.5 101.8 %attention_backward.1 = (bf16[384,768]{1,0:T(8,128)(2,1)}, bf16[576,768]{1,0:T(8,128)(2,1)}, bf16[768,768]{1,0:T(8,128)(2,1)}, bf16[768,768]{1,0:T(8,128)(2,1)},...) custom-call(s32[1]{0:T(128)S(6)} %copy.39.skip.skip_ref, bf16[768,384]{1,0:T(8,128)(2,1)} %get-tuple-element.56.gmixed, ...), custom_call_target="tpu_custom_call" | custom-call | tf_op jit(solution)/shard_map/attention_backward/pallas_call | solution.py:1121
  195.4 0.0 copy-start
  195.4 5.1 %outputs.1 = (f32[192,768]{1,0:T(8,128)}, f32[192,768]{1,0:T(8,128)}, f32[192,768]{1,0:T(8,128)}, f32[768,768]{1,0:T(8,128)}, f32[768,768]{1,0:T(8,128)}, /*inde...) custom-call(bf16[576,768]{1,0:T(8,128)(2,1)} %get-tuple-element.73.d, ...), custom_call_target="tpu_custom_call" | custom-call | tf_op jit(solution)/shard_map/outputs/pallas_call | solution.py:1203
  200.5 0.0 copy-start.1
  200.5 0.0 copy-done
  200.5 0.8 copy.40
  201.3 0.4 copy-done.1
  201.8 0.8 copy.41
Async XLA Ops:
  195.4 5.1 %copy-start = (bf16[384,768]{1,0:T(8,128)(2,1)S(1)}, bf16[384,768]{1,0:T(8,128)(2,1)}, u32[]{:S(2)}) copy-start(bf16[384,768]{1,0:T(8,128)(2,1)} %get-tuple-element.55) | copy-start | bytes 1769476
  200.5 1.3 copy-start.1

commit v6 on v5

--- a/solution.py
+++ b/solution.py
@@ -1013,7 +1013,7 @@
             at.send(piece, piece, dwo_s.at[3], dwo_r.at[i], at.across, z)
             at.send(piece, piece, dwf_s.at[0], dwo_r.at[i], at.sib, z)
 
-    for job, j in ((onward, 3), (M, 7), (small_sum, 0), (dw_across, 0), (N, 8), (dw_plane, 0), (M, 8), (onward, 2), (dw_final, 0), (U, 0), (Q, 1), (dw_pass, 0), (U, 1), (Q, 2), (V, 0), (small_end, 0), (U, 2), (V, 1), (V, 2)):
+    for job, j in ((onward, 3), (M, 7), (dw_across, 0), (small_sum, 0), (N, 8), (dw_plane, 0), (M, 8), (onward, 2), (U, 0), (dw_final, 0), (Q, 1), (dw_pass, 0), (U, 1), (Q, 2), (V, 0), (small_end, 0), (U, 2), (V, 1), (V, 2)):
         job(j)
 
     skipped = skip_ref[0] == 1
@@ -1150,7 +1150,9 @@
       x_all, w_t, mixed_heads, q_aug, k_aug, v_aug, k_t)
 
 
-def last_kernel(dw, up, down, out, small, *outs):
+def last_kernel(dw, up, down, out, small, layer, frames, layer_out, frames_out, *outs):
+    layer_out[...] = layer[...]
+    frames_out[...] = frames[...]
     z = lax.axis_index("mp")
     d_query, d_key, d_value, d_up, d_down, d_out, b_query, b_value, b_up = outs[:9]
     width = d_out.shape[0]
@@ -1200,13 +1202,13 @@
         wgrad, gup, gdown, gout, small = (
             lax.psum(v.astype(F32), "dp", axis_index_groups=groups) for v in (wgrad, gup, gdown, gout, small)
         )
-    d_query, d_key, d_value, d_up, d_down, d_out, b_q, b_v, b_u, *rest = pl.pallas_call(
+    layer, frames_grad, d_query, d_key, d_value, d_up, d_down, d_out, b_q, b_v, b_u, *rest = pl.pallas_call(
         last_kernel,
-        out_shape=tuple(
+        out_shape=(S((share, d)), S((share, d))) + tuple(
             S(s, F32) for s in [(width, d)] * 3 + [(d, f), (f, d), (width, d), (width,), (width,), (f,)] + [(d,)] * 6
         ),
-        in_specs=[VMEM] * 5, out_specs=[VMEM] * 15, compiler_params=params, name="outputs",
-    )(wgrad, gup, gdown, gout, small)
+        in_specs=[VMEM] * 7, out_specs=[VMEM] * 17, compiler_params=params, name="outputs",
+    )(wgrad, gup, gdown, gout, small, layer, frames_grad)
     b_down_grad, gain_two_grad, shift_two_grad, b_out_grad, gain_one_grad, shift_one_grad = rest
     return (
         layer[None], frames_grad[None], d_query.T, b_q, d_key.T, d_value.T, b_v,

time: 206 us -> 205 us (level)
  local copies, waits for them, and re-layouts: 2.08 us -> 0 us
    unnamed x6 -> x0, local copies, waits for them, and re-layouts: 2.08 us -> none
where the time goes in v6:
time: 205 us; the launch traced here: 201 us
  Pallas kernels  200 us (98%)
    pallas_call x1, Pallas kernels, run_backward(): pl.pallas_call(backward_kernel, out_shape=(S((share, d)), S((3 * width, d...  102 us
    pallas_call x1, Pallas kernels, run_forward(): pl.pallas_call(forward_kernel, out_shape=(S((4, share, d)), S((3 * width,...  92.2 us
    pallas_call x1, Pallas kernels, shards(): pl.pallas_call(last_kernel, out_shape=(S((share, d)), S((share, d))) + tu...  5.7 us

profile of v6, /device:TPU:1, one launch (start us, length us, event | category | flops | bytes accessed | tf_op | source)
XLA Modules:
  0.0 201.4 jit_solution(12752961260995172745)
XLA Ops:
  1.3 92.2 %forward.1 = (bf16[4,384,768]{2,1,0:T(8,128)(2,1)}, bf16[576,768]{1,0:T(8,128)(2,1)}, bf16[4,192,384]{2,1,0:T(8,128)(2,1)}, bf16[768,384]{1,0:T(8,128)(2,1)}, bf...) custom-call(s32[1]{0:T(128)S(6)} %copy.37.skip.skip_ref, ...), custom_call_target="tpu_custom_call" | custom-call | tf_op jit(solution)/shard_map/forward/pallas_call | solution.py:578
  93.5 101.7 %attention_backward.1 = (bf16[384,768]{1,0:T(8,128)(2,1)}, bf16[576,768]{1,0:T(8,128)(2,1)}, bf16[768,768]{1,0:T(8,128)(2,1)}, bf16[768,768]{1,0:T(8,128)(2,1)},...) custom-call(s32[1]{0:T(128)S(6)} %copy.37.skip.skip_ref, bf16[768,384]{1,0:T(8,128)(2,1)} %get-tuple-element.57.gmixed, ...), custom_call_target="tpu_custom_call" | custom-call | tf_op jit(solution)/shard_map/attention_backward/pallas_call | solution.py:1121
  195.3 5.7 %outputs.1 = (bf16[384,768]{1,0:T(8,128)(2,1)}, bf16[384,768]{1,0:T(8,128)(2,1)}, f32[192,768]{1,0:T(8,128)}, f32[192,768]{1,0:T(8,128)}, f32[192,768]{1,0:T(8,1...) custom-call(bf16[576,768]{1,0:T(8,128)(2,1)} %get-tuple-element.73.d, ...), custom_call_target="tpu_custom_call" | custom-call | tf_op jit(solution)/shard_map/outputs/pallas_call | solution.py:1205
